TPU v7x, 32 devices: a whole 2x2x4 slice. The times are simulated.
32 devices in a mesh: row: 8 (over z, y), col: 4 (over x, core).
Axes of the slice: x: 2, y: 2, z: 4, core: 2. Of those that a mesh axis runs over, the one named last changes fastest.
Arguments:
- hidden_in: bfloat16 [8192, 2048], P('row', 'col'), may hold values from -32 to 32
- seq_lengths: int32 [8, 4], P('row'), may hold values from 1 to 512, 1024 in all within a row
- attn_norm: float32 [2048], P('col'), may hold values from 0.5 to 1.5
- w_query: bfloat16 [2048, 2048], P('row', 'col'), may hold values from -0.125 to 0.125
- key_weight: bfloat16 [2048, 1024], P('row', 'col'), may hold values from -0.125 to 0.125
- value_weight: bfloat16 [2048, 1024], P('row', 'col'), may hold values from -0.125 to 0.125
- query_norm: float32 [128], replicated, may hold values from 0.8 to 2
- key_norm: float32 [128], replicated, may hold values from 0.8 to 2
- w_output: bfloat16 [2048, 2048], P('col', 'row'), may hold values from -0.5 to 0.5
- ffwd_norm: float32 [2048], P('col'), may hold values from 0.5 to 1.5
- w_gate: bfloat16 [2048, 6144], P('row', 'col'), may hold values from -0.125 to 0.125
- w_up: bfloat16 [2048, 6144], P('row', 'col'), may hold values from -0.125 to 0.125
- w_down: bfloat16 [6144, 2048], P('col', 'row'), may hold values from -0.078125 to 0.078125
- cotangent: bfloat16 [8192, 2048], P('row', 'col'), may hold values from -6 to 6
Outputs:
- hidden_out: bfloat16 [8192, 2048], P('row', 'col')
- hidden_grad: float32 [8192, 2048], P('row', 'col')
- attn_norm_grad: float32 [2048], P('col')
- query_grad: float32 [2048, 2048], P('row', 'col')
- key_grad: float32 [2048, 1024], P('row', 'col')
- value_grad: float32 [2048, 1024], P('row', 'col')
- query_norm_grad: float32 [128], replicated
- key_norm_grad: float32 [128], replicated
- output_grad: float32 [2048, 2048], P('col', 'row')
- ffwd_norm_grad: float32 [2048], P('col')
- gate_grad: float32 [2048, 6144], P('row', 'col')
- up_grad: float32 [2048, 6144], P('row', 'col')
- down_grad: float32 [6144, 2048], P('col', 'row')
Inputs may be any that keep to these rules, and one draw needn't show every extreme that they name: `seq_lengths`: each row sums to 1024 and has exactly one sequence of 512 tokens.
All inputs are finite; a program needn't handle non-finite values.
Results may differ from a plain program's by a relative error of at most 0.02.
Values may be sent and summed in bfloat16 or wider, within the bound.
No kernel may reach another device: no remote copies, remote signals or barrier semaphores. Data moves between devices by JAX's collectives and lax.ppermute only.
A program may use at most 256 MiB of HBM per device.

v0:
```python
import math

import jax
import jax.numpy as jnp
from jax import lax
from jax.sharding import PartitionSpec as P

EPS = 1e-06
THETA = 1000000.0
NEGATIVE = -1e30


def matrix_multiply(left_side, right_side):
    return jnp.dot(left_side, right_side, preferred_element_type=jnp.float32)


def times_transposed(left_side, right_side):
    return lax.dot_general(
        left_side, right_side, (((1,), (1,)), ((), ())), preferred_element_type=jnp.float32
    )


def transposed_times(left_side, right_side):
    return lax.dot_general(
        left_side, right_side, (((0,), (0,)), ((), ())), preferred_element_type=jnp.float32
    )


def tables(lengths_row, row_number_total):
    steps_idx = jnp.arange(row_number_total, dtype=jnp.int32)
    seq_ends = jnp.cumsum(lengths_row)
    seq_starts = seq_ends - lengths_row
    segment = jnp.sum((steps_idx[:, None] >= seq_ends[None, :]).astype(jnp.int32), 1)
    member = segment[:, None] == jnp.arange(lengths_row.shape[0], dtype=jnp.int32)[None, :]
    position = steps_idx - jnp.sum(jnp.where(member, seq_starts[None, :], 0), 1)
    return (segment, position)


def rotary(position, head_size):
    half_size = head_size // 2
    frequency = THETA ** (-(jnp.arange(half_size, dtype=jnp.float32) * 2.0 / head_size))
    angles = position.astype(jnp.float32)[:, None] * frequency[None, :]
    return (jnp.cos(angles), jnp.sin(angles))


def rotate(values, cos_table, sin_table):
    half_size = values.shape[-1] // 2
    first_half = values[..., :half_size]
    second_half = values[..., half_size:]
    cos_wide = cos_table[:, None, :]
    sin_wide = sin_table[:, None, :]
    return jnp.concatenate(
        [
            first_half * cos_wide - second_half * sin_wide,
            second_half * cos_wide + first_half * sin_wide,
        ],
        -1,
    )


def head_turn(raw_rows, gain_vec, cos_table, sin_table, head_count):
    shaped = raw_rows.reshape(raw_rows.shape[0], head_count, -1)
    normed = shaped * lax.rsqrt(jnp.mean(shaped * shaped, -1, keepdims=True) + EPS) * gain_vec
    return rotate(normed, cos_table, sin_table)


def swish_product(gate_values, up_values):
    return jax.nn.silu(gate_values) * up_values


def spread(values):
    return lax.all_gather(values, "col", axis=1, tiled=True)


def collect(partial_value):
    return lax.psum_scatter(partial_value, "col", scatter_dimension=1, tiled=True)


def norm_forward(row_values, gain_vec, full_width):
    totals = lax.psum(jnp.sum(row_values * row_values, 1), "col")
    factor = lax.rsqrt(totals / full_width + EPS)
    return ((row_values * factor[:, None] * gain_vec).astype(jnp.bfloat16), factor)


def norm_backward(row_values, factor, gain_vec, upstream, full_width):
    weighted = upstream * gain_vec
    totals = lax.psum(jnp.sum(weighted * row_values, 1), "col")
    result = factor[:, None] * weighted - row_values * (factor**3 * totals / full_width)[:, None]
    return (result, jnp.sum(upstream * row_values * factor[:, None], 0))


def block_mask(segment, token_index, start_row, block_rows):
    row_segment = lax.dynamic_slice_in_dim(segment, start_row, block_rows)
    row_index = start_row + jnp.arange(block_rows, dtype=jnp.int32)
    return (row_segment[:, None] == segment[None, :]) & (row_index[:, None] >= token_index[None, :])


def block_scores(query_block, key_turned, allowed, score_factor):
    raw_scores = (
        jnp.einsum("tgrd,ugd->grtu", query_block, key_turned, preferred_element_type=jnp.float32)
        * score_factor
    )
    return jnp.where(allowed[None, None], raw_scores, NEGATIVE)


def local(
    hidden_in,
    seq_lengths,
    attn_norm,
    w_query,
    key_weight,
    value_weight,
    query_norm,
    key_norm,
    w_output,
    ffwd_norm,
    w_gate,
    w_up,
    w_down,
    cotangent,
):
    row_number_total = hidden_in.shape[0]
    part_width = hidden_in.shape[1]
    full_width = part_width * lax.axis_size("col")
    head_size = query_norm.shape[0]
    kv_heads = key_weight.shape[1] // head_size
    q_heads = w_query.shape[1] // head_size
    heads_per_group = q_heads // kv_heads
    block_rows = min(512, row_number_total)
    blocks = row_number_total // block_rows
    score_factor = 1.0 / math.sqrt(head_size)
    segment, position = tables(seq_lengths[0], row_number_total)
    cos_table, sin_table = rotary(position, head_size)
    token_index = jnp.arange(row_number_total, dtype=jnp.int32)
    starts = jnp.arange(blocks, dtype=jnp.int32) * block_rows
    gathered = (
        lax.all_gather(w_query, "row", axis=0, tiled=True),
        lax.all_gather(key_weight, "row", axis=0, tiled=True),
        lax.all_gather(value_weight, "row", axis=0, tiled=True),
        lax.all_gather(w_output, "row", axis=1, tiled=True),
        lax.all_gather(w_gate, "row", axis=0, tiled=True),
        lax.all_gather(w_up, "row", axis=0, tiled=True),
        lax.all_gather(w_down, "row", axis=1, tiled=True),
    )
    query_all, key_all, value_all, output_all, gate_all, up_all, down_all = gathered
    residual = hidden_in.astype(jnp.float32)
    normed_one, factor_one = norm_forward(residual, attn_norm, full_width)
    wide_one = spread(normed_one)
    query_raw = matrix_multiply(wide_one, query_all)
    key_raw = matrix_multiply(wide_one, key_all)
    value_bf = (
        matrix_multiply(wide_one, value_all)
        .astype(jnp.bfloat16)
        .reshape(row_number_total, kv_heads, head_size)
    )

    def turn_query(raw_rows, gain_vec):
        return head_turn(raw_rows, gain_vec, cos_table, sin_table, q_heads)

    def turn_key(raw_rows, gain_vec):
        return head_turn(raw_rows, gain_vec, cos_table, sin_table, kv_heads)

    query_rotated = turn_query(query_raw, query_norm).astype(jnp.bfloat16)
    query_blocks = query_rotated.reshape(blocks, block_rows, kv_heads, heads_per_group, head_size)
    key_turned = turn_key(key_raw, key_norm).astype(jnp.bfloat16)

    def forward_block(packed):
        query_block, start_row = packed
        allowed = block_mask(segment, token_index, start_row, block_rows)
        scores = block_scores(query_block, key_turned, allowed, score_factor)
        row_peak = jnp.max(scores, -1, keepdims=True)
        exp_scores = jnp.exp(scores - row_peak)
        totals = jnp.sum(exp_scores, -1, keepdims=True)
        prob_rows = (exp_scores / totals).astype(jnp.bfloat16)
        mixed_out = jnp.einsum(
            "grtu,ugd->tgrd", prob_rows, value_bf, preferred_element_type=jnp.float32
        )
        return (mixed_out, row_peak + jnp.log(totals))

    mixed_blocks, log_totals = lax.map(forward_block, (query_blocks, starts))
    mixed_bf = mixed_blocks.reshape(row_number_total, q_heads * head_size).astype(jnp.bfloat16)
    attn_out = collect(matrix_multiply(mixed_bf, output_all))
    middle = residual + attn_out
    normed_two, factor_two = norm_forward(middle, ffwd_norm, full_width)
    wide_two = spread(normed_two)
    gate_pre = matrix_multiply(wide_two, gate_all)
    up_pre = matrix_multiply(wide_two, up_all)
    hidden_bf = swish_product(gate_pre, up_pre).astype(jnp.bfloat16)
    hidden_out = (middle + collect(matrix_multiply(hidden_bf, down_all))).astype(jnp.bfloat16)
    back_weights = (
        lax.all_gather(w_query, "row", axis=0, tiled=True),
        lax.all_gather(key_weight, "row", axis=0, tiled=True),
        lax.all_gather(value_weight, "row", axis=0, tiled=True),
        lax.all_gather(w_output, "row", axis=1, tiled=True),
        lax.all_gather(w_gate, "row", axis=0, tiled=True),
        lax.all_gather(w_up, "row", axis=0, tiled=True),
        lax.all_gather(w_down, "row", axis=1, tiled=True),
    )
    query_back, key_back, value_back, output_back, gate_back, up_back, down_back = back_weights
    upstream_wide = spread(cotangent)
    grad_down = transposed_times(hidden_bf, upstream_wide)
    grad_hidden = times_transposed(upstream_wide, down_back)
    _, pull_swish = jax.vjp(swish_product, gate_pre, up_pre)
    grad_gate_pre, grad_up_pre = pull_swish(grad_hidden)
    gate_low = grad_gate_pre.astype(jnp.bfloat16)
    up_low = grad_up_pre.astype(jnp.bfloat16)
    grad_gate = transposed_times(wide_two, gate_low)
    grad_upw = transposed_times(wide_two, up_low)
    grad_normed_two = collect(
        times_transposed(gate_low, gate_back) + times_transposed(up_low, up_back)
    )
    grad_middle_norm, ffwd_gain_grad = norm_backward(
        middle, factor_two, ffwd_norm, grad_normed_two, full_width
    )
    grad_middle = cotangent.astype(jnp.float32) + grad_middle_norm
    middle_wide = spread(grad_middle.astype(jnp.bfloat16))
    grad_output = transposed_times(mixed_bf, middle_wide)
    grad_mixed = times_transposed(middle_wide, output_back).astype(jnp.bfloat16)
    grad_mixed = grad_mixed.reshape(blocks, block_rows, kv_heads, heads_per_group, head_size)

    def backward_block(carried, packed):
        query_block, grad_block, log_block, start_row = packed
        allowed = block_mask(segment, token_index, start_row, block_rows)
        scores = block_scores(query_block, key_turned, allowed, score_factor)
        prob_rows = jnp.exp(scores - log_block)
        prob_low = prob_rows.astype(jnp.bfloat16)
        grad_probs = jnp.einsum(
            "tgrd,ugd->grtu", grad_block, value_bf, preferred_element_type=jnp.float32
        )
        row_delta = jnp.sum(grad_probs * prob_rows, -1, keepdims=True)
        grad_scores = (prob_rows * (grad_probs - row_delta)).astype(jnp.bfloat16)
        grad_qblock = (
            jnp.einsum(
                "grtu,ugd->tgrd", grad_scores, key_turned, preferred_element_type=jnp.float32
            )
            * score_factor
        )
        key_part = (
            jnp.einsum(
                "grtu,tgrd->ugd", grad_scores, query_block, preferred_element_type=jnp.float32
            )
            * score_factor
        )
        value_part = jnp.einsum(
            "grtu,tgrd->ugd", prob_low, grad_block, preferred_element_type=jnp.float32
        )
        return ((carried[0] + key_part, carried[1] + value_part), grad_qblock)

    zero_state = jnp.zeros((row_number_total, kv_heads, head_size), jnp.float32)
    (grad_kturned, grad_value), grad_qturned = lax.scan(
        backward_block, (zero_state, zero_state), (query_blocks, grad_mixed, log_totals, starts)
    )
    grad_qturned = grad_qturned.reshape(row_number_total, q_heads, head_size)
    _, pull_query = jax.vjp(turn_query, query_raw, query_norm)
    grad_query_raw, query_gain_grad = pull_query(grad_qturned)
    _, pull_key = jax.vjp(turn_key, key_raw, key_norm)
    grad_key_raw, key_gain_grad = pull_key(grad_kturned)
    query_low = grad_query_raw.astype(jnp.bfloat16)
    key_low = grad_key_raw.astype(jnp.bfloat16)
    value_low = grad_value.reshape(row_number_total, kv_heads * head_size).astype(jnp.bfloat16)
    grad_query = transposed_times(wide_one, query_low)
    grad_key = transposed_times(wide_one, key_low)
    grad_valuew = transposed_times(wide_one, value_low)
    grad_normed_one = collect(
        times_transposed(query_low, query_back)
        + times_transposed(key_low, key_back)
        + times_transposed(value_low, value_back)
    )
    grad_residual_norm, attn_gain_grad = norm_backward(
        residual, factor_one, attn_norm, grad_normed_one, full_width
    )
    hidden_grad = grad_middle + grad_residual_norm
    grad_totals = (
        lax.psum_scatter(
            grad_query.astype(jnp.bfloat16), "row", scatter_dimension=0, tiled=True
        ).astype(jnp.float32),
        lax.psum_scatter(
            grad_key.astype(jnp.bfloat16), "row", scatter_dimension=0, tiled=True
        ).astype(jnp.float32),
        lax.psum_scatter(
            grad_valuew.astype(jnp.bfloat16), "row", scatter_dimension=0, tiled=True
        ).astype(jnp.float32),
        lax.psum_scatter(
            grad_output.astype(jnp.bfloat16), "row", scatter_dimension=1, tiled=True
        ).astype(jnp.float32),
        lax.psum_scatter(
            grad_gate.astype(jnp.bfloat16), "row", scatter_dimension=0, tiled=True
        ).astype(jnp.float32),
        lax.psum_scatter(
            grad_upw.astype(jnp.bfloat16), "row", scatter_dimension=0, tiled=True
        ).astype(jnp.float32),
        lax.psum_scatter(
            grad_down.astype(jnp.bfloat16), "row", scatter_dimension=1, tiled=True
        ).astype(jnp.float32),
    )
    col_start = lax.axis_index("col") * part_width
    zero_width = jnp.zeros((full_width,), jnp.float32)
    first_wide = lax.dynamic_update_slice_in_dim(zero_width, attn_gain_grad, col_start, 0)
    second_wide = lax.dynamic_update_slice_in_dim(zero_width, ffwd_gain_grad, col_start, 0)
    gain_totals = lax.psum(
        (first_wide, second_wide, query_gain_grad, key_gain_grad), ("row", "col")
    )
    first_part = lax.dynamic_slice_in_dim(gain_totals[0], col_start, part_width)
    second_part = lax.dynamic_slice_in_dim(gain_totals[1], col_start, part_width)
    return (
        hidden_out,
        hidden_grad,
        first_part,
        grad_totals[0],
        grad_totals[1],
        grad_totals[2],
        gain_totals[2],
        gain_totals[3],
        grad_totals[3],
        second_part,
        grad_totals[4],
        grad_totals[5],
        grad_totals[6],
    )


def solution(mesh):
    in_specs = (
        P("row", "col"),
        P("row", None),
        P("col"),
        P("row", "col"),
        P("row", "col"),
        P("row", "col"),
        P(),
        P(),
        P("col", "row"),
        P("col"),
        P("row", "col"),
        P("row", "col"),
        P("col", "row"),
        P("row", "col"),
    )
    out_specs = (
        P("row", "col"),
        P("row", "col"),
        P("col"),
        P("row", "col"),
        P("row", "col"),
        P("row", "col"),
        P(),
        P(),
        P("col", "row"),
        P("col"),
        P("row", "col"),
        P("row", "col"),
        P("col", "row"),
    )
    return jax.shard_map(local, mesh=mesh, in_specs=in_specs, out_specs=out_specs, check_vma=False)
```

profile of v0, /device:TPU:0, one launch (start us, length us, event | category | flops | bytes accessed | tf_op | source)
XLA Modules:
  0.0 1635.5 jit_solution(6513335820717767333)
XLA Ops:
  26.3 26.7 %all-gather.18.cloned.1.call-done = bf16[2048,256]{1,0:T(8,128)(2,1)} async-done(((bf16[256,256]{1,0:T(8,128)(2,1)}), bf16[2048,256]{1,0:T(8,128)(2,1)}) %all-gather.18.cloned.1.call-update) | async-done | bytes 1048592 | tf_op jit(solution)/shard_map/all_gather | solution.py:139
  53.0 35.4 %all-gather.12.cloned.1.call-done = bf16[1024,2048]{1,0:T(8,128)(2,1)} async-done(((bf16[1024,512]{1,0:T(8,128)(2,1)}), bf16[1024,2048]{1,0:T(8,128)(2,1)}) %all-gather.12.cloned.1.call-update) | async-done | bytes 4194320 | tf_op jit(solution)/shard_map/all_gather | solution.py:72
  92.5 38.2 %all-gather.16.cloned.1.call-done = bf16[2048,256]{1,0:T(8,128)(2,1)} async-done(((bf16[256,256]{1,0:T(8,128)(2,1)}), bf16[2048,256]{1,0:T(8,128)(2,1)}) %all-gather.16.cloned.1.call-update) | async-done | bytes 1048592 | tf_op jit(solution)/shard_map/all_gather | solution.py:138
  136.0 44.8 %all-gather.14.cloned.1.call-done = bf16[2048,512]{1,0:T(8,128)(2,1)} async-done(((bf16[256,512]{1,0:T(8,128)(2,1)}), bf16[2048,512]{1,0:T(8,128)(2,1)}) %all-gather.14.cloned.1.call-update) | async-done | bytes 2097168 | tf_op jit(solution)/shard_map/all_gather | solution.py:137
  199.3 25.3 %while.28 = (s32[]{:T(128)}, bf16[2,512,2,2,128]{4,1,3,2,0:T(8,128)(2,1)}, f32[2,2,2,512,1]{3,2,1,4,0:T(2,128)S(1)}, s32[2]{0:T(128)S(1)}, s32[1024]{0:T(1024)S(...) while((s32[]{:T(128)}, ...), condition=%wide.region_10.11_spmd.clone, body=%wide.region_7.10_spmd.clone.sunk | while | flops 1100478976 | bytes 38353136 | solution.py:180
  240.7 69.2 %reduce-scatter.12.cloned.1.call-done = f32[1024,512]{1,0:T(8,128)} async-done(((f32[1024,2048]{1,0:T(8,128)}), f32[1024,512]{1,0:T(8,128)}) %reduce-scatter.12.cloned.1.call-update) | async-done | bytes 2097168 | tf_op jit(solution)/shard_map/reduce_scatter | solution.py:76
  321.2 90.1 %all-gather.26.cloned.1.call-done = bf16[2048,1536]{1,0:T(8,128)(2,1)} async-done(((bf16[256,1536]{1,0:T(8,128)(2,1)}), bf16[2048,1536]{1,0:T(8,128)(2,1)}) %all-gather.26.cloned.1.call-update) | async-done | bytes 6291472 | tf_op jit(solution)/shard_map/all_gather | solution.py:142
  411.4 34.9 %all-gather.22.cloned.1.call-done = bf16[1024,2048]{1,0:T(8,128)(2,1)} async-done(((bf16[1024,512]{1,0:T(8,128)(2,1)}), bf16[1024,2048]{1,0:T(8,128)(2,1)}) %all-gather.22.cloned.1.call-update) | async-done | bytes 4194320 | tf_op jit(solution)/shard_map/all_gather | solution.py:72
  458.1 89.6 %all-gather.24.cloned.1.call-done = bf16[2048,1536]{1,0:T(8,128)(2,1)} async-done(((bf16[256,1536]{1,0:T(8,128)(2,1)}), bf16[2048,1536]{1,0:T(8,128)(2,1)}) %all-gather.24.cloned.1.call-update) | async-done | bytes 6291472 | tf_op jit(solution)/shard_map/all_gather | solution.py:141
  559.4 22.5 %all-gather.30.cloned.1.call-done = bf16[1024,2048]{1,0:T(8,128)(2,1)} async-done(((bf16[1024,512]{1,0:T(8,128)(2,1)}), bf16[1024,2048]{1,0:T(8,128)(2,1)}) %all-gather.30.cloned.1.call-update) | async-done | bytes 4194320 | tf_op jit(solution)/shard_map/all_gather | solution.py:72
  582.0 102.2 %all-gather.28.cloned.1.call-done = bf16[1536,2048]{1,0:T(8,128)(2,1)} async-done(((bf16[1536,256]{1,0:T(8,128)(2,1)}), bf16[1536,2048]{1,0:T(8,128)(2,1)}) %all-gather.28.cloned.1.call-update) | async-done | bytes 6291472 | tf_op jit(solution)/shard_map/all_gather | solution.py:143
  684.2 16.9 %multiply_convert_fusion = (bf16[1024,1536]{1,0:T(8,128)(2,1)}, bf16[1024,1536]{1,0:T(8,128)(2,1)S(1)}, bf16[1024,1536]{1,0:T(8,128)(2,1)}) fusion(f32[1024,1536]{1,0:T(8,128)} %fusion.74, f32[1024,1536]{1,0:T(8,128)} %fusion.75, bf16[1024,2048]{1,0:T(8,128)(2,1)} %all-gather.30.cloned.1.call-done, bf16[1536,2048]{1,0:T(8,128)(2,1)} %all-gather.28.cloned.1.call-done), kind=kOutput, calls=%fused_computation.69 | convolution fusion | flops 6467616768 | bytes 32505856 | tf_op jit(solution)/shard_map/dot_general | solution.py:18
  719.9 70.0 %reduce-scatter.16.cloned.1.call-done = f32[1024,512]{1,0:T(8,128)} async-done(((f32[1024,2048]{1,0:T(8,128)}), f32[1024,512]{1,0:T(8,128)}) %reduce-scatter.16.cloned.1.call-update) | async-done | bytes 2097168 | tf_op jit(solution)/shard_map/reduce_scatter | solution.py:76
  846.1 38.5 %while.29 = (s32[]{:T(128)}, f32[1024,2,128]{0,2,1:T(8,128)S(1)}, f32[1024,2,128]{0,2,1:T(8,128)}, f32[2,512,2,2,128]{4,1,0,3,2:T(8,128)}, bf16[2,512,2,2,128]{4...) while((s32[]{:T(128)}, f32[1024,2,128]{0,2,1:T(8,128)S(1)}, ...), condition=%wide.region_20.21_spmd.clone, body=%wide.region_18.20_spmd.clone.sunk | while | flops 2718956032 | bytes 100211024 | solution.py:250
  938.0 21.4 %reduce-scatter.32.cloned.1.call-done = bf16[1536,256]{1,0:T(8,128)(2,1)} async-done(((bf16[1536,2048]{1,0:T(8,128)(2,1)}), bf16[1536,256]{1,0:T(8,128)(2,1)}) %reduce-scatter.32.cloned.1.call-update) | async-done | bytes 786448 | tf_op jit(solution)/shard_map/reduce_scatter | solution.py:292
  961.8 118.1 %reduce-scatter.30.cloned.1.call-done = bf16[256,1536]{1,0:T(8,128)(2,1)} async-done(((bf16[2048,1536]{1,0:T(8,128)(2,1)}), bf16[256,1536]{1,0:T(8,128)(2,1)}) %reduce-scatter.30.cloned.1.call-update) | async-done | bytes 786448 | tf_op jit(solution)/shard_map/reduce_scatter | solution.py:289
  1082.4 118.1 %reduce-scatter.28.cloned.1.call-done = bf16[256,1536]{1,0:T(8,128)(2,1)} async-done(((bf16[2048,1536]{1,0:T(8,128)(2,1)}), bf16[256,1536]{1,0:T(8,128)(2,1)}) %reduce-scatter.28.cloned.1.call-update) | async-done | bytes 786448 | tf_op jit(solution)/shard_map/reduce_scatter | solution.py:286
  1203.3 63.1 %reduce-scatter.22.cloned.1.call-done = bf16[256,256]{1,0:T(8,128)(2,1)} async-done(((bf16[2048,256]{1,0:T(8,128)(2,1)}), bf16[256,256]{1,0:T(8,128)(2,1)}) %reduce-scatter.22.cloned.1.call-update) | async-done | bytes 131088 | tf_op jit(solution)/shard_map/reduce_scatter | solution.py:277
  1267.9 65.1 %reduce-scatter.24.cloned.1.call-done = bf16[256,256]{1,0:T(8,128)(2,1)} async-done(((bf16[2048,256]{1,0:T(8,128)(2,1)}), bf16[256,256]{1,0:T(8,128)(2,1)}) %reduce-scatter.24.cloned.1.call-update) | async-done | bytes 131088 | tf_op jit(solution)/shard_map/reduce_scatter | solution.py:280
  1334.6 69.3 %reduce-scatter.26.cloned.1.call-done = bf16[512,256]{1,0:T(8,128)(2,1)} async-done(((bf16[512,2048]{1,0:T(8,128)(2,1)}), bf16[512,256]{1,0:T(8,128)(2,1)}) %reduce-scatter.26.cloned.1.call-update) | async-done | bytes 262160 | tf_op jit(solution)/shard_map/reduce_scatter | solution.py:283
  1405.7 68.8 %reduce-scatter.20.cloned.1.call-done = bf16[256,512]{1,0:T(8,128)(2,1)} async-done(((bf16[2048,512]{1,0:T(8,128)(2,1)}), bf16[256,512]{1,0:T(8,128)(2,1)}) %reduce-scatter.20.cloned.1.call-update) | async-done | bytes 262160 | tf_op jit(solution)/shard_map/reduce_scatter | solution.py:274
  1476.3 71.6 %reduce-scatter.18.cloned.1.call-done = f32[1024,512]{1,0:T(8,128)} async-done(((f32[1024,2048]{1,0:T(8,128)}), f32[1024,512]{1,0:T(8,128)}) %reduce-scatter.18.cloned.1.call-update) | async-done | bytes 2097168 | tf_op jit(solution)/shard_map/reduce_scatter | solution.py:76
  1550.7 40.0 %all-reduce.4 = (f32[2048]{0:T(1024)S(1)}, f32[128]{0:T(128)}, f32[128]{0:T(128)}, f32[2048]{0:T(1024)S(1)}) all-reduce(f32[2048]{0:T(1024)S(1)} %dynamic_update_slice.17, f32[128]{0:T(128)S(1)} %get-tuple-element.281, f32[128]{0:T(128)S(1)} %get-tuple-element.287, ...), channel_id=1, replica_groups=mesh['row'=8,'col'=4] {'row','col'}, use_global_device_ids=true, to_apply=%region_27.28 | all-reduce | flops 4352 | bytes 34816 | tf_op jit(solution)/shard_map/psum | solution.py:300
  1599.0 24.3 %reduce-scatter.14.cloned.1.call-done = f32[1024,512]{1,0:T(8,128)} async-done(((f32[1024,2048]{1,0:T(8,128)}), f32[1024,512]{1,0:T(8,128)}) %reduce-scatter.14.cloned.1.call-update) | async-done | bytes 2097168 | tf_op jit(solution)/shard_map/reduce_scatter | solution.py:76
  (311 shorter events, 311.4 us)
Async XLA Ops:
  7.2 45.8 %all-gather.18.cloned.1.call-start = ((), (), s32[]{:S(2)}) async-start(), calls=%async_computation.14 | async-start | bytes 1179648 | tf_op jit(solution)/shard_map/all_gather | solution.py:139
  7.9 80.5 %all-gather.12.cloned.1.call-start = ((), (), s32[]{:S(2)}) async-start(), calls=%async_computation.11 | async-start | bytes 5242880 | tf_op jit(solution)/shard_map/all_gather | solution.py:72
  21.0 109.8 %all-gather.16.cloned.1.call-start = ((), (), s32[]{:S(2)}) async-start(), calls=%async_computation.13 | async-start | bytes 1179648 | tf_op jit(solution)/shard_map/all_gather | solution.py:138
  21.7 159.1 %all-gather.14.cloned.1.call-start = ((), (), s32[]{:S(2)}) async-start(), calls=%async_computation.12 | async-start | bytes 2359296 | tf_op jit(solution)/shard_map/all_gather | solution.py:137
  22.3 210.0 %all-gather.20.cloned.1.call-start = ((), (), s32[]{:S(2)}) async-start(), calls=%async_computation.15 | async-start | bytes 2359296 | tf_op jit(solution)/shard_map/all_gather | solution.py:140
  22.9 287.0 %reduce-scatter.12.cloned.1.call-start = ((), (), s32[]{:S(2)}) async-start(), calls=%async_computation.16 | async-start | bytes 10485760 | tf_op jit(solution)/shard_map/reduce_scatter | solution.py:76
  239.9 171.5 %all-gather.26.cloned.1.call-start = ((), (), s32[]{:S(2)}) async-start(), calls=%async_computation.19 | async-start | bytes 7077888 | tf_op jit(solution)/shard_map/all_gather | solution.py:142
  240.6 205.7 %all-gather.22.cloned.1.call-start = ((), (), s32[]{:S(2)}) async-start(), calls=%async_computation.17 | async-start | bytes 5242880 | tf_op jit(solution)/shard_map/all_gather | solution.py:72
  319.1 228.7 %all-gather.24.cloned.1.call-start = ((), (), s32[]{:S(2)}) async-start(), calls=%async_computation.18 | async-start | bytes 7077888 | tf_op jit(solution)/shard_map/all_gather | solution.py:141
  319.9 262.1 %all-gather.30.cloned.1.call-start = ((), (), s32[]{:S(2)}) async-start(), calls=%async_computation.22 | async-start | bytes 5242880 | tf_op jit(solution)/shard_map/all_gather | solution.py:72
  320.5 363.7 %all-gather.28.cloned.1.call-start = ((), (), s32[]{:S(2)}) async-start(), calls=%async_computation.20 | async-start | bytes 7077888 | tf_op jit(solution)/shard_map/all_gather | solution.py:143
  321.2 468.7 %reduce-scatter.16.cloned.1.call-start = ((), (), s32[]{:S(2)}) async-start(), calls=%async_computation.23 | async-start | bytes 10485760 | tf_op jit(solution)/shard_map/reduce_scatter | solution.py:76
  719.8 117.7 %all-gather.32.cloned.1.call-start = ((), (), s32[]{:S(2)}) async-start(), calls=%async_computation.24 | async-start | bytes 5242880 | tf_op jit(solution)/shard_map/all_gather | solution.py:72
  801.7 157.6 %reduce-scatter.32.cloned.1.call-start = ((), (), s32[]{:S(2)}) async-start(), calls=%async_computation.32 | async-start | bytes 7077888 | tf_op jit(solution)/shard_map/reduce_scatter | solution.py:292
  813.1 266.8 %reduce-scatter.30.cloned.1.call-start = ((), (), s32[]{:S(2)}) async-start(), calls=%async_computation.31 | async-start | bytes 7077888 | tf_op jit(solution)/shard_map/reduce_scatter | solution.py:289
  825.0 375.5 %reduce-scatter.28.cloned.1.call-start = ((), (), s32[]{:S(2)}) async-start(), calls=%async_computation.30 | async-start | bytes 7077888 | tf_op jit(solution)/shard_map/reduce_scatter | solution.py:286
  836.8 429.6 %reduce-scatter.22.cloned.1.call-start = ((), (), s32[]{:S(2)}) async-start(), calls=%async_computation.27 | async-start | bytes 1179648 | tf_op jit(solution)/shard_map/reduce_scatter | solution.py:277
  890.6 442.4 %reduce-scatter.24.cloned.1.call-start = ((), (), s32[]{:S(2)}) async-start(), calls=%async_computation.28 | async-start | bytes 1179648 | tf_op jit(solution)/shard_map/reduce_scatter | solution.py:280
  896.4 507.5 %reduce-scatter.26.cloned.1.call-start = ((), (), s32[]{:S(2)}) async-start(), calls=%async_computation.29 | async-start | bytes 2359296 | tf_op jit(solution)/shard_map/reduce_scatter | solution.py:283
  902.6 571.9 %reduce-scatter.20.cloned.1.call-start = ((), (), s32[]{:S(2)}) async-start(), calls=%async_computation.26 | async-start | bytes 2359296 | tf_op jit(solution)/shard_map/reduce_scatter | solution.py:274
  916.3 631.6 %reduce-scatter.18.cloned.1.call-start = ((), (), s32[]{:S(2)}) async-start(), calls=%async_computation.25 | async-start | bytes 10485760 | tf_op jit(solution)/shard_map/reduce_scatter | solution.py:76
  925.3 698.0 %reduce-scatter.14.cloned.1.call-start = ((), (), s32[]{:S(2)}) async-start(), calls=%async_computation.21 | async-start | bytes 10485760 | tf_op jit(solution)/shard_map/reduce_scatter | solution.py:76
  961.8 586.2 %copy-start.38 = (f32[1024]{0:T(1024)S(1)}, f32[1024]{0:T(1024)}, u32[]{:S(2)}) copy-start(f32[1024]{0:T(1024)} %copy-done.37) | copy-start | bytes 12292
  961.8 586.2 %copy-start.49 = (f32[512]{0:T(512)S(1)}, f32[512]{0:T(512)}, u32[]{:S(2)}) copy-start(f32[512]{0:T(512)} %param.20) | copy-start | bytes 6148
  (65 other events, 4579.9 us)
Sparse Core Ops, SparseCore 0:
  10.1 42.8 all-gather.17
  55.2 33.2 all-gather.11
  90.6 40.1 all-gather.15
  132.7 48.0 all-gather.13
  182.7 49.5 all-gather.19
  240.0 69.8 reduce-scatter.11
  312.3 99.0 all-gather.25
  413.6 32.6 all-gather.21
  448.7 99.0 all-gather.23
  549.3 32.6 all-gather.29
  584.2 99.9 all-gather.27
  719.9 69.8 reduce-scatter.15
  801.9 35.5 all-gather.31
  841.0 118.3 reduce-scatter.31
  962.8 117.0 reduce-scatter.29
  1083.3 117.0 reduce-scatter.27
  1203.7 62.5 reduce-scatter.21
  1270.5 62.4 reduce-scatter.23
  1336.5 67.3 reduce-scatter.25
  1407.9 66.5 reduce-scatter.19
  1477.1 70.7 reduce-scatter.17
  1550.7 72.5 reduce-scatter.13
where the time goes:
time: 1640 us
  waiting for transfers between devices  1250 us (76%)
  matrix products  190 us (12%)
  blocking collectives  66.8 us (4%)
  other arithmetic  62 us (4%)
  local copies, waits for them, and re-layouts  38.4 us (2%)
    reduce_scatter x4, waiting for transfers between devices, collect(): lax.psum_scatter(partial_value, 'col', scatter_dimension=1, tiled=True)  235 us
    reduce_scatter x1, waiting for transfers between devices, local(): lax.psum_scatter(grad_upw.astype(jnp.bfloat16), 'row', scatter_dimension=...  118 us
    reduce_scatter x1, waiting for transfers between devices, local(): lax.psum_scatter(grad_gate.astype(jnp.bfloat16), 'row', scatter_dimension...  118 us
    all_gather x1, waiting for transfers between devices, local(): lax.all_gather(w_down, 'row', axis=1, tiled=True)  102 us
    all_gather x4, waiting for transfers between devices, spread(): return lax.all_gather(values, 'col', axis=1, tiled=True)  93.5 us
    all_gather x1, waiting for transfers between devices, local(): lax.all_gather(w_up, 'row', axis=0, tiled=True)  90.1 us
    all_gather x1, waiting for transfers between devices, local(): lax.all_gather(w_gate, 'row', axis=0, tiled=True)  89.6 us
    reduce_scatter x1, waiting for transfers between devices, local(): lax.psum_scatter(grad_output.astype(jnp.bfloat16), 'row', scatter_dimensi...  69.3 us
  transfers between devices with their start and end apart: 22, of which 22 were waited for; matrix products, arithmetic and copies ran while one was open for 14% of the time, Pallas kernels for 0%

commit v1 on v0

--- a/solution.py
+++ b/solution.py
@@ -68,12 +68,135 @@
     return jax.nn.silu(gate_values) * up_values
 
 
+def ring_order(count):
+    return list(range(0, count, 2)) + list(range(count - 1, 0, -2))
+
+
+class Ring:
+    def __init__(self, count):
+        self.count = count
+        self.half = count // 2
+        order = ring_order(count)
+        self.onward = [(order[i], order[(i + 1) % count]) for i in range(count)]
+        self.backward = [(b, a) for a, b in self.onward]
+        place_of = [order.index(r) for r in range(count)]
+        behind = [[order[(place_of[r] - j) % count] for j in range(count)] for r in range(count)]
+        distance = [[(place_of[r] - place_of[b]) % count for b in range(count)] for r in range(count)]
+        me = lax.axis_index("row")
+        self.behind = jnp.array(behind, jnp.int32)[me]
+        self.distance = jnp.array(distance, jnp.int32)[me]
+
+    def send_on(self, value):
+        return lax.ppermute(value, "row", self.onward)
+
+    def send_back(self, value):
+        return lax.ppermute(value, "row", self.backward)
+
+
+def after(value, *earlier):
+    return lax.optimization_barrier((value,) + earlier)[0]
+
+
+class Gather:
+    def __init__(self, ring, block):
+        self.ring, self.block = ring, block
+        self.from_behind, self.from_ahead = [], []
+        self.last = (block, block)
+
+    def step(self, number, *earlier):
+        ring = self.ring
+        on, back = self.last
+        if number == ring.half - 1:
+            cut = self.block.shape[0] // 2
+            on, back = on[:cut], back[cut:]
+        if earlier:
+            on, back = after(on, *earlier), after(back, *earlier)
+        on, back = ring.send_on(on), ring.send_back(back)
+        self.last = (on, back)
+        if number == ring.half - 1:
+            self.far = jnp.concatenate([on, back], 0)
+        else:
+            self.from_behind.append(on)
+            self.from_ahead.append(back)
+
+    def blocks(self):
+        return [self.block] + self.from_behind + [self.far] + self.from_ahead[::-1]
+
+
+class Scatter:
+    def __init__(self, ring, part):
+        self.ring, self.part = ring, part
+        self.on = self.back = None
+
+    def step(self, number, *earlier):
+        ring = self.ring
+        low = jnp.bfloat16
+        if number == 0:
+            whole = self.part(ring.half)
+            cut = whole.shape[0] // 2
+            on, back = whole[:cut].astype(low), whole[cut:].astype(low)
+        else:
+            on = self.part(ring.half + number)
+            back = self.part(ring.half - number)
+            if number == 1:
+                cut = on.shape[0] // 2
+                on = jnp.concatenate([on[:cut] + self.on, on[cut:]], 0)
+                back = jnp.concatenate([back[:cut], back[cut:] + self.back], 0)
+            else:
+                on, back = on + self.on, back + self.back
+            on, back = on.astype(low), back.astype(low)
+        if earlier:
+            on, back = after(on, *earlier), after(back, *earlier)
+        self.on, self.back = ring.send_on(on), ring.send_back(back)
+        self.last = (self.on, self.back)
+
+    def total(self):
+        return self.part(0) + self.on + self.back
+
+
+def col_swap(value, bit):
+    count = lax.axis_size("col")
+    return lax.ppermute(value, "col", [(i, i ^ bit) for i in range(count)])
+
+
 def spread(values):
-    return lax.all_gather(values, "col", axis=1, tiled=True)
-
-
-def collect(partial_value):
-    return lax.psum_scatter(partial_value, "col", scatter_dimension=1, tiled=True)
+    far = col_swap(values, 2)
+    return [values, col_swap(values, 1), far, col_swap(far, 1)]
+
+
+def spread_rel(ring, values):
+    blocks = jnp.concatenate(spread(values), 1)
+    width = values.shape[1]
+    me = lax.axis_index("col")
+    piece = blocks.shape[1] // ring.count
+    parts = []
+    for j in range(ring.count):
+        start = ring.behind[j] * piece
+        owner, inside = start // width, start % width
+        parts.append(lax.dynamic_slice_in_dim(blocks, (owner ^ me) * width + inside, piece, 1))
+    return jnp.concatenate(parts, 1)
+
+
+def collect_rel(ring, partial_value):
+    count = lax.axis_size("col")
+    width = partial_value.shape[1] // count
+    piece = partial_value.shape[1] // ring.count
+    me = lax.axis_index("col")
+
+    def block(j):
+        first = (me ^ j) * (width // piece)
+        return jnp.concatenate(
+            [
+                lax.dynamic_slice_in_dim(partial_value, ring.distance[first + i] * piece, piece, 1)
+                for i in range(width // piece)
+            ],
+            1,
+        )
+
+    low = jnp.bfloat16
+    near = col_swap(jnp.concatenate([block(1), block(3)], 1).astype(low), 1)
+    far = col_swap((block(2) + near[:, width:]).astype(low), 2)
+    return block(0) + near[:, :width] + far
 
 
 def norm_forward(row_values, gain_vec, full_width):
@@ -133,26 +256,31 @@
     cos_table, sin_table = rotary(position, head_size)
     token_index = jnp.arange(row_number_total, dtype=jnp.int32)
     starts = jnp.arange(blocks, dtype=jnp.int32) * block_rows
-    gathered = (
-        lax.all_gather(w_query, "row", axis=0, tiled=True),
-        lax.all_gather(key_weight, "row", axis=0, tiled=True),
-        lax.all_gather(value_weight, "row", axis=0, tiled=True),
-        lax.all_gather(w_output, "row", axis=1, tiled=True),
-        lax.all_gather(w_gate, "row", axis=0, tiled=True),
-        lax.all_gather(w_up, "row", axis=0, tiled=True),
-        lax.all_gather(w_down, "row", axis=1, tiled=True),
-    )
-    query_all, key_all, value_all, output_all, gate_all, up_all, down_all = gathered
+    ring = Ring(lax.axis_size("row"))
+    steps = ring.half
+    low = jnp.bfloat16
+    q_width, k_width = w_query.shape[1], key_weight.shape[1]
+    qkv_ring = Gather(ring, jnp.concatenate([w_query, key_weight, value_weight], 1))
+    out_ring = Gather(ring, w_output)
+    gate_ring, up_ring = Gather(ring, w_gate), Gather(ring, w_up)
+    ff_half = w_down.shape[0] // 2
+    down_rings = Gather(ring, w_down[:ff_half]), Gather(ring, w_down[ff_half:])
+    queue = [(g, s) for pair in ((qkv_ring, out_ring), (gate_ring, up_ring), down_rings) for s in range(steps) for g in pair]
+    for place, (gather, step) in enumerate(queue):
+        gather.step(step, *(queue[place - 2][0].last if place >= 2 and step == 0 else ()))
+    qkv_all = jnp.concatenate(qkv_ring.blocks(), 0)
+    output_all = jnp.concatenate(out_ring.blocks(), 1)
+    gate_all = jnp.concatenate(gate_ring.blocks(), 0)
+    up_all = jnp.concatenate(up_ring.blocks(), 0)
+    down_all = jnp.concatenate([jnp.concatenate(g.blocks(), 1) for g in down_rings], 0)
     residual = hidden_in.astype(jnp.float32)
     normed_one, factor_one = norm_forward(residual, attn_norm, full_width)
-    wide_one = spread(normed_one)
-    query_raw = matrix_multiply(wide_one, query_all)
-    key_raw = matrix_multiply(wide_one, key_all)
-    value_bf = (
-        matrix_multiply(wide_one, value_all)
-        .astype(jnp.bfloat16)
-        .reshape(row_number_total, kv_heads, head_size)
-    )
+    wide_one = spread_rel(ring, normed_one)
+    upstream_wide = spread_rel(ring, cotangent)
+    qkv_raw = matrix_multiply(wide_one, qkv_all)
+    query_raw = qkv_raw[:, :q_width]
+    key_raw = qkv_raw[:, q_width : q_width + k_width]
+    value_bf = qkv_raw[:, q_width + k_width :].astype(low).reshape(row_number_total, kv_heads, head_size)
 
     def turn_query(raw_rows, gain_vec):
         return head_turn(raw_rows, gain_vec, cos_table, sin_table, q_heads)
@@ -179,43 +307,31 @@
 
     mixed_blocks, log_totals = lax.map(forward_block, (query_blocks, starts))
     mixed_bf = mixed_blocks.reshape(row_number_total, q_heads * head_size).astype(jnp.bfloat16)
-    attn_out = collect(matrix_multiply(mixed_bf, output_all))
+    attn_out = collect_rel(ring, matrix_multiply(mixed_bf, output_all))
     middle = residual + attn_out
     normed_two, factor_two = norm_forward(middle, ffwd_norm, full_width)
-    wide_two = spread(normed_two)
+    wide_two = spread_rel(ring, normed_two)
     gate_pre = matrix_multiply(wide_two, gate_all)
     up_pre = matrix_multiply(wide_two, up_all)
-    hidden_bf = swish_product(gate_pre, up_pre).astype(jnp.bfloat16)
-    hidden_out = (middle + collect(matrix_multiply(hidden_bf, down_all))).astype(jnp.bfloat16)
-    back_weights = (
-        lax.all_gather(w_query, "row", axis=0, tiled=True),
-        lax.all_gather(key_weight, "row", axis=0, tiled=True),
-        lax.all_gather(value_weight, "row", axis=0, tiled=True),
-        lax.all_gather(w_output, "row", axis=1, tiled=True),
-        lax.all_gather(w_gate, "row", axis=0, tiled=True),
-        lax.all_gather(w_up, "row", axis=0, tiled=True),
-        lax.all_gather(w_down, "row", axis=1, tiled=True),
-    )
-    query_back, key_back, value_back, output_back, gate_back, up_back, down_back = back_weights
-    upstream_wide = spread(cotangent)
-    grad_down = transposed_times(hidden_bf, upstream_wide)
-    grad_hidden = times_transposed(upstream_wide, down_back)
+    hidden_bf = swish_product(gate_pre, up_pre).astype(low)
+    hidden_out = (middle + collect_rel(ring, matrix_multiply(hidden_bf, down_all))).astype(low)
+
+    def columns(wide, j):
+        piece = wide.shape[1] // ring.count
+        return wide[:, j * piece : (j + 1) * piece]
+
+    grad_hidden = times_transposed(upstream_wide, down_all)
     _, pull_swish = jax.vjp(swish_product, gate_pre, up_pre)
     grad_gate_pre, grad_up_pre = pull_swish(grad_hidden)
-    gate_low = grad_gate_pre.astype(jnp.bfloat16)
-    up_low = grad_up_pre.astype(jnp.bfloat16)
-    grad_gate = transposed_times(wide_two, gate_low)
-    grad_upw = transposed_times(wide_two, up_low)
-    grad_normed_two = collect(
-        times_transposed(gate_low, gate_back) + times_transposed(up_low, up_back)
-    )
+    gate_low = grad_gate_pre.astype(low)
+    up_low = grad_up_pre.astype(low)
+    grad_normed_two = collect_rel(ring, times_transposed(gate_low, gate_all) + times_transposed(up_low, up_all))
     grad_middle_norm, ffwd_gain_grad = norm_backward(
         middle, factor_two, ffwd_norm, grad_normed_two, full_width
     )
     grad_middle = cotangent.astype(jnp.float32) + grad_middle_norm
-    middle_wide = spread(grad_middle.astype(jnp.bfloat16))
-    grad_output = transposed_times(mixed_bf, middle_wide)
-    grad_mixed = times_transposed(middle_wide, output_back).astype(jnp.bfloat16)
+    middle_wide = spread_rel(ring, grad_middle.astype(low))
+    grad_mixed = times_transposed(middle_wide, output_all).astype(low)
     grad_mixed = grad_mixed.reshape(blocks, block_rows, kv_heads, heads_per_group, head_size)
 
     def backward_block(carried, packed):
@@ -258,41 +374,34 @@
     query_low = grad_query_raw.astype(jnp.bfloat16)
     key_low = grad_key_raw.astype(jnp.bfloat16)
     value_low = grad_value.reshape(row_number_total, kv_heads * head_size).astype(jnp.bfloat16)
-    grad_query = transposed_times(wide_one, query_low)
-    grad_key = transposed_times(wide_one, key_low)
-    grad_valuew = transposed_times(wide_one, value_low)
-    grad_normed_one = collect(
-        times_transposed(query_low, query_back)
-        + times_transposed(key_low, key_back)
-        + times_transposed(value_low, value_back)
+    qkv_low = jnp.concatenate([query_low, key_low, value_low], 1)
+    grad_normed_one = collect_rel(ring, times_transposed(qkv_low, qkv_all))
+    down_sums = tuple(
+        Scatter(ring, lambda j, h=h: transposed_times(h, columns(upstream_wide, j)))
+        for h in (hidden_bf[:, :ff_half], hidden_bf[:, ff_half:])
+    )
+    gate_sum = Scatter(ring, lambda j: transposed_times(columns(wide_two, j), gate_low))
+    up_sum = Scatter(ring, lambda j: transposed_times(columns(wide_two, j), up_low))
+    out_sum = Scatter(ring, lambda j: transposed_times(mixed_bf, columns(middle_wide, j)))
+    qkv_sum = Scatter(ring, lambda j: transposed_times(columns(wide_one, j), qkv_low))
+    queue = [(g, s) for pair in (down_sums, (gate_sum, up_sum), (out_sum, qkv_sum)) for s in range(steps) for g in pair]
+    for place, (scatter, step) in enumerate(queue):
+        scatter.step(step, *(queue[place - 2][0].last if place >= 2 and step == 0 else ()))
+    grad_down = jnp.concatenate([s.total() for s in down_sums], 0)
+    grad_qkv = qkv_sum.total()
+    grad_totals = (
+        grad_qkv[:, :q_width],
+        grad_qkv[:, q_width : q_width + k_width],
+        grad_qkv[:, q_width + k_width :],
+        out_sum.total(),
+        gate_sum.total(),
+        up_sum.total(),
+        grad_down,
     )
     grad_residual_norm, attn_gain_grad = norm_backward(
         residual, factor_one, attn_norm, grad_normed_one, full_width
     )
     hidden_grad = grad_middle + grad_residual_norm
-    grad_totals = (
-        lax.psum_scatter(
-            grad_query.astype(jnp.bfloat16), "row", scatter_dimension=0, tiled=True
-        ).astype(jnp.float32),
-        lax.psum_scatter(
-            grad_key.astype(jnp.bfloat16), "row", scatter_dimension=0, tiled=True
-        ).astype(jnp.float32),
-        lax.psum_scatter(
-            grad_valuew.astype(jnp.bfloat16), "row", scatter_dimension=0, tiled=True
-        ).astype(jnp.float32),
-        lax.psum_scatter(
-            grad_output.astype(jnp.bfloat16), "row", scatter_dimension=1, tiled=True
-        ).astype(jnp.float32),
-        lax.psum_scatter(
-            grad_gate.astype(jnp.bfloat16), "row", scatter_dimension=0, tiled=True
-        ).astype(jnp.float32),
-        lax.psum_scatter(
-            grad_upw.astype(jnp.bfloat16), "row", scatter_dimension=0, tiled=True
-        ).astype(jnp.float32),
-        lax.psum_scatter(
-            grad_down.astype(jnp.bfloat16), "row", scatter_dimension=1, tiled=True
-        ).astype(jnp.float32),
-    )
     col_start = lax.axis_index("col") * part_width
     zero_width = jnp.zeros((full_width,), jnp.float32)
     first_wide = lax.dynamic_update_slice_in_dim(zero_width, attn_gain_grad, col_start, 0)

time: 1640 us -> 884 us (0.54)
  waiting for transfers between devices: 1250 us -> 242 us
  starting transfers between devices: 1.35 us -> 112 us
  local copies, waits for them, and re-layouts: 38.4 us -> 129 us
  blocking collectives: 66.8 us -> 93.5 us
  matrix products: 190 us -> 207 us
    reduce_scatter x11 -> x0, waiting for transfers between devices: 759 us -> none  [the longest x4 235 us: collect(): lax.psum_scatter(partial_value, 'col', scatter_dimension=1, tiled=True)]
    all_gather x11 -> x0, waiting for transfers between devices: 489 us -> none  [the longest x1 102 us: local(): lax.all_gather(w_down, 'row', axis=1, tiled=True)]
    ppermute x0 -> x116, waiting for transfers between devices: none -> 242 us  [the longest x48 137 us: send_on(): return lax.ppermute(value, 'row', self.onward)]
    ppermute x0 -> x116, starting transfers between devices: none -> 112 us  [the longest x48 66.7 us: send_on(): return lax.ppermute(value, 'row', self.onward)]
    unnamed x113 -> x320, local copies, waits for them, and re-layouts: 11.1 us -> 63.5 us
    dot_general x7 -> x48, matrix products: 54.1 us -> 78 us  [transposed_times(): lax.dot_general(left_side, right_side, (((0,), (0,)), ((), ())), preferre...]
    dot_general x7 -> x5, matrix products: 50.1 us -> 38.6 us  [times_transposed(): lax.dot_general(left_side, right_side, (((1,), (1,)), ((), ())), preferre...]
    dot_general x7 -> x5, matrix products: 56 us -> 46.5 us  [matrix_multiply(): return jnp.dot(left_side, right_side, preferred_element_type=jnp.float32)]
  transfers between devices with their start and end apart: 22 -> 116, of which waited for: 22 -> 49; matrix products, arithmetic and copies ran while one was open for 14% -> 32% of each run, Pallas kernels for 0% -> 0%
where the time goes in v1:
time: 884 us; the launch traced here: 877 us
  waiting for transfers between devices  242 us (27%)
  matrix products  207 us (23%)
  local copies, waits for them, and re-layouts  129 us (15%)
  starting transfers between devices  112 us (13%)
  blocking collectives  93.5 us (11%)
  other arithmetic  68.9 us (8%)
  between operations  14.4 us (2%)
    ppermute x48, waiting for transfers between devices, send_on(): return lax.ppermute(value, 'row', self.onward)  137 us
    dot_general x48, matrix products, transposed_times(): lax.dot_general(left_side, right_side, (((0,), (0,)), ((), ())), preferre...  78 us
    ppermute x48, waiting for transfers between devices, send_back(): return lax.ppermute(value, 'row', self.backward)  77.3 us
    ppermute x48, starting transfers between devices, send_on(): return lax.ppermute(value, 'row', self.onward)  66.7 us
    unnamed x320, local copies, waits for them, and re-layouts  63.5 us
    psum x1, blocking collectives, local(): lax.psum((first_wide, second_wide, query_gain_grad, key_gain_grad), ('row...  52.3 us
    dot_general x5, matrix products, matrix_multiply(): return jnp.dot(left_side, right_side, preferred_element_type=jnp.float32)  46.5 us
    dot_general x5, matrix products, times_transposed(): lax.dot_general(left_side, right_side, (((1,), (1,)), ((), ())), preferre...  38.6 us
  transfers between devices with their start and end apart: 116, of which 49 were waited for; matrix products, arithmetic and copies ran while one was open for 32% of the time, Pallas kernels for 0%

profile of v1, /device:TPU:0, one launch (start us, length us, event | category | flops | bytes accessed | tf_op | source)
XLA Modules:
  0.0 876.7 jit_solution(11856182347948679227)
XLA Ops:
  14.5 23.7 %psum.56 = f32[1024]{0:T(1024)S(1)} all-reduce(f32[1024]{0:T(1024)S(1)} %fusion.68), channel_id=1, replica_groups=mesh['row'=8,'col'=4] {'col'}, use_global_device_ids=true, to_apply=%region_1.2 | all-reduce | flops 1024 | bytes 8192 | tf_op jit(solution)/shard_map/psum | solution.py:203
  102.0 13.1 %collective-permute-done.5 = bf16[256,1024]{1,0:T(8,128)(2,1)S(1)} collective-permute-done((bf16[256,1024]{1,0:T(8,128)(2,1)S(1)}, bf16[256,1024]{1,0:T(8,128)(2,1)S(1)}, u32[]{:S(2)}, u32[]{:S(2)}) %collective-permute-start.5) | collective-permute-done | bytes 524320 | tf_op jit(solution)/shard_map/ppermute | solution.py:90
  156.8 29.0 %while.28 = (s32[]{:T(128)}, bf16[2,512,2,2,128]{4,1,3,2,0:T(8,128)(2,1)}, f32[2,2,2,512,1]{3,2,1,4,0:T(2,128)}, s32[2]{0:T(128)S(1)}, s32[1024]{0:T(1024)S(1)},...) while((s32[]{:T(128)}, ...), condition=%wide.region_10.11_spmd.clone, body=%wide.region_7.10_spmd.clone.sunk | while | flops 1100478976 | bytes 38354140 | solution.py:308
  207.3 11.9 %collective-permute-done.34 = bf16[256,1536]{1,0:T(8,128)(2,1)S(1)} collective-permute-done((bf16[256,1536]{1,0:T(8,128)(2,1)}, bf16[256,1536]{1,0:T(8,128)(2,1)S(1)}, u32[]{:S(2)}, u32[]{:S(2)}) %collective-permute-start.34) | collective-permute-done | bytes 786464 | tf_op jit(solution)/shard_map/ppermute | solution.py:90
  222.4 13.7 %collective-permute-done.25 = bf16[256,1536]{1,0:T(8,128)(2,1)S(1)} collective-permute-done((bf16[256,1536]{1,0:T(8,128)(2,1)}, bf16[256,1536]{1,0:T(8,128)(2,1)S(1)}, u32[]{:S(2)}, u32[]{:S(2)}) %collective-permute-start.25) | collective-permute-done | bytes 786464 | tf_op jit(solution)/shard_map/ppermute | solution.py:90
  238.2 6.3 collective-permute-done.35
  254.8 12.2 %collective-permute-done.48 = bf16[768,256]{1,0:T(8,128)(2,1)S(1)} collective-permute-done((bf16[768,256]{1,0:T(8,128)(2,1)S(1)}, bf16[768,256]{1,0:T(8,128)(2,1)S(1)}, u32[]{:S(2)}, u32[]{:S(2)}) %collective-permute-start.48) | collective-permute-done | bytes 393248 | tf_op jit(solution)/shard_map/ppermute | solution.py:90
  343.6 9.8 %fusion.55 = f32[1024,1536]{1,0:T(8,128)} fusion(bf16[1024,2048]{1,0:T(8,128)(2,1)S(1)} %copy-done.91, bf16[768,2048]{1,0:T(8,128)(2,1)S(1)} %copy-done.97, bf16[768,2048]{1,0:T(8,128)(2,1)S(1)} %constant_dynamic-update-slice_fusion.39), kind=kOutput, calls=%fused_computation.79 | convolution fusion | flops 6455033856 | bytes 16777216 | tf_op jit(solution)/shard_map/dot_general | solution.py:18
  359.3 8.6 fusion.267
  367.9 16.8 %fusion.53 = (bf16[1024,1536]{1,0:T(8,128)(2,1)S(1)}, bf16[1024,1536]{1,0:T(8,128)(2,1)S(1)}, bf16[1024,1536]{1,0:T(8,128)(2,1)}) fusion(f32[1024,1536]{1,0:T(8,128)} %fusion.55, f32[1024,1536]{1,0:T(8,128)} %fusion.267, bf16[1024,2048]{1,0:T(8,128)(2,1)} %copy-done.92, bf16[2048,1536]{1,0:T(8,128)(2,1)} %copy-done.86), kind=kOutput, calls=%fused_computation.64 | convolution fusion | flops 6467616768 | bytes 32505856 | tf_op jit(solution)/shard_map/dot_general | solution.py:14
  406.7 9.0 %fusion.268 = f32[1024,2048]{1,0:T(8,128)} fusion(bf16[1024,1536]{1,0:T(8,128)(2,1)S(1)} %get-tuple-element.363, bf16[2048,1536]{1,0:T(8,128)(2,1)S(1)} %bitcast.296), kind=kOutput, calls=%fused_computation.550 | convolution fusion | flops 6442450944 | bytes 17825792 | tf_op jit(solution)/shard_map/dot_general | solution.py:18
  415.7 12.9 %convolution_add_fusion = f32[1024,2048]{1,0:T(8,128)} fusion(f32[1024,2048]{1,0:T(8,128)} %fusion.268, bf16[1024,1536]{1,0:T(8,128)(2,1)S(1)} %get-tuple-element.362, bf16[2048,1536]{1,0:T(8,128)(2,1)} %copy-done.86), kind=kOutput, calls=%fused_computation.81 | convolution fusion | flops 6444548096 | bytes 26214400 | tf_op jit(solution)/shard_map/dot_general | solution.py:18
  434.5 12.2 %fusion.56 = f32[1024,2048]{1,0:T(8,128)} fusion(bf16[1024,1536]{1,0:T(8,128)(2,1)} %get-tuple-element.364, bf16[768,2048]{1,0:T(8,128)(2,1)} %constant_dynamic-update-slice_fusion.46, bf16[768,2048]{1,0:T(8,128)(2,1)} %copy-done.96), kind=kOutput, calls=%fused_computation.80 | convolution fusion | flops 6455033856 | bytes 17825792 | tf_op jit(solution)/shard_map/dot_general | solution.py:14
  508.0 12.3 %collective-permute-done.75 = bf16[768,256]{1,0:T(8,128)(2,1)S(1)} collective-permute-done((bf16[768,256]{1,0:T(8,128)(2,1)S(1)}, bf16[768,256]{1,0:T(8,128)(2,1)S(1)}, u32[]{:S(2)}, u32[]{:S(2)}) %collective-permute-start.75) | collective-permute-done | bytes 393248 | tf_op jit(solution)/shard_map/ppermute | solution.py:93
  547.4 11.8 %collective-permute-done.81 = bf16[256,1536]{1,0:T(8,128)(2,1)S(1)} collective-permute-done((bf16[256,1536]{1,0:T(8,128)(2,1)S(1)}, bf16[256,1536]{1,0:T(8,128)(2,1)S(1)}, u32[]{:S(2)}, u32[]{:S(2)}) %collective-permute-start.81) | collective-permute-done | bytes 786464 | tf_op jit(solution)/shard_map/ppermute | solution.py:93
  565.8 10.2 %collective-permute-done.105 = bf16[256,1536]{1,0:T(8,128)(2,1)S(1)} collective-permute-done((bf16[256,1536]{1,0:T(8,128)(2,1)S(1)}, bf16[256,1536]{1,0:T(8,128)(2,1)S(1)}, u32[]{:S(2)}, u32[]{:S(2)}) %collective-permute-start.105) | collective-permute-done | bytes 786464 | tf_op jit(solution)/shard_map/ppermute | solution.py:93
  610.8 7.5 collective-permute-done.64
  627.1 8.6 collective-permute-done.79
  650.9 51.3 %while.29 = (s32[]{:T(128)}, f32[1024,2,128]{0,2,1:T(8,128)S(1)}, f32[1024,2,128]{0,2,1:T(8,128)}, f32[2,512,2,2,128]{4,1,0,3,2:T(8,128)}, bf16[2,512,2,2,128]{4...) while((s32[]{:T(128)}, f32[1024,2,128]{0,2,1:T(8,128)S(1)}, ...), condition=%wide.region_17.18_spmd.clone, body=%wide.region_15.17_spmd.clone.sunk | while | flops 2718956032 | bytes 163127104 | solution.py:366
  745.6 12.7 %collective-permute-done.110 = bf16[512,256]{1,0:T(8,128)(2,1)S(1)} collective-permute-done((bf16[512,256]{1,0:T(8,128)(2,1)S(1)}, bf16[512,256]{1,0:T(8,128)(2,1)S(1)}, u32[]{:S(2)}, u32[]{:S(2)}) %collective-permute-start.110) | collective-permute-done | bytes 262176 | tf_op jit(solution)/shard_map/ppermute | solution.py:90
  766.0 12.2 %collective-permute-done.86 = bf16[256,1024]{1,0:T(8,128)(2,1)S(1)} collective-permute-done((bf16[256,1024]{1,0:T(8,128)(2,1)S(1)}, bf16[256,1024]{1,0:T(8,128)(2,1)S(1)}, u32[]{:S(2)}, u32[]{:S(2)}) %collective-permute-start.86) | collective-permute-done | bytes 524320 | tf_op jit(solution)/shard_map/ppermute | solution.py:90
  796.4 12.6 %collective-permute-done.67 = bf16[1024,512]{1,0:T(8,128)(2,1)S(1)} collective-permute-done((bf16[1024,512]{1,0:T(8,128)(2,1)S(1)}, bf16[1024,512]{1,0:T(8,128)(2,1)S(1)}, u32[]{:S(2)}, u32[]{:S(2)}) %collective-permute-start.67) | collective-permute-done | bytes 1048608 | tf_op jit(solution)/shard_map/ppermute | solution.py:159
  810.3 52.3 %all-reduce.4 = (f32[2048]{0:T(1024)S(1)}, f32[128]{0:T(128)}, f32[128]{0:T(128)}, f32[2048]{0:T(1024)S(1)}) all-reduce(f32[2048]{0:T(1024)S(1)} %dynamic_update_slice.17, f32[128]{0:T(128)S(1)} %get-tuple-element.305, f32[128]{0:T(128)S(1)} %get-tuple-element.311, ...), channel_id=1, replica_groups=mesh['row'=8,'col'=4] {'row','col'}, use_global_device_ids=true, to_apply=%region_23.24 | all-reduce | flops 4352 | bytes 34816 | tf_op jit(solution)/shard_map/psum | solution.py:409
  869.8 6.5 fusion.73
  (818 shorter events, 556.8 us)
Async XLA Ops:
  6.0 60.7 %collective-permute-start.3 = (bf16[256,1024]{1,0:T(8,128)(2,1)}, bf16[256,1024]{1,0:T(8,128)(2,1)}, u32[]{:S(2)}, u32[]{:S(2)}) collective-permute-start(bf16[256,1024]{1,0:T(8,128)(2,1)} %get-tuple-element.427), channel_id=1, source_target_pairs={{0,8},{8,16},{16,24},{24,28},{28,20},{20,12},{12,4},{4,0},{1,9},{9... | collective-permute-start | bytes 1572872 | tf_op jit(solution)/shard_map/ppermute | solution.py:90
  9.0 67.8 %collective-permute-start.7 = (bf16[256,1024]{1,0:T(8,128)(2,1)}, bf16[256,1024]{1,0:T(8,128)(2,1)}, u32[]{:S(2)}, u32[]{:S(2)}) collective-permute-start(bf16[256,1024]{1,0:T(8,128)(2,1)} %get-tuple-element.427), channel_id=1, source_target_pairs={{8,0},{16,8},{24,16},{28,24},{20,28},{12,20},{4,12},{0,4},{9,1},{1... | collective-permute-start | bytes 1572872 | tf_op jit(solution)/shard_map/ppermute | solution.py:93
  9.0 35.5 %collective-permute-start.11 = (bf16[512,256]{1,0:T(8,128)(2,1)}, bf16[512,256]{1,0:T(8,128)(2,1)S(1)}, u32[]{:S(2)}, u32[]{:S(2)}) collective-permute-start(bf16[512,256]{1,0:T(8,128)(2,1)} %param.28), channel_id=1, source_target_pairs={{0,8},{8,16},{16,24},{24,28},{28,20},{20,12},{12,4},{4,0},{1,9},{9... | collective-permute-start | bytes 786440 | tf_op jit(solution)/shard_map/ppermute | solution.py:90
  11.1 36.1 %collective-permute-start.15 = (bf16[512,256]{1,0:T(8,128)(2,1)}, bf16[512,256]{1,0:T(8,128)(2,1)}, u32[]{:S(2)}, u32[]{:S(2)}) collective-permute-start(bf16[512,256]{1,0:T(8,128)(2,1)} %param.28), channel_id=1, source_target_pairs={{8,0},{16,8},{24,16},{28,24},{20,28},{12,20},{4,12},{0,4},{9,1},{1... | collective-permute-start | bytes 786440 | tf_op jit(solution)/shard_map/ppermute | solution.py:93
  11.1 76.2 %collective-permute-start.59 = (bf16[1024,512]{1,0:T(8,128)(2,1)}, bf16[1024,512]{1,0:T(8,128)(2,1)}, u32[]{:S(2)}, u32[]{:S(2)}) collective-permute-start(bf16[1024,512]{1,0:T(8,128)(2,1)} %param.33), channel_id=1, source_target_pairs={{0,2},{1,3},{2,0},{3,1},{4,6},{5,7},{6,4},{7,5},{8,10},{9,11},{10,... | collective-permute-start | bytes 3145736 | tf_op jit(solution)/shard_map/ppermute | solution.py:159
  54.3 35.8 %collective-permute-start.58 = (bf16[1024,512]{1,0:T(8,128)(2,1)S(1)}, bf16[1024,512]{1,0:T(8,128)(2,1)}, u32[]{:S(2)}, u32[]{:S(2)}) collective-permute-start(bf16[1024,512]{1,0:T(8,128)(2,1)S(1)} %copy-done.32), channel_id=1, source_target_pairs={{0,1},{1,0},{2,3},{3,2},{4,5},{5,4},{6,7},{7,6},{8,9},{9,8},{10,11... | collective-permute-start | bytes 3145736 | tf_op jit(solution)/shard_map/ppermute | solution.py:159
  87.3 33.8 %collective-permute-start.32 = (bf16[256,1536]{1,0:T(8,128)(2,1)}, bf16[256,1536]{1,0:T(8,128)(2,1)}, u32[]{:S(2)}, u32[]{:S(2)}) collective-permute-start(bf16[256,1536]{1,0:T(8,128)(2,1)} %param.31), channel_id=1, source_target_pairs={{0,8},{8,16},{16,24},{24,28},{28,20},{20,12},{12,4},{4,0},{1,9},{9... | collective-permute-start | bytes 2359304 | tf_op jit(solution)/shard_map/ppermute | solution.py:90
  126.0 72.5 %collective-permute-start.33 = (bf16[256,1536]{1,0:T(8,128)(2,1)}, bf16[256,1536]{1,0:T(8,128)(2,1)}, u32[]{:S(2)}, u32[]{:S(2)}) collective-permute-start(bf16[256,1536]{1,0:T(8,128)(2,1)} %collective-permute-done.32), channel_id=1, source_target_pairs={{0,8},{8,16},{16,24},{24,28},{28,20},{20,12},{12,4},{4,0},{1,9},{9... | collective-permute-start | bytes 2359304 | tf_op jit(solution)/shard_map/ppermute | solution.py:90
  127.5 72.4 %collective-permute-start.37 = (bf16[256,1536]{1,0:T(8,128)(2,1)}, bf16[256,1536]{1,0:T(8,128)(2,1)}, u32[]{:S(2)}, u32[]{:S(2)}) collective-permute-start(bf16[256,1536]{1,0:T(8,128)(2,1)} %collective-permute-done.36), channel_id=1, source_target_pairs={{8,0},{16,8},{24,16},{28,24},{20,28},{12,20},{4,12},{0,4},{9,1},{1... | collective-permute-start | bytes 2359304 | tf_op jit(solution)/shard_map/ppermute | solution.py:93
  129.4 71.7 %collective-permute-start.24 = (bf16[256,1536]{1,0:T(8,128)(2,1)}, bf16[256,1536]{1,0:T(8,128)(2,1)}, u32[]{:S(2)}, u32[]{:S(2)}) collective-permute-start(bf16[256,1536]{1,0:T(8,128)(2,1)} %param.30), channel_id=1, source_target_pairs={{0,8},{8,16},{16,24},{24,28},{28,20},{20,12},{12,4},{4,0},{1,9},{9... | collective-permute-start | bytes 2359304 | tf_op jit(solution)/shard_map/ppermute | solution.py:90
  130.8 71.7 %collective-permute-start.28 = (bf16[256,1536]{1,0:T(8,128)(2,1)}, bf16[256,1536]{1,0:T(8,128)(2,1)}, u32[]{:S(2)}, u32[]{:S(2)}) collective-permute-start(bf16[256,1536]{1,0:T(8,128)(2,1)} %param.30), channel_id=1, source_target_pairs={{8,0},{16,8},{24,16},{28,24},{20,28},{12,20},{4,12},{0,4},{9,1},{1... | collective-permute-start | bytes 2359304 | tf_op jit(solution)/shard_map/ppermute | solution.py:93
  193.9 78.1 %collective-permute-start.19 = (bf16[1024,1024]{1,0:T(8,128)(2,1)S(1)}, bf16[1024,1024]{1,0:T(8,128)(2,1)S(1)}, u32[]{:S(2)}, u32[]{:S(2)}) collective-permute-start(bf16[1024,1024]{1,0:T(8,128)(2,1)S(1)} %pad_maximum_fusion.6), channel_id=1, source_target_pairs={{0,1},{1,0},{2,3},{3,2},{4,5},{5,4},{6,7},{7,6},{8,9},{9,8},{10,11... | collective-permute-start | bytes 6291464 | tf_op jit(solution)/shard_map/ppermute | solution.py:159
  201.1 35.0 %collective-permute-start.25 = (bf16[256,1536]{1,0:T(8,128)(2,1)}, bf16[256,1536]{1,0:T(8,128)(2,1)S(1)}, u32[]{:S(2)}, u32[]{:S(2)}) collective-permute-start(bf16[256,1536]{1,0:T(8,128)(2,1)} %collective-permute-done.24), channel_id=1, source_target_pairs={{0,8},{8,16},{16,24},{24,28},{28,20},{20,12},{12,4},{4,0},{1,9},{9... | collective-permute-start | bytes 2359304 | tf_op jit(solution)/shard_map/ppermute | solution.py:90
  202.6 34.9 %collective-permute-start.29 = (bf16[256,1536]{1,0:T(8,128)(2,1)}, bf16[256,1536]{1,0:T(8,128)(2,1)S(1)}, u32[]{:S(2)}, u32[]{:S(2)}) collective-permute-start(bf16[256,1536]{1,0:T(8,128)(2,1)} %collective-permute-done.28), channel_id=1, source_target_pairs={{8,0},{16,8},{24,16},{28,24},{20,28},{12,20},{4,12},{0,4},{9,1},{1... | collective-permute-start | bytes 2359304 | tf_op jit(solution)/shard_map/ppermute | solution.py:93
  237.5 33.8 %collective-permute-start.30 = (bf16[256,1536]{1,0:T(8,128)(2,1)S(1)}, bf16[256,1536]{1,0:T(8,128)(2,1)S(1)}, u32[]{:S(2)}, u32[]{:S(2)}) collective-permute-start(bf16[256,1536]{1,0:T(8,128)(2,1)S(1)} %collective-permute-done.29), channel_id=1, source_target_pairs={{8,0},{16,8},{24,16},{28,24},{20,28},{12,20},{4,12},{0,4},{9,1},{1... | collective-permute-start | bytes 2359304 | tf_op jit(solution)/shard_map/ppermute | solution.py:93
  272.4 38.1 %collective-permute-start.20 = (bf16[1024,512]{1,0:T(8,128)(2,1)S(1)}, bf16[1024,512]{1,0:T(8,128)(2,1)S(1)}, u32[]{:S(2)}, u32[]{:S(2)}) collective-permute-start(bf16[1024,512]{1,0:T(8,128)(2,1)S(1)} %fusion.77), channel_id=1, source_target_pairs={{0,2},{1,3},{2,0},{3,1},{4,6},{5,7},{6,4},{7,5},{8,10},{9,11},{10,... | collective-permute-start | bytes 3145736 | tf_op jit(solution)/shard_map/ppermute | solution.py:159
  463.7 81.8 %collective-permute-start.61 = (bf16[1024,1024]{1,0:T(8,128)(2,1)S(1)}, bf16[1024,1024]{1,0:T(8,128)(2,1)S(1)}, u32[]{:S(2)}, u32[]{:S(2)}) collective-permute-start(bf16[1024,1024]{1,0:T(8,128)(2,1)S(1)} %pad_maximum_fusion.8), channel_id=1, source_target_pairs={{0,1},{1,0},{2,3},{3,2},{4,5},{5,4},{6,7},{7,6},{8,9},{9,8},{10,11... | collective-permute-start | bytes 6291464 | tf_op jit(solution)/shard_map/ppermute | solution.py:159
  520.3 86.9 %collective-permute-start.56 = (bf16[1024,1024]{1,0:T(8,128)(2,1)}, bf16[1024,1024]{1,0:T(8,128)(2,1)}, u32[]{:S(2)}, u32[]{:S(2)}) collective-permute-start(bf16[1024,1024]{1,0:T(8,128)(2,1)} %pad_maximum_fusion.7), channel_id=1, source_target_pairs={{0,1},{1,0},{2,3},{3,2},{4,5},{5,4},{6,7},{7,6},{8,9},{9,8},{10,11... | collective-permute-start | bytes 6291464 | tf_op jit(solution)/shard_map/ppermute | solution.py:159
  545.5 48.0 %collective-permute-start.101 = (bf16[256,1536]{1,0:T(8,128)(2,1)}, bf16[256,1536]{1,0:T(8,128)(2,1)}, u32[]{:S(2)}, u32[]{:S(2)}) collective-permute-start(bf16[256,1536]{1,0:T(8,128)(2,1)} %pad_maximum_fusion.15), channel_id=1, source_target_pairs={{0,8},{8,16},{16,24},{24,28},{28,20},{20,12},{12,4},{4,0},{1,9},{9... | collective-permute-start | bytes 2359304 | tf_op jit(solution)/shard_map/ppermute | solution.py:90
  562.8 34.9 %collective-permute-start.82 = (bf16[256,1536]{1,0:T(8,128)(2,1)}, bf16[256,1536]{1,0:T(8,128)(2,1)}, u32[]{:S(2)}, u32[]{:S(2)}) collective-permute-start(bf16[256,1536]{1,0:T(8,128)(2,1)} %fusion.62), channel_id=1, source_target_pairs={{8,0},{16,8},{24,16},{28,24},{20,28},{12,20},{4,12},{0,4},{9,1},{1... | collective-permute-start | bytes 2359304 | tf_op jit(solution)/shard_map/ppermute | solution.py:93
  621.7 105.3 %collective-permute-start.107 = (bf16[256,1536]{1,0:T(8,128)(2,1)}, bf16[256,1536]{1,0:T(8,128)(2,1)}, u32[]{:S(2)}, u32[]{:S(2)}) collective-permute-start(bf16[256,1536]{1,0:T(8,128)(2,1)} %fusion.65), channel_id=1, source_target_pairs={{8,0},{16,8},{24,16},{28,24},{20,28},{12,20},{4,12},{0,4},{9,1},{1... | collective-permute-start | bytes 2359304 | tf_op jit(solution)/shard_map/ppermute | solution.py:93
  626.8 100.3 %collective-permute-start.103 = (bf16[256,1536]{1,0:T(8,128)(2,1)}, bf16[256,1536]{1,0:T(8,128)(2,1)}, u32[]{:S(2)}, u32[]{:S(2)}) collective-permute-start(bf16[256,1536]{1,0:T(8,128)(2,1)} %fusion.63), channel_id=1, source_target_pairs={{0,8},{8,16},{16,24},{24,28},{28,20},{20,12},{12,4},{4,0},{1,9},{9... | collective-permute-start | bytes 2359304 | tf_op jit(solution)/shard_map/ppermute | solution.py:90
  732.0 50.4 %collective-permute-start.66 = (bf16[1024,1024]{1,0:T(8,128)(2,1)S(1)}, bf16[1024,1024]{1,0:T(8,128)(2,1)S(1)}, u32[]{:S(2)}, u32[]{:S(2)}) collective-permute-start(bf16[1024,1024]{1,0:T(8,128)(2,1)S(1)} %pad_maximum_fusion.10), channel_id=1, source_target_pairs={{0,1},{1,0},{2,3},{3,2},{4,5},{5,4},{6,7},{7,6},{8,9},{9,8},{10,11... | collective-permute-start | bytes 6291464 | tf_op jit(solution)/shard_map/ppermute | solution.py:159
  788.0 81.7 %collective-permute-start.57 = (bf16[1024,512]{1,0:T(8,128)(2,1)}, bf16[1024,512]{1,0:T(8,128)(2,1)}, u32[]{:S(2)}, u32[]{:S(2)}) collective-permute-start(bf16[1024,512]{1,0:T(8,128)(2,1)} %fusion.81), channel_id=1, source_target_pairs={{0,2},{1,3},{2,0},{3,1},{4,6},{5,7},{6,4},{7,5},{8,10},{9,11},{10,... | collective-permute-start | bytes 3145736 | tf_op jit(solution)/shard_map/ppermute | solution.py:159
  (228 other events, 4674.5 us)

commit v2 on v1

v2 whole, which is shorter than its diff:
```python
import math

import jax
import jax.numpy as jnp
from jax import lax
from jax.experimental import pallas as pl
from jax.experimental.pallas import tpu as pltpu
from jax.sharding import PartitionSpec as P

EPS = 1e-06
THETA = 1000000.0
NEGATIVE = -1e30
MOST = 512


def tables(lengths_row, row_number_total):
    steps_idx = jnp.arange(row_number_total, dtype=jnp.int32)
    seq_ends = jnp.cumsum(lengths_row)
    seq_starts = seq_ends - lengths_row
    segment = jnp.sum((steps_idx[:, None] >= seq_ends[None, :]).astype(jnp.int32), 1)
    member = segment[:, None] == jnp.arange(lengths_row.shape[0], dtype=jnp.int32)[None, :]
    return steps_idx - jnp.sum(jnp.where(member, seq_starts[None, :], 0), 1)


def rotary(position, head_size):
    half_size = head_size // 2
    frequency = THETA ** (-(jnp.arange(half_size, dtype=jnp.float32) * 2.0 / head_size))
    angles = position.astype(jnp.float32)[:, None] * frequency[None, :]
    cosines, sines = jnp.cos(angles), jnp.sin(angles)
    return jnp.concatenate([cosines, cosines], 1), jnp.concatenate([-sines, sines], 1)


def ring_order(count):
    return list(range(0, count, 2)) + list(range(count - 1, 0, -2))


class Ring:
    def __init__(self):
        rows = lax.axis_size("row")
        self.count = count = min(8, rows)
        self.half = count // 2
        self.members = members = rows // count
        self.groups = [[g * members + m for m in range(members)] for g in range(count)]
        order = ring_order(count)
        pairs = [(order[i], order[(i + 1) % count]) for i in range(count)]
        self.onward = [(a * members + m, b * members + m) for a, b in pairs for m in range(members)]
        self.backward = [(b, a) for a, b in self.onward]
        cols = lax.axis_size("col")
        per_col = count // cols
        behind = [[order[(order.index(g) - j) % count] for j in range(count)] for g in range(count)]
        place = [
            [[COL_ORDER.index((b // per_col) ^ c) * per_col + b % per_col for b in row] for c in range(cols)]
            for row in behind
        ]
        self.place = jnp.array(place, jnp.int32)[lax.axis_index("row") // members, lax.axis_index("col")]

    def send_on(self, value):
        return lax.ppermute(value, "row", self.onward)

    def send_back(self, value):
        return lax.ppermute(value, "row", self.backward)


def after(value, *earlier):
    return lax.optimization_barrier((value,) + earlier)[0]


class Gather:
    def __init__(self, ring, block, axis):
        if ring.members > 1:
            block = lax.all_gather(block, "row", axis=axis, tiled=True, axis_index_groups=ring.groups)
        self.ring, self.block = ring, block
        self.from_behind, self.from_ahead = [], []
        self.last = (block, block)

    def step(self, number, *earlier):
        ring = self.ring
        on, back = self.last
        if number == ring.half - 1:
            cut = self.block.shape[0] // 2
            on, back = on[:cut], back[cut:]
        if earlier:
            on, back = after(on, *earlier), after(back, *earlier)
        on, back = ring.send_on(on), ring.send_back(back)
        self.last = (on, back)
        if number == ring.half - 1:
            self.far = jnp.concatenate([on, back], 0)
        else:
            self.from_behind.append(on)
            self.from_ahead.append(back)

    def blocks(self):
        return [self.block] + self.from_behind + [self.far] + self.from_ahead[::-1]


class Scatter:
    def __init__(self, ring, part, axis):
        self.ring, self.part, self.axis = ring, part, axis
        self.on = self.back = None

    def step(self, number, *earlier):
        ring = self.ring
        low = jnp.bfloat16
        if number == 0:
            whole = self.part(ring.half)
            cut = whole.shape[0] // 2
            on, back = whole[:cut].astype(low), whole[cut:].astype(low)
        else:
            on = self.part(ring.half + number)
            back = self.part(ring.half - number)
            if number == 1:
                cut = on.shape[0] // 2
                on = jnp.concatenate([on[:cut] + self.on, on[cut:]], 0)
                back = jnp.concatenate([back[:cut], back[cut:] + self.back], 0)
            else:
                on, back = on + self.on, back + self.back
            on, back = on.astype(low), back.astype(low)
        if earlier:
            on, back = after(on, *earlier), after(back, *earlier)
        self.on, self.back = ring.send_on(on), ring.send_back(back)
        self.last = (self.on, self.back)

    def total(self):
        value = self.part(0) + self.on + self.back
        if self.ring.members == 1:
            return value
        return lax.psum_scatter(
            value.astype(jnp.bfloat16),
            "row",
            scatter_dimension=self.axis,
            tiled=True,
            axis_index_groups=self.ring.groups,
        ).astype(jnp.float32)


COL_ORDER = (0, 2, 1, 3)


def swap(value, axis, bit):
    return lax.ppermute(value, axis, [(i, i ^ bit) for i in range(lax.axis_size(axis))])


def spread(values):
    far = swap(values, "col", 2)
    return [values, far, swap(values, "col", 1), swap(far, "col", 1)]


def collect(keep, send):
    near = swap(send, "col", 1)
    width = keep.shape[1] // 2
    both = keep.astype(jnp.float32) + near
    far = swap(both[:, width:].astype(jnp.bfloat16), "col", 2)
    return both[:, :width] + far


def sum_over(value, axis):
    bit = 1
    while bit < lax.axis_size(axis):
        value = value + swap(value, axis, bit)
        bit *= 2
    return value


def dot_nt(left_side, right_side):
    return lax.dot_general(
        left_side, right_side, (((1,), (1,)), ((), ())), preferred_element_type=jnp.float32
    )


def dot_nn(left_side, right_side):
    return jnp.dot(left_side, right_side, preferred_element_type=jnp.float32)


def dot_tn(left_side, right_side):
    return lax.dot_general(
        left_side, right_side, (((0,), (0,)), ((), ())), preferred_element_type=jnp.float32
    )


def cost(flops, *arrays):
    moved = sum(math.prod(a.shape) * jnp.dtype(a.dtype).itemsize for a in arrays)
    return pl.CostEstimate(flops=flops, bytes_accessed=moved, transcendentals=0)


def kernel_call(body, places, operands, specs, outs, out_specs, grid, scratch, flops, mib):
    return pl.pallas_call(
        body,
        grid_spec=pltpu.PrefetchScalarGridSpec(
            num_scalar_prefetch=1,
            grid=grid,
            in_specs=specs,
            out_specs=out_specs,
            scratch_shapes=scratch,
        ),
        out_shape=outs,
        cost_estimate=cost(flops, *operands, *outs),
        compiler_params=pltpu.CompilerParams(vmem_limit_bytes=mib << 20),
    )(places, *operands)


def whole_spec(array, buffers=1):
    zeros = (0,) * len(array.shape)
    return pl.BlockSpec(array.shape, lambda *_: zeros, pipeline_mode=pl.Buffered(buffers))


def rows_spec(array, rows):
    return pl.BlockSpec((rows,) + tuple(array.shape[1:]), lambda i, *_: (i,) + (0,) * (len(array.shape) - 1))


def columns_spec(array, columns):
    return pl.BlockSpec((array.shape[0], columns), lambda i, *_: (0, i))


def shape_of(shape, dtype):
    return jax.ShapeDtypeStruct(shape, dtype)


def piece_at(place_ref, j, piece):
    return pl.ds(pl.multiple_of(place_ref[j] * piece, piece), piece)


def gather_norm_matmul(place, hidden_blocks, gain, weights, eps):
    tokens, width = hidden_blocks[0].shape
    full = width * len(hidden_blocks)
    count = len(weights)
    piece, columns = weights[0].shape
    tile = min(512, columns)
    many = len(hidden_blocks)

    def body(place_ref, *refs):
        x_refs, gain_ref = refs[:many], refs[many]
        w_refs = refs[many + 1 : many + 1 + count]
        wide_ref, factor_ref, out_ref, all_ref = refs[many + 1 + count :]

        @pl.when(pl.program_id(0) == 0)
        def _():
            total = jnp.zeros((tokens, 1), jnp.float32)
            for i in range(many):
                value = x_refs[i][...]
                all_ref[:, i * width : (i + 1) * width] = value
                value = value.astype(jnp.float32)
                total = total + jnp.sum(value * value, 1, keepdims=True)
            factor = lax.rsqrt(total / full + eps)
            factor_ref[...] = factor
            for j in range(count):
                at = piece_at(place_ref, j, piece)
                value = all_ref[:, at].astype(jnp.float32) * factor * gain_ref[:, at]
                wide_ref[:, j * piece : (j + 1) * piece] = value.astype(jnp.bfloat16)

        total = dot_nn(wide_ref[:, :piece], w_refs[0][...])
        for j in range(1, count):
            total = total + dot_nn(wide_ref[:, j * piece : (j + 1) * piece], w_refs[j][...])
        out_ref[...] = total

    outs = (
        shape_of((tokens, full), jnp.bfloat16),
        shape_of((tokens, 1), jnp.float32),
        shape_of((tokens, columns), jnp.float32),
    )
    operands = (*hidden_blocks, gain, *weights)
    specs = [whole_spec(b) for b in hidden_blocks] + [whole_spec(gain)] + [columns_spec(w, tile) for w in weights]
    out_specs = (whole_spec(outs[0]), whole_spec(outs[1]), columns_spec(outs[2], tile))
    scratch = [pltpu.VMEM((tokens, full), jnp.bfloat16)]
    return kernel_call(
        body, place, operands, specs, outs, out_specs, (columns // tile,), scratch, 2 * tokens * full * columns, 48
    )


def gather_swish(place, blocks, gates, ups):
    tokens, width = blocks[0].shape
    full, many, count = width * len(blocks), len(blocks), len(gates)
    piece, columns = gates[0].shape
    tile = min(256, columns)

    def body(place_ref, *refs):
        x_refs, g_refs, u_refs = refs[:many], refs[many : many + count], refs[many + count : many + 2 * count]
        wide_ref, gate_ref, up_ref, hidden_ref, all_ref = refs[many + 2 * count :]

        @pl.when(pl.program_id(0) == 0)
        def _():
            for i in range(many):
                all_ref[:, i * width : (i + 1) * width] = x_refs[i][...]
            for j in range(count):
                wide_ref[:, j * piece : (j + 1) * piece] = all_ref[:, piece_at(place_ref, j, piece)]

        def product(w_refs):
            total = dot_nn(wide_ref[:, :piece], w_refs[0][...])
            for j in range(1, count):
                total = total + dot_nn(wide_ref[:, j * piece : (j + 1) * piece], w_refs[j][...])
            return total

        gate = product(g_refs)
        gate_ref[...] = gate
        up = product(u_refs)
        up_ref[...] = up
        hidden_ref[...] = (gate / (1.0 + jnp.exp(-gate)) * up).astype(jnp.bfloat16)

    outs = (
        shape_of((tokens, full), jnp.bfloat16),
        shape_of((tokens, columns), jnp.float32),
        shape_of((tokens, columns), jnp.float32),
        shape_of((tokens, columns), jnp.bfloat16),
    )
    operands = (*blocks, *gates, *ups)
    specs = [whole_spec(b) for b in blocks] + [columns_spec(w, tile) for w in (*gates, *ups)]
    out_specs = (whole_spec(outs[0]),) + tuple(columns_spec(o, tile) for o in outs[1:])
    scratch = [pltpu.VMEM((tokens, full), jnp.bfloat16)]
    return kernel_call(
        body, place, operands, specs, outs, out_specs, (columns // tile,), scratch, 4 * tokens * full * columns, 48
    )


def spread_product(place, lefts, groups, transposed):
    tokens = lefts[0].shape[0]
    count = len(groups[0])
    piece = groups[0][0].shape[0 if transposed else 1]
    many = len(lefts)
    full = piece * count
    tile = min(256, tokens)
    dot = dot_nt if transposed else dot_nn

    def body(place_ref, *refs):
        y_refs = refs[:many]
        w_refs = [refs[many + g * count : many + (g + 1) * count] for g in range(many)]
        keep_ref, send_ref, all_ref = refs[many + many * count :]
        for j in range(count):
            total = dot(y_refs[0][...], w_refs[0][j][...])
            for g in range(1, many):
                total = total + dot(y_refs[g][...], w_refs[g][j][...])
            all_ref[:, piece_at(place_ref, j, piece)] = total.astype(jnp.bfloat16)
        keep_ref[...] = all_ref[:, : full // 2]
        send_ref[...] = all_ref[:, full // 2 :]

    outs = (shape_of((tokens, full // 2), jnp.bfloat16),) * 2
    operands = (*lefts, *(w for group in groups for w in group))
    specs = [rows_spec(y, tile) for y in lefts] + [whole_spec(w) for w in operands[many:]]
    out_specs = tuple(rows_spec(o, tile) for o in outs)
    inner = sum(y.shape[1] for y in lefts)
    return kernel_call(
        body, place, operands, specs, outs, out_specs, (tokens // tile,), [pltpu.VMEM((tile, full), jnp.bfloat16)],
        2 * tokens * full * inner, 48
    )


def gather_transposed(place, blocks, groups):
    tokens, width = blocks[0].shape
    many, count = len(blocks), len(groups[0])
    piece = groups[0][0].shape[1]
    full = width * many
    widths = [group[0].shape[0] for group in groups]
    tile = min(256, tokens)

    def body(place_ref, *refs):
        x_refs = refs[:many]
        w_refs = [refs[many + g * count : many + (g + 1) * count] for g in range(len(groups))]
        wide_ref, out_ref, all_ref = refs[many + len(groups) * count :]
        for i in range(many):
            all_ref[:, i * width : (i + 1) * width] = x_refs[i][...]
        for j in range(count):
            wide_ref[:, j * piece : (j + 1) * piece] = all_ref[:, piece_at(place_ref, j, piece)]
        start = 0
        for g, span in enumerate(widths):
            total = dot_nt(wide_ref[:, :piece], w_refs[g][0][...])
            for j in range(1, count):
                total = total + dot_nt(wide_ref[:, j * piece : (j + 1) * piece], w_refs[g][j][...])
            out_ref[:, start : start + span] = total.astype(jnp.bfloat16)
            start += span

    outs = (shape_of((tokens, full), jnp.bfloat16), shape_of((tokens, sum(widths)), jnp.bfloat16))
    operands = (*blocks, *(w for group in groups for w in group))
    specs = [rows_spec(b, tile) for b in blocks] + [whole_spec(w) for w in operands[many:]]
    out_specs = tuple(rows_spec(o, tile) for o in outs)
    scratch = [pltpu.VMEM((tile, full), jnp.bfloat16)]
    return kernel_call(
        body, place, operands, specs, outs, out_specs, (tokens // tile,), scratch, 2 * tokens * full * sum(widths), 48
    )


def gather_swish_back(place, blocks, groups, gate, up):
    tokens, width = blocks[0].shape
    many, count = len(blocks), len(groups[0])
    piece = groups[0][0].shape[1]
    full = width * many
    widths = [group[0].shape[0] for group in groups]
    tile = min(256, tokens)

    def body(place_ref, *refs):
        x_refs, gate_ref, up_ref = refs[:many], refs[many], refs[many + 1]
        first = many + 2
        w_refs = [refs[first + g * count : first + (g + 1) * count] for g in range(len(groups))]
        wide_ref, gate_out, up_out, all_ref = refs[first + len(groups) * count :]
        for i in range(many):
            all_ref[:, i * width : (i + 1) * width] = x_refs[i][...]
        for j in range(count):
            wide_ref[:, j * piece : (j + 1) * piece] = all_ref[:, piece_at(place_ref, j, piece)]
        start = 0
        for g, span in enumerate(widths):
            total = dot_nt(wide_ref[:, :piece], w_refs[g][0][...])
            for j in range(1, count):
                total = total + dot_nt(wide_ref[:, j * piece : (j + 1) * piece], w_refs[g][j][...])
            at = slice(start, start + span)
            gate_value, up_value = gate_ref[:, at], up_ref[:, at]
            sigma = 1.0 / (1.0 + jnp.exp(-gate_value))
            gate_out[:, at] = (total * up_value * sigma * (1.0 + gate_value * (1.0 - sigma))).astype(jnp.bfloat16)
            up_out[:, at] = (total * gate_value * sigma).astype(jnp.bfloat16)
            start += span

    outs = (shape_of((tokens, full), jnp.bfloat16),) + (shape_of((tokens, sum(widths)), jnp.bfloat16),) * 2
    operands = (*blocks, gate, up, *(w for group in groups for w in group))
    specs = [rows_spec(b, tile) for b in (*blocks, gate, up)] + [whole_spec(w) for w in operands[many + 2 :]]
    out_specs = tuple(rows_spec(o, tile) for o in outs)
    scratch = [pltpu.VMEM((tile, full), jnp.bfloat16)]
    return kernel_call(
        body, place, operands, specs, outs, out_specs, (tokens // tile,), scratch, 2 * tokens * full * sum(widths), 48
    )


def turn(values, cos_wide, sin_wide):
    return values * cos_wide + pltpu.roll(values, values.shape[1] // 2, 1) * sin_wide


def band(rows, cols, first_row, first_col, position):
    distance = (
        lax.broadcasted_iota(jnp.int32, (rows, cols), 0)
        + (first_row - first_col)
        - lax.broadcasted_iota(jnp.int32, (rows, cols), 1)
    )
    return (distance >= 0) & (distance <= position)


def attention_blocks(tokens, most):
    rows = min(256, tokens)
    reach = -(-(most - 1) // rows)
    return rows, [(i * rows, max(0, i - reach) * rows, (i + 1) * rows) for i in range(tokens // rows)]


def attend(raw, position, cos_wide, sin_wide, query_norm, key_norm, q_width, k_width, most, eps):
    tokens = raw.shape[0]
    size = query_norm.shape[1]
    kv_heads, per_group = k_width // size, q_width // k_width
    factor = 1.0 / math.sqrt(size)
    rows, plan = attention_blocks(tokens, most)

    def body(_, q_ref, k_ref, v_ref, pos_ref, cos_ref, sin_ref, qn_ref, kn_ref, qt_ref, kt_ref, vb_ref, mix_ref):
        def turned(value, gain):
            scale = lax.rsqrt(jnp.mean(value * value, 1, keepdims=True) + eps)
            return turn(value * scale * gain, cos_ref[...], sin_ref[...]).astype(jnp.bfloat16)

        kt_ref[...] = turned(k_ref[...], kn_ref[...])
        vb_ref[...] = v_ref[...].astype(jnp.bfloat16)
        for g in range(per_group):
            at = slice(g * size, (g + 1) * size)
            qt_ref[:, at] = turned(q_ref[:, at], qn_ref[...])
        for first, low, high in plan:
            span = slice(first, first + rows)
            allowed = band(rows, high - low, first, low, pos_ref[span, :])
            for g in range(per_group):
                at = slice(g * size, (g + 1) * size)
                scores = dot_nt(qt_ref[span, at], kt_ref[low:high, :]) * factor
                scores = jnp.where(allowed, scores, NEGATIVE)
                weights = jnp.exp(scores - jnp.max(scores, 1, keepdims=True))
                weights = (weights * (1.0 / jnp.sum(weights, 1, keepdims=True))).astype(jnp.bfloat16)
                mix_ref[span, at] = dot_nn(weights, vb_ref[low:high, :]).astype(jnp.bfloat16)

    group = per_group * size
    outs = tuple(shape_of((tokens, w), jnp.bfloat16) for w in (q_width, k_width, k_width, q_width))
    q_spec = pl.BlockSpec((tokens, group), lambda i, *_: (0, i))
    k_spec = pl.BlockSpec((tokens, size), lambda i, *_: (0, q_width // size + i))
    v_spec = pl.BlockSpec((tokens, size), lambda i, *_: (0, (q_width + k_width) // size + i))
    one = pl.BlockSpec((tokens, size), lambda i, *_: (0, i))
    operands = (raw, raw, raw, position, cos_wide, sin_wide, query_norm, key_norm)
    specs = [q_spec, k_spec, v_spec] + [whole_spec(a) for a in operands[3:]]
    flops = 4 * tokens * (high_sum(plan) * rows // tokens) * q_width
    return kernel_call(
        body, jnp.zeros((1,), jnp.int32), operands, specs, outs, (q_spec, one, one, q_spec), (kv_heads,), [], flops, 48
    )


def high_sum(plan):
    return sum(high - low for _, low, high in plan)


def attend_back(raw, turned_q, turned_k, values, grad_mixed, position, cos_wide, sin_wide, query_norm, key_norm, most, eps):
    tokens, q_width = turned_q.shape
    k_width = turned_k.shape[1]
    size = query_norm.shape[1]
    kv_heads, per_group = k_width // size, q_width // k_width
    factor = 1.0 / math.sqrt(size)
    rows, plan = attention_blocks(tokens, most)

    def body(_, q_ref, k_ref, qt_ref, kt_ref, v_ref, dm_ref, pos_ref, cos_ref, sin_ref, qn_ref, kn_ref,
             dq_ref, dk_ref, dv_ref, gain_ref, key_sum, value_sum):
        key_sum[...] = jnp.zeros_like(key_sum)
        value_sum[...] = jnp.zeros_like(value_sum)

        def back(raw_rows, gain, upstream, span):
            scale = lax.rsqrt(jnp.mean(raw_rows * raw_rows, 1, keepdims=True) + eps)
            turned_back = turn(upstream, cos_ref[span, :], -sin_ref[span, :])
            inner = jnp.mean(turned_back * gain * raw_rows, 1, keepdims=True)
            grad = scale * gain * turned_back - raw_rows * (scale * scale * scale * inner)
            return grad.astype(jnp.bfloat16), jnp.sum(turned_back * raw_rows * scale, 0, keepdims=True)

        query_gain = jnp.zeros((1, size), jnp.float32)
        for first, low, high in plan:
            span = slice(first, first + rows)
            allowed = band(rows, high - low, first, low, pos_ref[span, :])
            for g in range(per_group):
                at = slice(g * size, (g + 1) * size)
                queries, upstream = qt_ref[span, at], dm_ref[span, at]
                scores = dot_nt(queries, kt_ref[low:high, :]) * factor
                scores = jnp.where(allowed, scores, NEGATIVE)
                probs = jnp.exp(scores - jnp.max(scores, 1, keepdims=True))
                probs = probs * (1.0 / jnp.sum(probs, 1, keepdims=True))
                grads = dot_nt(upstream, v_ref[low:high, :])
                weighted = probs * grads
                total = jnp.sum(weighted, 1, keepdims=True)
                grads = (weighted - probs * total).astype(jnp.bfloat16)
                value_sum[low:high, :] += dot_tn(probs.astype(jnp.bfloat16), upstream)
                key_sum[low:high, :] += dot_tn(grads, queries)
                grad_turned = dot_nn(grads, kt_ref[low:high, :]) * factor
                grad, gain = back(q_ref[span, at], qn_ref[...], grad_turned, span)
                dq_ref[span, at] = grad
                query_gain = query_gain + gain
        grad, key_gain = back(k_ref[...], kn_ref[...], key_sum[...] * factor, slice(0, tokens))
        dk_ref[...] = grad
        dv_ref[...] = value_sum[...].astype(jnp.bfloat16)
        gain_ref[...] = jnp.concatenate([query_gain, key_gain, jnp.zeros((6, size), jnp.float32)], 0)

    group = per_group * size
    outs = (
        shape_of((tokens, q_width), jnp.bfloat16),
        shape_of((tokens, k_width), jnp.bfloat16),
        shape_of((tokens, k_width), jnp.bfloat16),
        shape_of((8 * kv_heads, size), jnp.float32),
    )
    q_spec = pl.BlockSpec((tokens, group), lambda i, *_: (0, i))
    k_spec = pl.BlockSpec((tokens, size), lambda i, *_: (0, q_width // size + i))
    one = pl.BlockSpec((tokens, size), lambda i, *_: (0, i))
    operands = (raw, raw, turned_q, turned_k, values, grad_mixed, position, cos_wide, sin_wide, query_norm, key_norm)
    specs = [q_spec, k_spec, q_spec, one, one, q_spec] + [whole_spec(a) for a in operands[6:]]
    out_specs = (q_spec, one, one, pl.BlockSpec((8, size), lambda i, *_: (i, 0)))
    scratch = [pltpu.VMEM((tokens, size), jnp.float32)] * 2
    flops = 10 * tokens * (high_sum(plan) * rows // tokens) * q_width
    return kernel_call(
        body, jnp.zeros((1,), jnp.int32), operands, specs, outs, out_specs, (kv_heads,), scratch, flops, 48
    )


def local(
    hidden_in,
    seq_lengths,
    attn_norm,
    w_query,
    key_weight,
    value_weight,
    query_norm,
    key_norm,
    w_output,
    ffwd_norm,
    w_gate,
    w_up,
    w_down,
    cotangent,
):
    low = jnp.bfloat16
    tokens, part_width = hidden_in.shape
    full_width = part_width * lax.axis_size("col")
    head_size = query_norm.shape[0]
    q_width, k_width = w_query.shape[1], key_weight.shape[1]
    ring = Ring()
    place = ring.place
    steps = ring.half

    hidden_blocks = spread(hidden_in)
    gains = jnp.concatenate(spread(attn_norm[None, :]), 1)
    qkv_ring = Gather(ring, jnp.concatenate([w_query, key_weight, value_weight], 1), 0)
    out_ring = Gather(ring, w_output, 1)
    gate_ring, up_ring = Gather(ring, w_gate, 0), Gather(ring, w_up, 0)
    ff_half = w_down.shape[0] // 2
    down_rings = Gather(ring, w_down[:ff_half], 1), Gather(ring, w_down[ff_half:], 1)
    queue = [(g, s) for pair in ((qkv_ring, out_ring), (gate_ring, up_ring), down_rings) for s in range(steps) for g in pair]
    for spot, (gather, step) in enumerate(queue):
        gather.step(step, *(queue[spot - 2][0].last if spot >= 2 and step == 0 else ()))
    qkv_all, output_all = qkv_ring.blocks(), out_ring.blocks()
    gate_all, up_all = gate_ring.blocks(), up_ring.blocks()
    down_all = [g.blocks() for g in down_rings]

    position = tables(seq_lengths[0], tokens)
    cos_wide, sin_wide = rotary(position, head_size)
    turning = (position[:, None], cos_wide, sin_wide, query_norm[None, :], key_norm[None, :])
    residual = hidden_in.astype(jnp.float32)
    wide_one, factor_one, qkv_raw = gather_norm_matmul(place, hidden_blocks, gains, qkv_all, EPS)
    turned_q, turned_k, values, mixed = attend(qkv_raw, *turning, q_width, k_width, MOST, EPS)
    middle = residual + collect(*spread_product(place, [mixed], [output_all], False))
    factor_two = lax.rsqrt(sum_over(jnp.sum(middle * middle, 1), "col") / full_width + EPS)[:, None]
    normed_two = (middle * factor_two * ffwd_norm).astype(low)
    wide_two, gate, up, hidden = gather_swish(place, spread(normed_two), gate_all, up_all)
    hidden_parts = [hidden[:, :ff_half], hidden[:, ff_half:]]
    hidden_out = (middle + collect(*spread_product(place, hidden_parts, down_all, False))).astype(low)

    upstream, gate_low, up_low = gather_swish_back(place, spread(cotangent), down_all, gate, up)
    grad_normed = collect(*spread_product(place, [gate_low, up_low], [gate_all, up_all], True))
    weighted = grad_normed * ffwd_norm
    inner = sum_over(jnp.sum(weighted * middle, 1), "col")[:, None] / full_width
    grad_middle = cotangent.astype(jnp.float32) + factor_two * weighted - middle * (factor_two**3 * inner)
    ffwd_gain = jnp.sum(grad_normed * middle * factor_two, 0)
    middle_wide, grad_mixed = gather_transposed(place, spread(grad_middle.astype(low)), [output_all])
    query_low, key_low, value_low, head_gains = attend_back(
        qkv_raw, turned_q, turned_k, values, grad_mixed, *turning, MOST, EPS
    )
    qkv_low = jnp.concatenate([query_low, key_low, value_low], 1)
    grad_first = collect(*spread_product(place, [qkv_low], [qkv_all], True))
    weighted = grad_first * attn_norm
    inner = sum_over(jnp.sum(weighted * residual, 1), "col")[:, None] / full_width
    hidden_grad = grad_middle + factor_one * weighted - residual * (factor_one**3 * inner)
    attn_gain = jnp.sum(grad_first * residual * factor_one, 0)

    def columns(wide, j):
        piece = wide.shape[1] // ring.count
        return wide[:, j * piece : (j + 1) * piece]

    down_sums = tuple(
        Scatter(ring, lambda j, h=h: dot_tn(h, columns(upstream, j)), 1) for h in hidden_parts
    )
    gate_sum = Scatter(ring, lambda j: dot_tn(columns(wide_two, j), gate_low), 0)
    up_sum = Scatter(ring, lambda j: dot_tn(columns(wide_two, j), up_low), 0)
    out_sum = Scatter(ring, lambda j: dot_tn(mixed, columns(middle_wide, j)), 1)
    qkv_sum = Scatter(ring, lambda j: dot_tn(columns(wide_one, j), qkv_low), 0)
    queue = [(g, s) for pair in (down_sums, (gate_sum, up_sum), (out_sum, qkv_sum)) for s in range(steps) for g in pair]
    for spot, (scatter, step) in enumerate(queue):
        scatter.step(step, *(queue[spot - 2][0].last if spot >= 2 and step == 0 else ()))
    grad_qkv = qkv_sum.total()

    head_gains = jnp.sum(head_gains.reshape(-1, 8, head_size), 0)[:2].reshape(-1)
    gain_sums = sum_over(jnp.concatenate([ffwd_gain, sum_over(head_gains, "col")]), "row")
    return (
        hidden_out,
        hidden_grad,
        sum_over(attn_gain, "row"),
        grad_qkv[:, :q_width],
        grad_qkv[:, q_width : q_width + k_width],
        grad_qkv[:, q_width + k_width :],
        gain_sums[part_width : part_width + head_size],
        gain_sums[part_width + head_size :],
        out_sum.total(),
        gain_sums[:part_width],
        gate_sum.total(),
        up_sum.total(),
        jnp.concatenate([s.total() for s in down_sums], 0),
    )


def solution(mesh):
    in_specs = (
        P("row", "col"),
        P("row", None),
        P("col"),
        P("row", "col"),
        P("row", "col"),
        P("row", "col"),
        P(),
        P(),
        P("col", "row"),
        P("col"),
        P("row", "col"),
        P("row", "col"),
        P("col", "row"),
        P("row", "col"),
    )
    out_specs = (
        P("row", "col"),
        P("row", "col"),
        P("col"),
        P("row", "col"),
        P("row", "col"),
        P("row", "col"),
        P(),
        P(),
        P("col", "row"),
        P("col"),
        P("row", "col"),
        P("row", "col"),
        P("col", "row"),
    )
    return jax.shard_map(local, mesh=mesh, in_specs=in_specs, out_specs=out_specs, check_vma=False)
```

time: 884 us -> 734 us (0.83)
  matrix products: 207 us -> 50.1 us
  Pallas kernels: 0 us -> 133 us
  blocking collectives: 93.5 us -> 0 us
  waiting for transfers between devices: 242 us -> 331 us
  local copies, waits for them, and re-layouts: 129 us -> 47.6 us
  other arithmetic: 68.9 us -> 29.3 us
  starting transfers between devices: 112 us -> 134 us
  between operations: 14.4 us -> 2.92 us
    dot_general x72 -> x48, matrix products: 207 us -> 50.1 us  [dot_tn(): lax.dot_general(left_side, right_side, (((0,), (0,)), ((), ())), preferre...]
    pallas_call x0 -> x10, Pallas kernels: none -> 133 us  [kernel_call(): pl.pallas_call(body, grid_spec=pltpu.PrefetchScalarGridSpec(num_scalar_pr...]
    psum x5 -> x0, blocking collectives: 93.5 us -> none  [the longest x1 52.3 us: local(): lax.psum((first_wide, second_wide, query_gain_grad, key_gain_grad), ('row...]
    ppermute x48, waiting for transfers between devices: 137 us -> 210 us  [send_on(): return lax.ppermute(value, 'row', self.onward)]
    unnamed x320 -> x264, local copies, waits for them, and re-layouts: 63.5 us -> 25.5 us
    ppermute x20 -> x37, starting transfers between devices: 7.93 us -> 29.9 us  [swap(): lax.ppermute(value, axis, [(i, i ^ bit) for i in range(lax.axis_size(axis...]
    dynamic_slice x18 -> x0, local copies, waits for them, and re-layouts: 13.9 us -> none  [the longest x4 7.95 us: block(): lax.dynamic_slice_in_dim(partial_value, ring.distance[first + i] * piece,...]
    convert_element_type x12 -> x2, other arithmetic: 16.2 us -> 3.54 us  [the longest x1 2.32 us: local(): grad_middle.astype(low)]
  transfers between devices with their start and end apart: 116 -> 133, of which waited for: 49 -> 59; matrix products, arithmetic and copies ran while one was open for 32% -> 11% of each run, Pallas kernels for 0% -> 11%
where the time goes in v2:
time: 734 us; the launch traced here: 729 us
  waiting for transfers between devices  331 us (45%)
  starting transfers between devices  134 us (18%)
  Pallas kernels  133 us (18%)
  matrix products  50.1 us (7%)
  local copies, waits for them, and re-layouts  47.6 us (6%)
  other arithmetic  29.3 us (4%)
    ppermute x48, waiting for transfers between devices, send_on(): return lax.ppermute(value, 'row', self.onward)  210 us
    pallas_call x10, Pallas kernels, kernel_call(): pl.pallas_call(body, grid_spec=pltpu.PrefetchScalarGridSpec(num_scalar_pr...  133 us
    ppermute x48, waiting for transfers between devices, send_back(): return lax.ppermute(value, 'row', self.backward)  82.3 us
    ppermute x48, starting transfers between devices, send_on(): return lax.ppermute(value, 'row', self.onward)  79.2 us
    dot_general x48, matrix products, dot_tn(): lax.dot_general(left_side, right_side, (((0,), (0,)), ((), ())), preferre...  50.1 us
    ppermute x37, waiting for transfers between devices, swap(): lax.ppermute(value, axis, [(i, i ^ bit) for i in range(lax.axis_size(axis...  38.6 us
    ppermute x37, starting transfers between devices, swap(): lax.ppermute(value, axis, [(i, i ^ bit) for i in range(lax.axis_size(axis...  29.9 us
    unnamed x264, local copies, waits for them, and re-layouts  25.5 us
  transfers between devices with their start and end apart: 133, of which 59 were waited for; matrix products, arithmetic and copies ran while one was open for 11% of the time, Pallas kernels for 11%

profile of v2, /device:TPU:0, one launch (start us, length us, event | category | flops | bytes accessed | tf_op | source)
XLA Modules:
  0.0 729.0 jit_solution(17613890949389249889)
XLA Ops:
  12.9 6.4 collective-permute-done.6.refs_6_.refs_2_
  27.0 12.0 %collective-permute-done.18.refs_8_.refs_11_ = bf16[512,256]{1,0:T(8,128)(2,1)S(1)} collective-permute-done((bf16[512,256]{1,0:T(8,128)(2,1)}, bf16[512,256]{1,0:T(8,128)(2,1)S(1)}, u32[]{:S(2)}, u32[]{:S(2)}) %collective-permute-start.18) | collective-permute-done | bytes 262176 | tf_op jit(solution)/shard_map/ppermute | solution.py:61
  52.0 10.5 %collective-permute-done.20.refs_6_.refs_9_ = bf16[512,256]{1,0:T(8,128)(2,1)} collective-permute-done((bf16[512,256]{1,0:T(8,128)(2,1)}, bf16[512,256]{1,0:T(8,128)(2,1)}, u32[]{:S(2)}, u32[]{:S(2)}) %collective-permute-start.20) | collective-permute-done | bytes 262176 | tf_op jit(solution)/shard_map/ppermute | solution.py:61
  81.0 11.3 %shard_map.246 = (bf16[1024,2048]{1,0:T(8,128)(2,1)}, f32[1024,1]{1,0:T(8,128)S(1)}, f32[1024,1024]{1,0:T(8,128)}) custom-call(s32[8]{0:T(128)S(1)} %dynamic-slice_bitcast_fusion.place_ref, bf16[1024,512]{1,0:T(8,128)(2,1)S(1)} %copy-done, bf16[1024,512]{1,0:T(8,128)(2,1)} %collective-permute-done.refs_1_, bf16[1024,512]{1,0:T(8,128)(2,1)} %copy-done.108, ...), custom_call_target="tpu_custom_call" | custom-call | flops 4294967296 | bytes 16789504 | tf_op jit(solution)/shard_map/pallas_call | solution.py:186
  92.3 13.9 %shard_map.247 = (bf16[1024,512]{1,0:T(8,128)(2,1)S(1)}, bf16[1024,256]{1,0:T(8,128)(2,1)S(1)}, bf16[1024,256]{1,0:T(8,128)(2,1)S(1)}, bf16[1024,512]{1,0:T(8,128)(2,1)S(1)}) custom-call(s32[1]{0:T(128)} %constant.44.clone.1._, f32[1024,1024]{1,0:T(8,128)} %get-tuple-element.53.q_ref.k_ref.v_ref, f32[1024,1024]{1,0:T(8,128)} %get-tuple-element.53.q_ref.k_ref.v_ref, ...), custom_call_target="tpu_custom_call" | custom-call | flops 1207959552 | bytes 16782336 | tf_op jit(solution)/shard_map/pallas_call | solution.py:186
  119.1 16.3 %collective-permute-done.37.refs_13_.refs_11_ = bf16[256,1536]{1,0:T(8,128)(2,1)S(1)} collective-permute-done((bf16[256,1536]{1,0:T(8,128)(2,1)S(1)}, bf16[256,1536]{1,0:T(8,128)(2,1)S(1)}, u32[]{:S(2)}, u32[]{:S(2)}) %collective-permute-start.37) | collective-permute-done | bytes 786464 | tf_op jit(solution)/shard_map/ppermute | solution.py:58
  140.1 12.1 %collective-permute-done.29.refs_5_.refs_3_ = bf16[256,1536]{1,0:T(8,128)(2,1)S(1)} collective-permute-done((bf16[256,1536]{1,0:T(8,128)(2,1)S(1)}, bf16[256,1536]{1,0:T(8,128)(2,1)S(1)}, u32[]{:S(2)}, u32[]{:S(2)}) %collective-permute-start.29) | collective-permute-done | bytes 786464 | tf_op jit(solution)/shard_map/ppermute | solution.py:58
  154.3 14.8 %collective-permute-done.38.refs_14_.refs_12_ = bf16[256,1536]{1,0:T(8,128)(2,1)S(1)} collective-permute-done((bf16[256,1536]{1,0:T(8,128)(2,1)S(1)}, bf16[256,1536]{1,0:T(8,128)(2,1)S(1)}, u32[]{:S(2)}, u32[]{:S(2)}) %collective-permute-start.38) | collective-permute-done | bytes 786464 | tf_op jit(solution)/shard_map/ppermute | solution.py:58
  171.2 14.8 %collective-permute-done.30.refs_6_.refs_4_ = bf16[256,1536]{1,0:T(8,128)(2,1)S(1)} collective-permute-done((bf16[256,1536]{1,0:T(8,128)(2,1)S(1)}, bf16[256,1536]{1,0:T(8,128)(2,1)S(1)}, u32[]{:S(2)}, u32[]{:S(2)}) %collective-permute-start.30) | collective-permute-done | bytes 786464 | tf_op jit(solution)/shard_map/ppermute | solution.py:58
  188.0 14.8 %collective-permute-done.39.refs_15_.refs_13_ = bf16[256,1536]{1,0:T(8,128)(2,1)S(1)} collective-permute-done((bf16[256,1536]{1,0:T(8,128)(2,1)S(1)}, bf16[256,1536]{1,0:T(8,128)(2,1)S(1)}, u32[]{:S(2)}, u32[]{:S(2)}) %collective-permute-start.39) | collective-permute-done | bytes 786464 | tf_op jit(solution)/shard_map/ppermute | solution.py:58
  209.6 18.1 %collective-permute-done.40 = bf16[128,1536]{1,0:T(8,128)(2,1)S(1)} collective-permute-done((bf16[128,1536]{1,0:T(8,128)(2,1)S(1)}, bf16[128,1536]{1,0:T(8,128)(2,1)S(1)}, u32[]{:S(2)}, u32[]{:S(2)}) %collective-permute-start.40) | collective-permute-done | bytes 393248 | tf_op jit(solution)/shard_map/ppermute | solution.py:58
  311.1 21.5 %shard_map.249 = (bf16[1024,2048]{1,0:T(8,128)(2,1)}, f32[1024,1536]{1,0:T(8,128)}, f32[1024,1536]{1,0:T(8,128)}, bf16[1024,1536]{1,0:T(8,128)(2,1)}) custom-call(s32[8]{0:T(128)S(1)} %dynamic-slice_bitcast_fusion.place_ref, bf16[1024,512]{1,0:T(8,128)(2,1)} %multiply_convert_fusion.refs_0_, bf16[1024,512]{1,0:T(8,128)(2,1)} %collective-permute-done.26.refs_1_, ...), custom_call_target="tpu_custom_call" | custom-call | flops 12884901888 | bytes 36700160 | tf_op jit(solution)/shard_map/pallas_call | solution.py:186
  332.6 15.2 %shard_map.251 = (bf16[1024,2048]{1,0:T(8,128)(2,1)}, bf16[1024,1536]{1,0:T(8,128)(2,1)}, bf16[1024,1536]{1,0:T(8,128)(2,1)}) custom-call(s32[8]{0:T(128)S(1)} %dynamic-slice_bitcast_fusion.place_ref, bf16[1024,512]{1,0:T(8,128)(2,1)} %refs_0_.3, bf16[1024,512]{1,0:T(8,128)(2,1)} %copy-done.107, bf16[1024,512]{1,0:T(8,128)(2,1)} %collective-permute-done.64.refs_2_, ...), custom_call_target="tpu_custom_call" | custom-call | flops 6442450944 | bytes 33554432 | tf_op jit(solution)/shard_map/pallas_call | solution.py:186
  378.9 11.6 %shard_map.250 = (bf16[1024,1024]{1,0:T(8,128)(2,1)}, bf16[1024,1024]{1,0:T(8,128)(2,1)}) custom-call(s32[8]{0:T(128)S(1)} %dynamic-slice_bitcast_fusion.place_ref, bf16[1024,768]{1,0:T(8,128)(2,1)} %get-tuple-element.102.refs_0_, bf16[1024,768]{1,0:T(8,128)(2,1)} %get-tuple-element.101.refs_1_, bf16[768,256]{1,0:T(8,128)(2,1)} %get-tuple-element.60.refs_2_.refs_6_, ...), custom_call_target="tpu_custom_call" | custom-call | flops 6442450944 | bytes 13631488 | tf_op jit(solution)/shard_map/pallas_call | solution.py:186
  408.1 7.3 %collective-permute-done.85 = bf16[768,256]{1,0:T(8,128)(2,1)S(1)} collective-permute-done((bf16[768,256]{1,0:T(8,128)(2,1)S(1)}, bf16[768,256]{1,0:T(8,128)(2,1)S(1)}, u32[]{:S(2)}, u32[]{:S(2)}) %collective-permute-start.85) | collective-permute-done | bytes 393248 | tf_op jit(solution)/shard_map/ppermute | solution.py:61
  420.5 11.2 %collective-permute-done.86 = bf16[768,256]{1,0:T(8,128)(2,1)S(1)} collective-permute-done((bf16[768,256]{1,0:T(8,128)(2,1)S(1)}, bf16[768,256]{1,0:T(8,128)(2,1)S(1)}, u32[]{:S(2)}, u32[]{:S(2)}) %collective-permute-start.86) | collective-permute-done | bytes 393248 | tf_op jit(solution)/shard_map/ppermute | solution.py:61
  446.7 19.4 %shard_map.252 = (bf16[1024,1024]{1,0:T(8,128)(2,1)}, bf16[1024,1024]{1,0:T(8,128)(2,1)}) custom-call(s32[8]{0:T(128)S(1)} %dynamic-slice_bitcast_fusion.place_ref, bf16[1024,1536]{1,0:T(8,128)(2,1)} %get-tuple-element.66.refs_0_, bf16[1024,1536]{1,0:T(8,128)(2,1)} %get-tuple-element.67.refs_1_, bf16[256,1536]{1,0:T(8,128)(2,1)S(1)} %copy-done.29, ...), custom_call_target="tpu_custom_call" | custom-call | flops 12884901888 | bytes 23068672 | tf_op jit(solution)/shard_map/pallas_call | solution.py:186
  506.1 10.5 %collective-permute-done.67 = bf16[1024,512]{1,0:T(8,128)(2,1)S(1)} collective-permute-done((bf16[1024,512]{1,0:T(8,128)(2,1)S(1)}, bf16[1024,512]{1,0:T(8,128)(2,1)S(1)}, u32[]{:S(2)}, u32[]{:S(2)}) %collective-permute-start.67) | collective-permute-done | bytes 1048608 | tf_op jit(solution)/shard_map/ppermute | solution.py:140
  523.5 13.3 %collective-permute-done.69 = f32[1024]{0:T(1024)S(1)} collective-permute-done((f32[1024]{0:T(1024)S(1)}, f32[1024]{0:T(1024)S(1)}, u32[]{:S(2)}, u32[]{:S(2)}) %collective-permute-start.69) | collective-permute-done | bytes 4128 | tf_op jit(solution)/shard_map/ppermute | solution.py:140
  592.1 6.2 shard_map.253
  604.8 19.5 %shard_map.254 = (bf16[1024,512]{1,0:T(8,128)(2,1)S(1)}, bf16[1024,256]{1,0:T(8,128)(2,1)S(1)}, bf16[1024,256]{1,0:T(8,128)(2,1)S(1)}, f32[16,128]{1,0:T(8,128)S(1)}) custom-call(s32[1]{0:T(128)} %constant.44.clone.1._, f32[1024,1024]{1,0:T(8,128)} %get-tuple-element.53.q_ref.k_ref.v_ref, f32[1024,1024]{1,0:T(8,128)} %get-tuple-element.53.q_ref.k_ref.v_ref, ...), custom_call_target="tpu_custom_call" | custom-call | flops 3019898880 | bytes 14693376 | tf_op jit(solution)/shard_map/pallas_call | solution.py:186
  632.1 8.8 %shard_map.255 = (bf16[1024,1024]{1,0:T(8,128)(2,1)}, bf16[1024,1024]{1,0:T(8,128)(2,1)}) custom-call(s32[8]{0:T(128)S(1)} %dynamic-slice_bitcast_fusion.place_ref, bf16[1024,1024]{1,0:T(8,128)(2,1)} %copy-done.52, bf16[256,1024]{1,0:T(8,128)(2,1)S(1)} %copy-done.19, bf16[256,1024]{1,0:T(8,128)(2,1)S(1)} %copy-done.38, ...), custom_call_target="tpu_custom_call" | custom-call | flops 4294967296 | bytes 10485760 | tf_op jit(solution)/shard_map/pallas_call | solution.py:186
  666.2 13.4 %collective-permute-done.127 = bf16[512,256]{1,0:T(8,128)(2,1)S(1)} collective-permute-done((bf16[512,256]{1,0:T(8,128)(2,1)S(1)}, bf16[512,256]{1,0:T(8,128)(2,1)S(1)}, u32[]{:S(2)}, u32[]{:S(2)}) %collective-permute-start.127) | collective-permute-done | bytes 262176 | tf_op jit(solution)/shard_map/ppermute | solution.py:58
  687.9 11.4 %collective-permute-done.98 = bf16[256,1024]{1,0:T(8,128)(2,1)S(1)} collective-permute-done((bf16[256,1024]{1,0:T(8,128)(2,1)S(1)}, bf16[256,1024]{1,0:T(8,128)(2,1)S(1)}, u32[]{:S(2)}, u32[]{:S(2)}) %collective-permute-start.98) | collective-permute-done | bytes 524320 | tf_op jit(solution)/shard_map/ppermute | solution.py:58
  (679 shorter events, 411.9 us)
Async XLA Ops:
  9.3 41.2 %collective-permute-start = (bf16[1024,512]{1,0:T(8,128)(2,1)}, bf16[1024,512]{1,0:T(8,128)(2,1)}, u32[]{:S(2)}, u32[]{:S(2)}) collective-permute-start(bf16[1024,512]{1,0:T(8,128)(2,1)} %refs_0_.2), channel_id=1, source_target_pairs={{0,2},{1,3},{2,0},{3,1},{4,6},{5,7},{6,4},{7,5},{8,10},{9,11},{10,... | collective-permute-start | bytes 3145736 | tf_op jit(solution)/shard_map/ppermute | solution.py:140
  117.1 35.2 %collective-permute-start.29 = (bf16[256,1536]{1,0:T(8,128)(2,1)S(1)}, bf16[256,1536]{1,0:T(8,128)(2,1)S(1)}, u32[]{:S(2)}, u32[]{:S(2)}) collective-permute-start(bf16[256,1536]{1,0:T(8,128)(2,1)S(1)} %copy-done.28), channel_id=1, source_target_pairs={{0,8},{8,16},{16,24},{24,28},{28,20},{20,12},{12,4},{4,0},{1,9},{9... | collective-permute-start | bytes 2359304 | tf_op jit(solution)/shard_map/ppermute | solution.py:58
  118.7 35.2 %collective-permute-start.33 = (bf16[256,1536]{1,0:T(8,128)(2,1)S(1)}, bf16[256,1536]{1,0:T(8,128)(2,1)S(1)}, u32[]{:S(2)}, u32[]{:S(2)}) collective-permute-start(bf16[256,1536]{1,0:T(8,128)(2,1)S(1)} %copy-done.28), channel_id=1, source_target_pairs={{8,0},{16,8},{24,16},{28,24},{20,28},{12,20},{4,12},{0,4},{9,1},{1... | collective-permute-start | bytes 2359304 | tf_op jit(solution)/shard_map/ppermute | solution.py:61
  135.4 33.7 %collective-permute-start.38 = (bf16[256,1536]{1,0:T(8,128)(2,1)S(1)}, bf16[256,1536]{1,0:T(8,128)(2,1)S(1)}, u32[]{:S(2)}, u32[]{:S(2)}) collective-permute-start(bf16[256,1536]{1,0:T(8,128)(2,1)S(1)} %collective-permute-done.37.refs_13_.refs_11_), channel_id=1, source_target_pairs={{0,8},{8,16},{16,24},{24,28},{28,20},{20,12},{12,4},{4,0},{1,9},{9... | collective-permute-start | bytes 2359304 | tf_op jit(solution)/shard_map/ppermute | solution.py:58
  137.1 33.7 %collective-permute-start.42 = (bf16[256,1536]{1,0:T(8,128)(2,1)S(1)}, bf16[256,1536]{1,0:T(8,128)(2,1)S(1)}, u32[]{:S(2)}, u32[]{:S(2)}) collective-permute-start(bf16[256,1536]{1,0:T(8,128)(2,1)S(1)} %collective-permute-done.41.refs_19_.refs_17_), channel_id=1, source_target_pairs={{8,0},{16,8},{24,16},{28,24},{20,28},{12,20},{4,12},{0,4},{9,1},{1... | collective-permute-start | bytes 2359304 | tf_op jit(solution)/shard_map/ppermute | solution.py:61
  138.6 66.9 %collective-permute-start.23 = (bf16[1024,512]{1,0:T(8,128)(2,1)S(1)}, bf16[1024,512]{1,0:T(8,128)(2,1)S(1)}, u32[]{:S(2)}, u32[]{:S(2)}) collective-permute-start(bf16[1024,512]{1,0:T(8,128)(2,1)S(1)} %slice.707), channel_id=1, source_target_pairs={{0,2},{1,3},{2,0},{3,1},{4,6},{5,7},{6,4},{7,5},{8,10},{9,11},{10,... | collective-permute-start | bytes 3145736 | tf_op jit(solution)/shard_map/ppermute | solution.py:140
  152.3 33.7 %collective-permute-start.30 = (bf16[256,1536]{1,0:T(8,128)(2,1)S(1)}, bf16[256,1536]{1,0:T(8,128)(2,1)S(1)}, u32[]{:S(2)}, u32[]{:S(2)}) collective-permute-start(bf16[256,1536]{1,0:T(8,128)(2,1)S(1)} %collective-permute-done.29.refs_5_.refs_3_), channel_id=1, source_target_pairs={{0,8},{8,16},{16,24},{24,28},{28,20},{20,12},{12,4},{4,0},{1,9},{9... | collective-permute-start | bytes 2359304 | tf_op jit(solution)/shard_map/ppermute | solution.py:58
  153.9 33.7 %collective-permute-start.34 = (bf16[256,1536]{1,0:T(8,128)(2,1)S(1)}, bf16[256,1536]{1,0:T(8,128)(2,1)S(1)}, u32[]{:S(2)}, u32[]{:S(2)}) collective-permute-start(bf16[256,1536]{1,0:T(8,128)(2,1)S(1)} %collective-permute-done.33.refs_11_.refs_9_), channel_id=1, source_target_pairs={{8,0},{16,8},{24,16},{28,24},{20,28},{12,20},{4,12},{0,4},{9,1},{1... | collective-permute-start | bytes 2359304 | tf_op jit(solution)/shard_map/ppermute | solution.py:61
  169.1 33.7 %collective-permute-start.39 = (bf16[256,1536]{1,0:T(8,128)(2,1)S(1)}, bf16[256,1536]{1,0:T(8,128)(2,1)S(1)}, u32[]{:S(2)}, u32[]{:S(2)}) collective-permute-start(bf16[256,1536]{1,0:T(8,128)(2,1)S(1)} %collective-permute-done.38.refs_14_.refs_12_), channel_id=1, source_target_pairs={{0,8},{8,16},{16,24},{24,28},{28,20},{20,12},{12,4},{4,0},{1,9},{9... | collective-permute-start | bytes 2359304 | tf_op jit(solution)/shard_map/ppermute | solution.py:58
  170.8 33.8 %collective-permute-start.43 = (bf16[256,1536]{1,0:T(8,128)(2,1)S(1)}, bf16[256,1536]{1,0:T(8,128)(2,1)S(1)}, u32[]{:S(2)}, u32[]{:S(2)}) collective-permute-start(bf16[256,1536]{1,0:T(8,128)(2,1)S(1)} %collective-permute-done.42.refs_18_.refs_16_), channel_id=1, source_target_pairs={{8,0},{16,8},{24,16},{28,24},{20,28},{12,20},{4,12},{0,4},{9,1},{1... | collective-permute-start | bytes 2359304 | tf_op jit(solution)/shard_map/ppermute | solution.py:61
  186.0 45.0 %collective-permute-start.31 = (bf16[256,1536]{1,0:T(8,128)(2,1)S(1)}, bf16[256,1536]{1,0:T(8,128)(2,1)S(1)}, u32[]{:S(2)}, u32[]{:S(2)}) collective-permute-start(bf16[256,1536]{1,0:T(8,128)(2,1)S(1)} %collective-permute-done.30.refs_6_.refs_4_), channel_id=1, source_target_pairs={{0,8},{8,16},{16,24},{24,28},{28,20},{20,12},{12,4},{4,0},{1,9},{9... | collective-permute-start | bytes 2359304 | tf_op jit(solution)/shard_map/ppermute | solution.py:58
  187.6 45.0 %collective-permute-start.35 = (bf16[256,1536]{1,0:T(8,128)(2,1)S(1)}, bf16[256,1536]{1,0:T(8,128)(2,1)S(1)}, u32[]{:S(2)}, u32[]{:S(2)}) collective-permute-start(bf16[256,1536]{1,0:T(8,128)(2,1)S(1)} %collective-permute-done.34.refs_10_.refs_8_), channel_id=1, source_target_pairs={{8,0},{16,8},{24,16},{28,24},{20,28},{12,20},{4,12},{0,4},{9,1},{1... | collective-permute-start | bytes 2359304 | tf_op jit(solution)/shard_map/ppermute | solution.py:61
  234.5 52.7 %collective-permute-start.26 = (bf16[1024,512]{1,0:T(8,128)(2,1)}, bf16[1024,512]{1,0:T(8,128)(2,1)}, u32[]{:S(2)}, u32[]{:S(2)}) collective-permute-start(bf16[1024,512]{1,0:T(8,128)(2,1)} %multiply_convert_fusion.refs_0_), channel_id=1, source_target_pairs={{0,2},{1,3},{2,0},{3,1},{4,6},{5,7},{6,4},{7,5},{8,10},{9,11},{10,... | collective-permute-start | bytes 3145736 | tf_op jit(solution)/shard_map/ppermute | solution.py:140
  393.8 96.7 %collective-permute-start.61 = (bf16[1024,1024]{1,0:T(8,128)(2,1)}, bf16[1024,1024]{1,0:T(8,128)(2,1)}, u32[]{:S(2)}, u32[]{:S(2)}) collective-permute-start(bf16[1024,1024]{1,0:T(8,128)(2,1)} %get-tuple-element.63), channel_id=1, source_target_pairs={{0,1},{1,0},{2,3},{3,2},{4,5},{5,4},{6,7},{7,6},{8,9},{9,8},{10,11... | collective-permute-start | bytes 6291464 | tf_op jit(solution)/shard_map/ppermute | solution.py:140
  438.3 30.0 %collective-permute-start.112 = (bf16[768,256]{1,0:T(8,128)(2,1)}, bf16[768,256]{1,0:T(8,128)(2,1)}, u32[]{:S(2)}, u32[]{:S(2)}) collective-permute-start(bf16[768,256]{1,0:T(8,128)(2,1)} %fusion.27), channel_id=1, source_target_pairs={{0,8},{8,16},{16,24},{24,28},{28,20},{20,12},{12,4},{4,0},{1,9},{9... | collective-permute-start | bytes 1179656 | tf_op jit(solution)/shard_map/ppermute | solution.py:58
  487.2 31.9 %collective-permute-start.122 = (bf16[256,1536]{1,0:T(8,128)(2,1)S(1)}, bf16[256,1536]{1,0:T(8,128)(2,1)S(1)}, u32[]{:S(2)}, u32[]{:S(2)}) collective-permute-start(bf16[256,1536]{1,0:T(8,128)(2,1)S(1)} %pad_maximum_fusion.4), channel_id=1, source_target_pairs={{8,0},{16,8},{24,16},{28,24},{20,28},{12,20},{4,12},{0,4},{9,1},{1... | collective-permute-start | bytes 2359304 | tf_op jit(solution)/shard_map/ppermute | solution.py:61
  488.4 32.5 %collective-permute-start.118 = (bf16[256,1536]{1,0:T(8,128)(2,1)S(1)}, bf16[256,1536]{1,0:T(8,128)(2,1)S(1)}, u32[]{:S(2)}, u32[]{:S(2)}) collective-permute-start(bf16[256,1536]{1,0:T(8,128)(2,1)S(1)} %pad_maximum_fusion.3), channel_id=1, source_target_pairs={{0,8},{8,16},{16,24},{24,28},{28,20},{20,12},{12,4},{4,0},{1,9},{9... | collective-permute-start | bytes 2359304 | tf_op jit(solution)/shard_map/ppermute | solution.py:58
  499.2 39.3 %collective-permute-start.62 = (bf16[1024,512]{1,0:T(8,128)(2,1)S(1)}, bf16[1024,512]{1,0:T(8,128)(2,1)S(1)}, u32[]{:S(2)}, u32[]{:S(2)}) collective-permute-start(bf16[1024,512]{1,0:T(8,128)(2,1)S(1)} %slice.706), channel_id=1, source_target_pairs={{0,2},{1,3},{2,0},{3,1},{4,6},{5,7},{6,4},{7,5},{8,10},{9,11},{10,... | collective-permute-start | bytes 3145736 | tf_op jit(solution)/shard_map/ppermute | solution.py:140
  504.0 38.5 %collective-permute-start.94 = (bf16[256,1536]{1,0:T(8,128)(2,1)S(1)}, bf16[256,1536]{1,0:T(8,128)(2,1)S(1)}, u32[]{:S(2)}, u32[]{:S(2)}) collective-permute-start(bf16[256,1536]{1,0:T(8,128)(2,1)S(1)} %fusion.5), channel_id=1, source_target_pairs={{8,0},{16,8},{24,16},{28,24},{20,28},{12,20},{4,12},{0,4},{9,1},{1... | collective-permute-start | bytes 2359304 | tf_op jit(solution)/shard_map/ppermute | solution.py:61
  550.8 30.9 %collective-permute-start.124 = (bf16[256,1536]{1,0:T(8,128)(2,1)S(1)}, bf16[256,1536]{1,0:T(8,128)(2,1)S(1)}, u32[]{:S(2)}, u32[]{:S(2)}) collective-permute-start(bf16[256,1536]{1,0:T(8,128)(2,1)S(1)} %fusion.8), channel_id=1, source_target_pairs={{8,0},{16,8},{24,16},{28,24},{20,28},{12,20},{4,12},{0,4},{9,1},{1... | collective-permute-start | bytes 2359304 | tf_op jit(solution)/shard_map/ppermute | solution.py:61
  602.6 51.2 %collective-permute-start.125 = (bf16[256,256]{1,0:T(8,128)(2,1)S(1)}, bf16[256,256]{1,0:T(8,128)(2,1)S(1)}, u32[]{:S(2)}, u32[]{:S(2)}) collective-permute-start(bf16[256,256]{1,0:T(8,128)(2,1)S(1)} %get-tuple-element.91), channel_id=1, source_target_pairs={{0,8},{8,16},{16,24},{24,28},{28,20},{20,12},{12,4},{4,0},{1,9},{9... | collective-permute-start | bytes 393224 | tf_op jit(solution)/shard_map/ppermute | solution.py:58
  604.4 51.3 %collective-permute-start.129 = (bf16[256,256]{1,0:T(8,128)(2,1)S(1)}, bf16[256,256]{1,0:T(8,128)(2,1)S(1)}, u32[]{:S(2)}, u32[]{:S(2)}) collective-permute-start(bf16[256,256]{1,0:T(8,128)(2,1)S(1)} %get-tuple-element.92), channel_id=1, source_target_pairs={{8,0},{16,8},{24,16},{28,24},{20,28},{12,20},{4,12},{0,4},{9,1},{1... | collective-permute-start | bytes 393224 | tf_op jit(solution)/shard_map/ppermute | solution.py:61
  652.8 31.1 %collective-permute-start.73 = (bf16[1024,1024]{1,0:T(8,128)(2,1)S(1)}, bf16[1024,1024]{1,0:T(8,128)(2,1)S(1)}, u32[]{:S(2)}, u32[]{:S(2)}) collective-permute-start(bf16[1024,1024]{1,0:T(8,128)(2,1)S(1)} %copy-done.106), channel_id=1, source_target_pairs={{0,1},{1,0},{2,3},{3,2},{4,5},{5,4},{6,7},{7,6},{8,9},{9,8},{10,11... | collective-permute-start | bytes 6291464 | tf_op jit(solution)/shard_map/ppermute | solution.py:140
  680.1 31.0 %collective-permute-start.128 = (bf16[512,256]{1,0:T(8,128)(2,1)S(1)}, bf16[512,256]{1,0:T(8,128)(2,1)S(1)}, u32[]{:S(2)}, u32[]{:S(2)}) collective-permute-start(bf16[512,256]{1,0:T(8,128)(2,1)S(1)} %fusion.32), channel_id=1, source_target_pairs={{0,8},{8,16},{16,24},{24,28},{28,20},{20,12},{12,4},{4,0},{1,9},{9... | collective-permute-start | bytes 786440 | tf_op jit(solution)/shard_map/ppermute | solution.py:58
  (236 other events, 3501.7 us)

commit v3 on v2

v3 whole, which is shorter than its diff:
```python
import math

import jax
import jax.numpy as jnp
from jax import lax
from jax.experimental import pallas as pl
from jax.experimental.pallas import tpu as pltpu
from jax.sharding import PartitionSpec as P

EPS = 1e-06
THETA = 1000000.0
NEGATIVE = -1e30
MOST = 512
COST_SCALE = 0.02


def tables(lengths_row, row_number_total):
    steps_idx = jnp.arange(row_number_total, dtype=jnp.int32)
    seq_ends = jnp.cumsum(lengths_row)
    seq_starts = seq_ends - lengths_row
    segment = jnp.sum((steps_idx[:, None] >= seq_ends[None, :]).astype(jnp.int32), 1)
    member = segment[:, None] == jnp.arange(lengths_row.shape[0], dtype=jnp.int32)[None, :]
    return steps_idx - jnp.sum(jnp.where(member, seq_starts[None, :], 0), 1)


def rotary(position, head_size):
    half_size = head_size // 2
    frequency = THETA ** (-(jnp.arange(half_size, dtype=jnp.float32) * 2.0 / head_size))
    angles = position.astype(jnp.float32)[:, None] * frequency[None, :]
    cosines, sines = jnp.cos(angles), jnp.sin(angles)
    return jnp.concatenate([cosines, cosines], 1), jnp.concatenate([-sines, sines], 1)


def ring_order(count):
    return list(range(0, count, 2)) + list(range(count - 1, 0, -2))


class Ring:
    def __init__(self):
        rows = lax.axis_size("row")
        self.count = count = min(8, rows)
        self.half = count // 2
        self.members = members = rows // count
        self.groups = [[g * members + m for m in range(members)] for g in range(count)]
        self.lanes = None if members == 1 else [[g * members + m for g in range(count)] for m in range(members)]
        order = ring_order(count)
        self.onward = self.spell([(order[i], order[(i + 1) % count]) for i in range(count)])
        self.backward = [(b, a) for a, b in self.onward]
        self.partner = self.spell([(g, g ^ 1) for g in range(count)])
        self.pairs = [[(2 * p + side) * members + m for p in range(count // 2)] for side in range(2) for m in range(members)]
        group = lax.axis_index("row") // members
        self.parity = group % 2
        self.place = self.places([[order[(order.index(g) - j) % count] for j in range(count)] for g in range(count)])
        self.behind = jnp.array([[order[(order.index(g) - j) % count] for j in range(count)] for g in range(count)])[group]
        self.plain_place = self.places([list(range(count))] * count)
        self.pair_place = self.places(
            [[j // 2 * 2 + (g % 2 ^ j % 2) for j in range(count)] for g in range(count)]
        )

    def spell(self, pairs):
        return [(a * self.members + m, b * self.members + m) for a, b in pairs for m in range(self.members)]

    def places(self, behind):
        cols = lax.axis_size("col")
        per_col = self.count // cols
        table = [
            [[COL_ORDER.index((b // per_col) ^ c) * per_col + b % per_col for b in row] for c in range(cols)]
            for row in behind
        ]
        return jnp.array(table, jnp.int32)[lax.axis_index("row") // self.members, lax.axis_index("col")]

    def send_on(self, value):
        return lax.ppermute(value, "row", self.onward)

    def send_back(self, value):
        return lax.ppermute(value, "row", self.backward)

    def to_partner(self, value):
        return lax.ppermute(value, "row", self.partner)

    def gather_stack(self, block):
        return lax.all_gather(block, "row", axis=0, axis_index_groups=self.lanes)

    def sum_stack(self, blocks):
        return lax.psum_scatter(blocks, "row", scatter_dimension=0, axis_index_groups=self.lanes)

    def inner_gather(self, block, axis):
        if self.members == 1:
            return block
        return lax.all_gather(block, "row", axis=axis, tiled=True, axis_index_groups=self.groups)

    def inner_sum(self, value, axis):
        if self.members == 1:
            return value
        value = value.astype(jnp.bfloat16)
        return lax.psum_scatter(
            value, "row", scatter_dimension=axis, tiled=True, axis_index_groups=self.groups
        ).astype(jnp.float32)


def side_of(blocks, axis, number):
    halves = [b.shape[axis] // 2 for b in blocks]
    cuts = [lax.dynamic_slice_in_dim(b, number * h, h, axis) for b, h in zip(blocks, halves, strict=True)]
    return jnp.concatenate(cuts, axis)


def pair_gather(ring, unit):
    return lax.all_gather(unit, "row", axis=0, axis_index_groups=ring.pairs)


def pair_sum(ring, units):
    return lax.psum_scatter(units, "row", scatter_dimension=0, axis_index_groups=ring.pairs)


def pair_join(ring, mine, got, axis):
    first = ring.parity == 0
    mine, got = mine.astype(jnp.float32), got.astype(jnp.float32)
    value = jnp.concatenate([jnp.where(first, mine, got), jnp.where(first, got, mine)], axis)
    return ring.inner_sum(value, 1 - axis)


class Chain:
    def __init__(self):
        self.token = lax.create_token()

    def pin(self, *values):
        self.token, *values = lax.optimization_barrier((self.token, *values))
        return values if len(values) > 1 else values[0]

    def run(self, kernel, *operands, beside=()):
        results = kernel(*self.pin(operands))
        results = tuple(results) if isinstance(results, (list, tuple)) else (results,)
        return self.pin(*results, *beside)


COL_ORDER = (0, 2, 1, 3)


def swap(value, axis, bit):
    return lax.ppermute(value, axis, [(i, i ^ bit) for i in range(lax.axis_size(axis))])


def dot_nt(left_side, right_side):
    return lax.dot_general(
        left_side, right_side, (((1,), (1,)), ((), ())), preferred_element_type=jnp.float32
    )


def dot_nn(left_side, right_side):
    return jnp.dot(left_side, right_side, preferred_element_type=jnp.float32)


def dot_tn(left_side, right_side):
    return lax.dot_general(
        left_side, right_side, (((0,), (0,)), ((), ())), preferred_element_type=jnp.float32
    )


def cost(flops):
    return pl.CostEstimate(flops=int(COST_SCALE * flops), bytes_accessed=1 << 16, transcendentals=0)


def kernel_call(body, places, operands, specs, outs, out_specs, grid, scratch, flops, mib):
    return pl.pallas_call(
        body,
        grid_spec=pltpu.PrefetchScalarGridSpec(
            num_scalar_prefetch=1,
            grid=grid,
            in_specs=specs,
            out_specs=out_specs,
            scratch_shapes=scratch,
        ),
        out_shape=outs,
        cost_estimate=cost(flops),
        compiler_params=pltpu.CompilerParams(vmem_limit_bytes=mib << 20),
    )(places, *operands)


def whole_spec(array, buffers=1):
    zeros = (0,) * len(array.shape)
    return pl.BlockSpec(array.shape, lambda *_: zeros, pipeline_mode=pl.Buffered(buffers))


def rows_spec(array, rows):
    return pl.BlockSpec((rows,) + tuple(array.shape[1:]), lambda i, *_: (i,) + (0,) * (len(array.shape) - 1))


def columns_spec(array, columns):
    return pl.BlockSpec((array.shape[0], columns), lambda i, *_: (0, i))


def shape_of(shape, dtype):
    return jax.ShapeDtypeStruct(shape, dtype)


def piece_at(place_ref, j, piece):
    return pl.ds(pl.multiple_of(place_ref[j] * piece, piece), piece)


def norm_rows(place_ref, x_refs, gain_ref, wide_ref, factor_ref, all_ref, piece, eps):
    tokens, full = wide_ref.shape
    width = x_refs[0].shape[1]
    total = jnp.zeros((tokens, 1), jnp.float32)
    for i, x_ref in enumerate(x_refs):
        value = x_ref[...]
        all_ref[:, i * width : (i + 1) * width] = value
        value = value.astype(jnp.float32)
        total = total + jnp.sum(value * value, 1, keepdims=True)
    factor = lax.rsqrt(total / full + eps)
    factor_ref[...] = factor
    for j in range(full // piece):
        at = piece_at(place_ref, j, piece)
        value = all_ref[:, at].astype(jnp.float32) * factor * gain_ref[:, at]
        wide_ref[:, j * piece : (j + 1) * piece] = value.astype(jnp.bfloat16)


def gather_norm_matmul(place, hidden_blocks, gain, weights, eps):
    tokens, width = hidden_blocks[0].shape
    full = width * len(hidden_blocks)
    count = len(weights)
    piece, columns = weights[0].shape
    tile = min(512, columns)
    many = len(hidden_blocks)

    def body(place_ref, *refs):
        x_refs, gain_ref = refs[:many], refs[many]
        w_refs = refs[many + 1 : many + 1 + count]
        wide_ref, factor_ref, out_ref, all_ref = refs[many + 1 + count :]

        @pl.when(pl.program_id(0) == 0)
        def _():
            norm_rows(place_ref, x_refs, gain_ref, wide_ref, factor_ref, all_ref, piece, eps)

        total = dot_nn(wide_ref[:, :piece], w_refs[0][...])
        for j in range(1, count):
            total = total + dot_nn(wide_ref[:, j * piece : (j + 1) * piece], w_refs[j][...])
        out_ref[...] = total

    outs = (
        shape_of((tokens, full), jnp.bfloat16),
        shape_of((tokens, 1), jnp.float32),
        shape_of((tokens, columns), jnp.float32),
    )
    operands = (*hidden_blocks, gain, *weights)
    specs = [whole_spec(b) for b in hidden_blocks] + [whole_spec(gain)] + [columns_spec(w, tile) for w in weights]
    out_specs = (whole_spec(outs[0]), whole_spec(outs[1]), columns_spec(outs[2], tile))
    scratch = [pltpu.VMEM((tokens, full), jnp.bfloat16)]
    return kernel_call(
        body, place, operands, specs, outs, out_specs, (columns // tile,), scratch, 2 * tokens * full * columns, 48
    )


def units_of(refs):
    return [refs[0].at[j] for j in range(refs[0].shape[0])] if len(refs) == 1 else refs


def gather_swish(place, blocks, gain, weights, eps):
    tokens, width = blocks[0].shape
    count, unit, both = weights.shape
    columns = both // 2
    full, many = width * len(blocks), len(blocks)
    piece = full // place.shape[0]
    tile = min(256, columns)

    def body(place_ref, *refs):
        x_refs, gain_ref, g_ref, u_ref = refs[:many], refs[many], refs[many + 1], refs[many + 2]
        wide_ref, factor_ref, gate_ref, up_ref, hidden_ref, all_ref = refs[many + 3 :]

        @pl.when(pl.program_id(0) == 0)
        def _():
            norm_rows(place_ref, x_refs, gain_ref, wide_ref, factor_ref, all_ref, piece, eps)

        def product(w_ref):
            total = dot_nn(wide_ref[:, :unit], w_ref[0])
            for j in range(1, count):
                total = total + dot_nn(wide_ref[:, j * unit : (j + 1) * unit], w_ref[j])
            return total

        gate = product(g_ref)
        gate_ref[...] = gate
        up = product(u_ref)
        up_ref[...] = up
        hidden_ref[...] = (gate / (1.0 + jnp.exp(-gate)) * up).astype(jnp.bfloat16)

    outs = (
        shape_of((tokens, full), jnp.bfloat16),
        shape_of((tokens, 1), jnp.float32),
        shape_of((tokens, columns), jnp.float32),
        shape_of((tokens, columns), jnp.float32),
        shape_of((tokens, columns), jnp.bfloat16),
    )
    operands = (*blocks, gain, weights, weights)
    steps = columns // tile
    specs = [whole_spec(b) for b in (*blocks, gain)] + [
        pl.BlockSpec((count, unit, tile), lambda i, *_: (0, 0, i)),
        pl.BlockSpec((count, unit, tile), lambda i, *_: (0, 0, i + steps)),
    ]
    out_specs = (whole_spec(outs[0]), whole_spec(outs[1])) + tuple(columns_spec(o, tile) for o in outs[2:])
    scratch = [pltpu.VMEM((tokens, full), jnp.bfloat16)]
    return kernel_call(
        body, place, operands, specs, outs, out_specs, (steps,), scratch, 4 * tokens * full * columns, 48
    )


def spread_product(place, left, weights, transposed, normed=None, by_feature=False):
    tokens, inner = left.shape
    many = len(weights)
    count = many if many > 1 else weights[0].shape[0]
    unit = weights[0].shape[-2 if transposed else -1]
    full = unit * count
    piece = full // place.shape[0]
    per_unit = unit // piece
    tile = min(256, tokens)
    dot = dot_nt if transposed else dot_nn
    extras = () if normed is None else (normed,)

    def body(place_ref, *refs):
        y_ref, w_refs = refs[0], units_of(refs[1 : 1 + many])
        rest = refs[1 + many + len(extras) :]
        keep_ref, send_ref, all_ref = rest[0], rest[1], rest[-1]
        rows = jnp.zeros((tile, 1), jnp.float32)
        if by_feature:

            @pl.when(pl.program_id(0) == 0)
            def _():
                rest[3][...] = jnp.zeros_like(rest[3])

        for j in range(count):
            total = dot(y_ref[...], w_refs[j][...])
            if extras:
                weighted = total * refs[1 + many][:, j * unit : (j + 1) * unit].astype(jnp.float32)
                rows = rows + jnp.sum(weighted, 1, keepdims=True)
                if by_feature:
                    sums = jnp.broadcast_to(jnp.sum(weighted, 0, keepdims=True), (8, unit))
                    for i in range(per_unit):
                        at = piece_at(place_ref, j * per_unit + i, piece)
                        rest[3][:, at] += sums[:, i * piece : (i + 1) * piece]
            total = total.astype(jnp.bfloat16)
            for i in range(per_unit):
                at = piece_at(place_ref, j * per_unit + i, piece)
                all_ref[:, at] = total[:, i * piece : (i + 1) * piece]
        keep_ref[...] = all_ref[:, : full // 2]
        send_ref[...] = all_ref[:, full // 2 :]
        if extras:
            rest[2][...] = rows

    outs = (shape_of((tokens, full // 2), jnp.bfloat16),) * 2
    if extras:
        outs += (shape_of((tokens, 1), jnp.float32),)
    operands = (left, *weights, *extras)
    specs = [rows_spec(left, tile)] + [whole_spec(w) for w in weights] + [rows_spec(e, tile) for e in extras]
    out_specs = tuple(rows_spec(o, tile) for o in outs)
    if by_feature:
        outs += (shape_of((8, full), jnp.float32),)
        out_specs += (whole_spec(outs[3]),)
    scratch = [pltpu.VMEM((tile, full), jnp.bfloat16)]
    return kernel_call(
        body, place, operands, specs, outs, out_specs, (tokens // tile,), scratch, 2 * tokens * full * inner, 48
    )


def assemble(place, blocks):
    tokens, width = blocks[0].shape
    many = len(blocks)
    full = width * many
    piece = full // place.shape[0]
    tile = min(256, tokens)

    def body(place_ref, *refs):
        x_refs, (wide_ref, all_ref) = refs[:many], refs[many:]
        for i in range(many):
            all_ref[:, i * width : (i + 1) * width] = x_refs[i][...]
        for j in range(full // piece):
            wide_ref[:, j * piece : (j + 1) * piece] = all_ref[:, piece_at(place_ref, j, piece)]

    outs = (shape_of((tokens, full), jnp.bfloat16),)
    specs = [rows_spec(b, tile) for b in blocks]
    scratch = [pltpu.VMEM((tile, full), jnp.bfloat16)]
    return kernel_call(
        body, place, blocks, specs, outs, (rows_spec(outs[0], tile),), (tokens // tile,), scratch, 1500 * tokens * 1024, 32
    )[0]


def times_transposed(wide, weights, order):
    return back_product(wide, weights, (), lambda total: (total,), order)


def swish_back(wide, weights, gate, up):
    def gradients(total, gate_value, up_value):
        sigma = 1.0 / (1.0 + jnp.exp(-gate_value))
        grad_gate = total * up_value * sigma * (1.0 + gate_value * (1.0 - sigma))
        return grad_gate, total * gate_value * sigma

    return back_product(wide, weights, (gate, up), gradients)


def back_product(wide, weights, extras, epilogue, order=None):
    tokens, full = wide.shape
    others, units = len(extras), len(weights)
    count = units if units > 1 else weights[0].shape[0]
    columns, unit = weights[0].shape[-2:]
    tile = min(256, tokens)
    parts = max(1, others)

    stacked = order is not None

    def body(order_ref, *refs):
        wide_ref, extra_refs = refs[0], refs[1 : 1 + others]
        w_refs, out_ref = refs[1 + others : -1], refs[-1]
        if not stacked:
            w_refs = units_of(w_refs)
        else:
            w_refs = [w_refs[0].at[order_ref[j]] for j in range(count)]
        total = dot_nt(wide_ref[:, :unit], w_refs[0][...])
        for j in range(1, count):
            total = total + dot_nt(wide_ref[:, j * unit : (j + 1) * unit], w_refs[j][...])
        for i, part in enumerate(epilogue(total, *(e[...] for e in extra_refs))):
            out_ref[:, i * columns : (i + 1) * columns] = part.astype(jnp.bfloat16)

    outs = (shape_of((tokens, parts * columns), jnp.bfloat16),)
    operands = (wide, *extras, *weights)
    specs = [rows_spec(b, tile) for b in (wide, *extras)] + [whole_spec(w) for w in weights]
    order = order if stacked else jnp.zeros((1,), jnp.int32)
    return kernel_call(
        body, order, operands, specs, outs, (rows_spec(outs[0], tile),), (tokens // tile,), [],
        2 * tokens * full * columns, 48,
    )[0]


def weight_grad(lefts, rights, order, by_left):
    tokens, rows = lefts[0].shape
    columns = rights[0].shape[1]
    many = len(lefts)
    units = order.shape[0]
    rows, columns = (rows // units, columns) if by_left else (rows, columns // units)

    def body(_, *refs):
        out_ref = refs[-1]
        total = dot_tn(refs[0][...], refs[many][...])
        for c in range(1, many):
            total = total + dot_tn(refs[c][...], refs[many + c][...])
        out_ref[0] = total.astype(jnp.bfloat16)

    outs = (shape_of((units, rows, columns), jnp.bfloat16),)
    moving = pl.BlockSpec((tokens, rows if by_left else columns), lambda i, *_: (0, i))
    left_specs = [moving if by_left else whole_spec(a) for a in lefts]
    right_specs = [whole_spec(a) if by_left else moving for a in rights]
    out_specs = (pl.BlockSpec((1, rows, columns), lambda i, order_ref: (order_ref[i], 0, 0)),)
    flops = 2 * tokens * many * units * rows * columns
    operands = (*lefts, *rights)
    return kernel_call(
        body, order, operands, left_specs + right_specs, outs, out_specs, (units,), [], flops, 56
    )[0]


def block_grad(lefts, rights, number, count, extras):
    tokens, full = lefts[0].shape
    rows = full // count
    widths = [right.shape[1] for right in rights]
    many, more = len(lefts), len(extras)

    def body(_, *refs):
        out_ref = refs[-1]
        start = 0
        for c, width in enumerate(widths):
            at = slice(start, start + width)
            total = dot_tn(refs[c][...], refs[many + c][...])
            for e, (value, first) in enumerate(extras):
                got = refs[2 * many + e][:, at].astype(jnp.float32)
                if value.shape[0] == rows:
                    total = total + got
                elif first == 0:
                    total = jnp.concatenate([total[: value.shape[0]] + got, total[value.shape[0] :]], 0)
                else:
                    total = jnp.concatenate([total[:first], total[first:] + got], 0)
            out_ref[:, at] = total.astype(jnp.bfloat16)
            start += width

    outs = (shape_of((rows, sum(widths)), jnp.bfloat16),)
    operands = (*lefts, *rights, *(value for value, _ in extras))
    specs = [pl.BlockSpec((tokens, rows), lambda *_: (0, number))] * many + [whole_spec(a) for a in operands[many:]]
    return kernel_call(
        body, jnp.zeros((1,), jnp.int32), operands, specs, outs, (whole_spec(outs[0]),), (1,), [],
        2 * tokens * rows * sum(widths), 32,
    )[0]


def turn(values, cos_wide, sin_wide):
    return values * cos_wide + pltpu.roll(values, values.shape[1] // 2, 1) * sin_wide


def band(rows, cols, first_row, first_col, position):
    distance = (
        lax.broadcasted_iota(jnp.int32, (rows, cols), 0)
        + (first_row - first_col)
        - lax.broadcasted_iota(jnp.int32, (rows, cols), 1)
    )
    return (distance >= 0) & (distance <= position)


def attention_blocks(tokens, most):
    rows = min(256, tokens)
    reach = -(-(most - 1) // rows)
    return rows, [(i * rows, max(0, i - reach) * rows, (i + 1) * rows) for i in range(tokens // rows)]


def attend(raw, position, cos_wide, sin_wide, query_norm, key_norm, q_width, k_width, most, eps):
    tokens = raw.shape[0]
    size = query_norm.shape[1]
    kv_heads, per_group = k_width // size, q_width // k_width
    factor = 1.0 / math.sqrt(size)
    rows, plan = attention_blocks(tokens, most)

    def body(_, q_ref, k_ref, v_ref, pos_ref, cos_ref, sin_ref, qn_ref, kn_ref, qt_ref, kt_ref, vb_ref, mix_ref):
        def turned(value, gain):
            scale = lax.rsqrt(jnp.mean(value * value, 1, keepdims=True) + eps)
            return turn(value * scale * gain, cos_ref[...], sin_ref[...]).astype(jnp.bfloat16)

        kt_ref[...] = turned(k_ref[...], kn_ref[...])
        vb_ref[...] = v_ref[...].astype(jnp.bfloat16)
        for g in range(per_group):
            at = slice(g * size, (g + 1) * size)
            qt_ref[:, at] = turned(q_ref[:, at], qn_ref[...])
        for first, low, high in plan:
            span = slice(first, first + rows)
            allowed = band(rows, high - low, first, low, pos_ref[span, :])
            for g in range(per_group):
                at = slice(g * size, (g + 1) * size)
                scores = dot_nt(qt_ref[span, at], kt_ref[low:high, :]) * factor
                scores = jnp.where(allowed, scores, NEGATIVE)
                weights = jnp.exp(scores - jnp.max(scores, 1, keepdims=True))
                weights = (weights * (1.0 / jnp.sum(weights, 1, keepdims=True))).astype(jnp.bfloat16)
                mix_ref[span, at] = dot_nn(weights, vb_ref[low:high, :]).astype(jnp.bfloat16)

    group = per_group * size
    outs = tuple(shape_of((tokens, w), jnp.bfloat16) for w in (q_width, k_width, k_width, q_width))
    q_spec = pl.BlockSpec((tokens, group), lambda i, *_: (0, i))
    k_spec = pl.BlockSpec((tokens, size), lambda i, *_: (0, q_width // size + i))
    v_spec = pl.BlockSpec((tokens, size), lambda i, *_: (0, (q_width + k_width) // size + i))
    one = pl.BlockSpec((tokens, size), lambda i, *_: (0, i))
    operands = (raw, raw, raw, position, cos_wide, sin_wide, query_norm, key_norm)
    specs = [q_spec, k_spec, v_spec] + [whole_spec(a) for a in operands[3:]]
    flops = 20 * tokens * (high_sum(plan) * rows // tokens) * q_width
    return kernel_call(
        body, jnp.zeros((1,), jnp.int32), operands, specs, outs, (q_spec, one, one, q_spec), (kv_heads,), [], flops, 48
    )


def high_sum(plan):
    return sum(high - low for _, low, high in plan)


def attend_back(raw, turned_q, turned_k, values, grad_mixed, position, cos_wide, sin_wide, query_norm, key_norm, most, eps):
    tokens, q_width = turned_q.shape
    k_width = turned_k.shape[1]
    size = query_norm.shape[1]
    kv_heads, per_group = k_width // size, q_width // k_width
    factor = 1.0 / math.sqrt(size)
    rows, plan = attention_blocks(tokens, most)

    def body(_, q_ref, k_ref, qt_ref, kt_ref, v_ref, dm_ref, pos_ref, cos_ref, sin_ref, qn_ref, kn_ref,
             dq_ref, dk_ref, dv_ref, gain_ref, key_sum, value_sum):
        key_sum[...] = jnp.zeros_like(key_sum)
        value_sum[...] = jnp.zeros_like(value_sum)

        def back(raw_rows, gain, upstream, span):
            scale = lax.rsqrt(jnp.mean(raw_rows * raw_rows, 1, keepdims=True) + eps)
            turned_back = turn(upstream, cos_ref[span, :], -sin_ref[span, :])
            inner = jnp.mean(turned_back * gain * raw_rows, 1, keepdims=True)
            grad = scale * gain * turned_back - raw_rows * (scale * scale * scale * inner)
            return grad.astype(jnp.bfloat16), jnp.sum(turned_back * raw_rows * scale, 0, keepdims=True)

        query_gain = jnp.zeros((1, size), jnp.float32)
        for first, low, high in plan:
            span = slice(first, first + rows)
            allowed = band(rows, high - low, first, low, pos_ref[span, :])
            for g in range(per_group):
                at = slice(g * size, (g + 1) * size)
                queries, upstream = qt_ref[span, at], dm_ref[span, at]
                scores = dot_nt(queries, kt_ref[low:high, :]) * factor
                scores = jnp.where(allowed, scores, NEGATIVE)
                probs = jnp.exp(scores - jnp.max(scores, 1, keepdims=True))
                probs = probs * (1.0 / jnp.sum(probs, 1, keepdims=True))
                grads = dot_nt(upstream, v_ref[low:high, :])
                weighted = probs * grads
                total = jnp.sum(weighted, 1, keepdims=True)
                grads = (weighted - probs * total).astype(jnp.bfloat16)
                value_sum[low:high, :] += dot_tn(probs.astype(jnp.bfloat16), upstream)
                key_sum[low:high, :] += dot_tn(grads, queries)
                grad_turned = dot_nn(grads, kt_ref[low:high, :]) * factor
                grad, gain = back(q_ref[span, at], qn_ref[...], grad_turned, span)
                dq_ref[span, at] = grad
                query_gain = query_gain + gain
        grad, key_gain = back(k_ref[...], kn_ref[...], key_sum[...] * factor, slice(0, tokens))
        dk_ref[...] = grad
        dv_ref[...] = value_sum[...].astype(jnp.bfloat16)
        gain_ref[...] = jnp.concatenate([query_gain, key_gain, jnp.zeros((6, size), jnp.float32)], 0)

    group = per_group * size
    outs = (
        shape_of((tokens, q_width), jnp.bfloat16),
        shape_of((tokens, k_width), jnp.bfloat16),
        shape_of((tokens, k_width), jnp.bfloat16),
        shape_of((8 * kv_heads, size), jnp.float32),
    )
    q_spec = pl.BlockSpec((tokens, group), lambda i, *_: (0, i))
    k_spec = pl.BlockSpec((tokens, size), lambda i, *_: (0, q_width // size + i))
    one = pl.BlockSpec((tokens, size), lambda i, *_: (0, i))
    operands = (raw, raw, turned_q, turned_k, values, grad_mixed, position, cos_wide, sin_wide, query_norm, key_norm)
    specs = [q_spec, k_spec, q_spec, one, one, q_spec] + [whole_spec(a) for a in operands[6:]]
    out_specs = (q_spec, one, one, pl.BlockSpec((8, size), lambda i, *_: (i, 0)))
    scratch = [pltpu.VMEM((tokens, size), jnp.float32)] * 2
    flops = 28 * tokens * (high_sum(plan) * rows // tokens) * q_width
    return kernel_call(
        body, jnp.zeros((1,), jnp.int32), operands, specs, outs, out_specs, (kv_heads,), scratch, flops, 48
    )


def local(
    hidden_in,
    seq_lengths,
    attn_norm,
    w_query,
    key_weight,
    value_weight,
    query_norm,
    key_norm,
    w_output,
    ffwd_norm,
    w_gate,
    w_up,
    w_down,
    cotangent,
):
    low, f32 = jnp.bfloat16, jnp.float32
    tokens, part_width = hidden_in.shape
    full_width = part_width * lax.axis_size("col")
    head_size = query_norm.shape[0]
    q_width, k_width = w_query.shape[1], key_weight.shape[1]
    ring = Ring()
    place, plain_place, pair_place = ring.place, ring.plain_place, ring.pair_place
    steps, pairs, half = ring.half, ring.half, tokens // 2
    pair_order = jnp.arange(pairs, dtype=jnp.int32)
    chain = Chain()
    pin, run = chain.pin, chain.run

    def near(value):
        return swap(value, "col", 1)

    def far(value):
        return swap(value, "col", 2)

    qkv = pin(jnp.concatenate([w_query, key_weight, value_weight], 1))
    qkv = ring.inner_gather(qkv, 0)
    on, back = ring.send_on(qkv), ring.send_back(qkv)
    output_all = ring.gather_stack(ring.inner_gather(w_output, 1))
    hidden_far = far(hidden_in)
    gains = jnp.stack([attn_norm, ffwd_norm])
    gains_far = far(gains)
    behind, ahead = [], []
    on, back = pin(on, back)
    behind.append(on)
    ahead.append(back)
    on, back = ring.send_on(on), ring.send_back(back)
    hidden_far, gains_far = pin(hidden_far, gains_far)
    hidden_blocks = [hidden_in, hidden_far, near(hidden_in), near(hidden_far)]
    gains_near = near(gains)
    on, back, gains_near, gate, up = pin(on, back, gains_near, w_gate, w_up)
    behind.append(on)
    ahead.append(back)
    on, back = ring.send_on(on), ring.send_back(back)
    gate_up = [ring.inner_gather(w, 0) for w in (gate, up)]
    gate_up_mine = side_of(gate_up, 1, ring.parity)
    gate_up_got = ring.to_partner(side_of(gate_up, 1, 1 - ring.parity))
    gains_diagonal, gate_up_mine, *hidden_blocks = pin(near(gains_far), gate_up_mine, *hidden_blocks)
    on, back = pin(on, back)
    behind.append(on)
    ahead.append(back)
    cut = on.shape[0] // 2
    on, back = ring.send_on(on[:cut]), ring.send_back(back[cut:])
    on, back, gate_up_got = pin(on, back, gate_up_got)
    qkv_all = [qkv, *behind, jnp.concatenate([on, back], 0), *ahead[::-1]]
    gate_up, output_all = pin(jnp.concatenate([gate_up_mine, gate_up_got], 0), output_all)
    gate_up_all = pair_gather(ring, gate_up)
    gains = jnp.stack([gains, gains_far, gains_near, gains_diagonal], 1).reshape(2, 1, full_width)

    down, upstream = pin(w_down, cotangent)
    down = [ring.inner_gather(down, 1)]
    down_mine = side_of(down, 0, ring.parity)
    down_got = ring.to_partner(side_of(down, 0, 1 - ring.parity))
    up_far, up_partner = far(upstream), ring.to_partner(upstream)
    position = tables(seq_lengths[0], tokens)
    cos_wide, sin_wide = rotary(position, head_size)
    turning = (position[:, None], cos_wide, sin_wide, query_norm[None, :], key_norm[None, :])
    residual = hidden_in.astype(f32)
    wide_one, factor_one, qkv_raw = run(
        lambda blocks, gain, weights: gather_norm_matmul(place, blocks, gain, weights, EPS), hidden_blocks, gains[0], qkv_all
    )
    turned_q, turned_k, values, mixed = run(
        lambda raw: attend(raw, *turning, q_width, k_width, MOST, EPS), qkv_raw
    )
    up_far, up_partner, down_got, down_mine = pin(up_far, up_partner, down_got, down_mine)
    keep, send = run(lambda left, weights: spread_product(plain_place, left, [weights], False), mixed, output_all)
    got = near(send)
    up_near, up_diagonal = near(upstream), near(up_far)
    keep, got = pin(keep, got)
    both = keep.astype(f32) + got
    attended = far(pin(both[:, part_width:].astype(low)))
    corner = far(pin(up_partner[:half])), ring.to_partner(up_far[half:])
    up_near, up_diagonal = pin(up_near, up_diagonal)
    upstream_wide = run(lambda *blocks: assemble(pair_place, blocks), upstream, up_far, up_near, up_diagonal)
    attended, both = pin(attended, both)

    middle = residual + both[:, :part_width] + attended
    middle, middle_low = pin(middle, middle.astype(low))
    mid_far, mid_partner = far(middle_low), ring.to_partner(middle_low)
    mid_near = near(middle_low)
    up_corner = pin(jnp.concatenate(pin(*corner), 0))
    up_partner_near, up_corner_near = near(up_partner), near(up_corner)
    down_unit = pin(jnp.concatenate([down_mine, down_got], 1))
    mid_near, up_partner_near, up_corner_near = pin(mid_near, up_partner_near, up_corner_near)
    upstream_other = run(lambda *blocks: assemble(pair_place, blocks), up_partner, up_corner, up_partner_near, up_corner_near)
    mid_far = pin(mid_far)
    mid_diagonal = near(mid_far)
    mid_partner = pin(mid_partner)
    corner = far(mid_partner[:half]), ring.to_partner(mid_far[half:])
    mid_partner_near = near(mid_partner)
    gate_up_all = pin(gate_up_all)
    down_all = pair_gather(ring, pin(down_unit))
    mid_diagonal = pin(mid_diagonal)

    def swish(blocks, gain, weights):
        return gather_swish(pair_place, blocks, gain, weights, EPS)

    normed, factor_two, gate, up, hidden = run(
        swish, [middle_low, mid_far, mid_near, mid_diagonal], gains[1], gate_up_all
    )
    mid_partner_near, *corner = pin(mid_partner_near, *corner)
    mid_corner = pin(jnp.concatenate(corner, 0))
    mid_corner_near = pin(near(mid_corner))
    normed_other, _, gate_other, up_other, hidden_other = run(
        swish, [mid_partner, mid_corner, mid_partner_near, mid_corner_near], gains[1], gate_up_all
    )
    down_grad = run(
        lambda *ops: weight_grad(ops[:2], ops[2:], pair_order, False), hidden, hidden_other, upstream_wide, upstream_other
    )
    down_grad = pair_sum(ring, down_grad)

    down_all = pin(down_all)

    def back_swish(wide, weights, gate_value, up_value):
        return swish_back(wide, [weights], gate_value, up_value)

    def spread_back(left, weights, normed_rows):
        return spread_product(pair_place, left, [weights], True, normed_rows)

    low_other = run(back_swish, upstream_other, down_all, gate_other, up_other)
    keep_other, send_other, inner_other = run(spread_back, low_other, gate_up_all, normed_other)
    got_other, inner_other = near(send_other), ring.to_partner(pin(inner_other[:, 0]))
    low_mine, got_other, inner_other = run(
        back_swish, upstream_wide, down_all, gate, up, beside=(got_other, inner_other)
    )
    both_other = pin(keep_other).astype(f32) + got_other
    both_other, corner = pin(both_other, both_other[:, part_width:].astype(low))
    from_far, from_partner = far(corner[:half]), ring.to_partner(corner[half:])
    gate_up_grad, from_far, from_partner = run(
        lambda *ops: weight_grad(ops[:2], ops[2:], pair_order, True),
        normed,
        normed_other,
        low_mine,
        low_other,
        beside=(from_far, from_partner),
    )
    to_partner = jnp.concatenate([both_other[:half, :part_width] + from_far, both_other[half:, :part_width]], 0)
    to_partner, down_grad = pin(to_partner.astype(low), down_grad)
    gate_up_grad = pair_sum(ring, gate_up_grad)
    to_partner = ring.to_partner(to_partner)
    keep, send, inner = run(spread_back, low_mine, gate_up_all, normed)
    got = near(send)
    inner = pin(inner[:, 0] + inner_other)
    inner_near = near(inner)
    keep, got, inner_near = pin(keep, got, inner_near)
    both = keep.astype(f32) + got
    to_far = jnp.concatenate([both[:half, part_width:], both[half:, part_width:] + from_partner], 0)
    own, to_far, inner = pin(both[:, :part_width], to_far.astype(low), inner + inner_near)
    inner_far = far(inner)
    from_far = far(to_far)
    cut = down_grad.shape[1] // 2
    down_got = ring.to_partner(pin(down_grad[:, cut:]))

    def spread_down(left, weights):
        return spread_product(pair_place, left, [weights], False)

    out_keep_other, out_send_other = run(spread_down, hidden_other, down_all)
    out_keep, out_send, inner_far = run(spread_down, hidden, down_all, beside=(inner_far,))
    own, from_partner, from_far = pin(own, to_partner, from_far)
    grad_normed = own + from_partner + from_far
    inner = (inner + inner_far)[:, None] / full_width
    grad_middle = (
        cotangent.astype(f32)
        + factor_two * ffwd_norm * grad_normed
        - middle * (factor_two * factor_two * inner)
    )
    grad_middle, grad_low = pin(grad_middle, grad_middle.astype(low))
    grad_far, grad_near = far(grad_low), near(grad_low)
    out_got_other, out_got = near(out_send_other), near(out_send)
    out_got_other, out_got, out_keep_other = pin(out_got_other, out_got, out_keep_other)
    both_other = out_keep_other.astype(f32) + out_got_other
    both_other, corner = pin(both_other, both_other[:, part_width:].astype(low))
    grad_far, grad_near, down_got = pin(grad_far, grad_near, down_got)
    grad_diagonal = pin(near(grad_far))

    middle_wide = run(lambda *blocks: assemble(place, blocks), grad_low, grad_far, grad_near, grad_diagonal)
    grad_mixed = run(lambda wide, weights: times_transposed(wide, [weights], ring.behind), middle_wide, output_all)
    gate_up_grad = pin(gate_up_grad)
    columns_here = gate_up_grad.shape[0] // 2
    gate_up_got = ring.to_partner(pin(gate_up_grad[columns_here:]))
    out_far, out_partner = far(corner[:half]), ring.to_partner(corner[half:])
    query_low, key_low, value_low, head_gains, gate_up_got, out_far, out_partner = run(
        lambda *ops: attend_back(*ops, *turning, MOST, EPS),
        qkv_raw,
        turned_q,
        turned_k,
        values,
        grad_mixed,
        beside=(gate_up_got, out_far, out_partner),
    )
    qkv_low = pin(jnp.concatenate([query_low, key_low, value_low], 1))

    def part(j, extras):
        ops = (wide_one, middle_wide, qkv_low, mixed, *(value for value, _ in extras))
        return run(
            lambda *ops: block_grad(ops[:2], ops[2:4], j, ring.count, list(zip(ops[4:], (r for _, r in extras), strict=True))), *ops
        )

    first = part(ring.half, [])
    cut = first.shape[0] // 2
    on, back = ring.send_on(first[:cut]), ring.send_back(first[cut:])
    keep, send, inner, attn_gain, on, back = run(
        lambda left, weights, wide: spread_product(place, left, weights, True, wide, True),
        qkv_low,
        qkv_all,
        wide_one,
        beside=(on, back),
    )
    got = near(send)
    gain_keep, gain_send = attn_gain[:1, : full_width // 2], attn_gain[:1, full_width // 2 :]
    head_gains = jnp.sum(head_gains.reshape(-1, 8, head_size), 0)[:2].reshape(-1)
    sums = pin(jnp.concatenate([gain_send[0], head_gains, inner[:, 0]]))
    sums_got = near(sums)
    on = part(ring.half + 1, [(on, 0)])
    back, got, sums_got = run(
        lambda *ops: block_grad(ops[:2], ops[2:4], ring.half - 1, ring.count, [(ops[4], cut)]),
        wide_one,
        middle_wide,
        qkv_low,
        mixed,
        back,
        beside=(got, sums_got),
    )
    on, back = ring.send_on(on), ring.send_back(back)
    both_gain = gain_keep[0] + sums_got[: full_width // 2]
    sums = jnp.concatenate([both_gain[part_width:], (sums + sums_got)[full_width // 2 :]])
    sums = pin(sums)
    sums_got = far(sums)
    both = keep.astype(f32) + got
    both, to_far, sums_got = pin(both, both[:, part_width:].astype(low), sums_got)
    grad_far = far(to_far)
    to_partner = jnp.concatenate([both_other[:half, :part_width] + out_far, both_other[half:, :part_width]], 0)
    out_both = out_keep.astype(f32) + out_got
    to_far = jnp.concatenate([out_both[:half, part_width:], out_both[half:, part_width:] + out_partner], 0)
    attn_gain = (both_gain[:part_width] + sums_got[:part_width]) / attn_norm
    rest = (sums + sums_got)[part_width:]
    inner = rest[2 * head_size :][:, None] / full_width
    ffwd_gain = jnp.sum(grad_normed * middle * factor_two, 0)
    sums = jnp.concatenate([attn_gain, ffwd_gain, rest[: 2 * head_size]])
    out_own, to_partner, to_far, sums, on, back = pin(
        out_both[:, :part_width], to_partner.astype(low), to_far.astype(low), sums, on, back
    )
    on, back = part(ring.half + 2, [(on, 0)]), part(ring.half - 2, [(back, 0)])
    on, back = ring.send_on(on), ring.send_back(back)
    bit, rows = 1, lax.axis_size("row")
    sums_got = swap(sums, "row", bit)
    grad_far, sums_got = pin(grad_far, sums_got)
    out_partner, out_far = ring.to_partner(to_partner), far(to_far)
    hidden_grad = (
        grad_middle
        + factor_one * attn_norm * (both[:, :part_width] + grad_far)
        - residual * (factor_one * factor_one * inner)
    )
    sums, hidden_grad = pin(sums + sums_got, hidden_grad)
    gate_grad, up_grad = (
        pair_join(ring, gate_up_grad[:columns_here, at], gate_up_got[:, at], 1)
        for at in (slice(0, gate_up_grad.shape[1] // 2), slice(gate_up_grad.shape[1] // 2, None))
    )
    gate_grad, up_grad = pin(gate_grad, up_grad)
    bit *= 2
    sums_got = swap(sums, "row", bit)
    on, back, sums_got = pin(on, back, sums_got)
    on, back = part(ring.half + 3, [(on, 0)]), part(ring.half - 3, [(back, 0)])
    on, back = ring.send_on(on), ring.send_back(back)
    sums = pin(sums + sums_got)
    bit *= 2
    while bit < rows:
        sums = pin(sums + swap(sums, "row", bit))
        bit *= 2
    out_partner, out_far = pin(out_partner, out_far)
    hidden_out = pin((middle + out_own + out_partner + out_far).astype(low))
    down_cut = down_grad.shape[1] // 2
    down_out = pin(pair_join(ring, down_grad[:, :down_cut], down_got, 0))
    on, back = pin(on, back)
    total = ring.inner_sum(part(0, [(on, 0), (back, 0)]).astype(f32), 0)
    attn_gain, ffwd_gain, query_gain, key_gain = jnp.split(
        sums, [part_width, 2 * part_width, 2 * part_width + head_size]
    )
    return (
        hidden_out,
        hidden_grad,
        attn_gain,
        total[:, :q_width],
        total[:, q_width : q_width + k_width],
        total[:, q_width + k_width : q_width + 2 * k_width],
        query_gain,
        key_gain,
        total[:, q_width + 2 * k_width :].T,
        ffwd_gain,
        gate_grad,
        up_grad,
        down_out,
    )


def solution(mesh):
    in_specs = (
        P("row", "col"),
        P("row", None),
        P("col"),
        P("row", "col"),
        P("row", "col"),
        P("row", "col"),
        P(),
        P(),
        P("col", "row"),
        P("col"),
        P("row", "col"),
        P("row", "col"),
        P("col", "row"),
        P("row", "col"),
    )
    out_specs = (
        P("row", "col"),
        P("row", "col"),
        P("col"),
        P("row", "col"),
        P("row", "col"),
        P("row", "col"),
        P(),
        P(),
        P("col", "row"),
        P("col"),
        P("row", "col"),
        P("row", "col"),
        P("col", "row"),
    )
    return jax.shard_map(local, mesh=mesh, in_specs=in_specs, out_specs=out_specs, check_vma=False)
```

time: 734 us -> 642 us (0.87)
  waiting for transfers between devices: 331 us -> 222 us
  Pallas kernels: 133 us -> 207 us
  starting transfers between devices: 134 us -> 60.2 us
  matrix products: 50.1 us -> 0 us
  other arithmetic: 29.3 us -> 60.3 us
  local copies, waits for them, and re-layouts: 47.6 us -> 70.9 us
  between operations: 2.92 us -> 15.2 us
    ppermute x48 -> x8, waiting for transfers between devices: 210 us -> 44.5 us  [send_on(): return lax.ppermute(value, 'row', self.onward)]
    pallas_call x10 -> x27, Pallas kernels: 133 us -> 207 us  [kernel_call(): pl.pallas_call(body, grid_spec=pltpu.PrefetchScalarGridSpec(num_scalar_pr...]
    ppermute x48 -> x8, starting transfers between devices: 79.2 us -> 9.77 us  [send_on(): return lax.ppermute(value, 'row', self.onward)]
    dot_general x48 -> x0, matrix products: 50.1 us -> none  [dot_tn(): lax.dot_general(left_side, right_side, (((0,), (0,)), ((), ())), preferre...]
    ppermute x48 -> x8, waiting for transfers between devices: 82.3 us -> 35.5 us  [send_back(): return lax.ppermute(value, 'row', self.backward)]
    ppermute x37 -> x40, waiting for transfers between devices: 38.6 us -> 80.4 us  [swap(): lax.ppermute(value, axis, [(i, i ^ bit) for i in range(lax.axis_size(axis...]
    ppermute x0 -> x13, waiting for transfers between devices: none -> 37.7 us  [to_partner(): return lax.ppermute(value, 'row', self.partner)]
    ppermute x48 -> x8, starting transfers between devices: 25.3 us -> 7.76 us  [send_back(): return lax.ppermute(value, 'row', self.backward)]
  transfers between devices with their start and end apart: 133 -> 74, of which waited for: 59 -> 38; matrix products, arithmetic and copies ran while one was open for 11% -> 14% of each run, Pallas kernels for 11% -> 32%
where the time goes in v3:
time: 642 us; the launch traced here: 635 us
  waiting for transfers between devices  222 us (35%)
  Pallas kernels  207 us (32%)
  local copies, waits for them, and re-layouts  70.9 us (11%)
  other arithmetic  60.3 us (9%)
  starting transfers between devices  60.2 us (9%)
  between operations  15.2 us (2%)
    pallas_call x27, Pallas kernels, kernel_call(): pl.pallas_call(body, grid_spec=pltpu.PrefetchScalarGridSpec(num_scalar_pr...  207 us
    ppermute x40, waiting for transfers between devices, swap(): lax.ppermute(value, axis, [(i, i ^ bit) for i in range(lax.axis_size(axis...  80.4 us
    ppermute x8, waiting for transfers between devices, send_on(): return lax.ppermute(value, 'row', self.onward)  44.5 us
    unnamed x203, local copies, waits for them, and re-layouts  41.5 us
    ppermute x13, waiting for transfers between devices, to_partner(): return lax.ppermute(value, 'row', self.partner)  37.7 us
    ppermute x8, waiting for transfers between devices, send_back(): return lax.ppermute(value, 'row', self.backward)  35.5 us
    ppermute x40, starting transfers between devices, swap(): lax.ppermute(value, axis, [(i, i ^ bit) for i in range(lax.axis_size(axis...  28.2 us
    all_gather x2, waiting for transfers between devices, pair_gather(): return lax.all_gather(unit, 'row', axis=0, axis_index_groups=ring.pairs)  16.2 us
  transfers between devices with their start and end apart: 74, of which 38 were waited for; matrix products, arithmetic and copies ran while one was open for 14% of the time, Pallas kernels for 32%

profile of v3, /device:TPU:0, one launch (start us, length us, event | category | flops | bytes accessed | tf_op | source)
XLA Modules:
  0.0 635.2 jit_solution(10341173244949636103)
XLA Ops:
  14.2 14.3 %collective-permute-done.1.refs_12_.refs_8_ = bf16[256,1024]{1,0:T(8,128)(2,1)S(1)} collective-permute-done((bf16[256,1024]{1,0:T(8,128)(2,1)S(1)}, bf16[256,1024]{1,0:T(8,128)(2,1)S(1)}, u32[]{:S(2)}, u32[]{:S(2)}) %collective-permute-start.1) | collective-permute-done | bytes 524320 | tf_op jit(solution)/shard_map/ppermute | solution.py:76
  53.0 16.8 %collective-permute-done.10.refs_8_.refs_4_ = bf16[256,1024]{1,0:T(8,128)(2,1)S(1)} collective-permute-done((bf16[256,1024]{1,0:T(8,128)(2,1)S(1)}, bf16[256,1024]{1,0:T(8,128)(2,1)S(1)}, u32[]{:S(2)}, u32[]{:S(2)}) %collective-permute-start.10) | collective-permute-done | bytes 524320 | tf_op jit(solution)/shard_map/ppermute | solution.py:73
  76.6 10.1 %collective-permute-done.14 = bf16[256,1536]{1,0:T(8,128)(2,1)S(1)} collective-permute-done((bf16[256,1536]{1,0:T(8,128)(2,1)S(1)}, bf16[256,1536]{1,0:T(8,128)(2,1)S(1)}, u32[]{:S(2)}, u32[]{:S(2)}) %collective-permute-start.14) | collective-permute-done | bytes 786464 | tf_op jit(solution)/shard_map/ppermute | solution.py:79
  101.2 11.6 %shard_map.273 = (bf16[1024,2048]{1,0:T(8,128)(2,1)}, f32[1024,1]{1,0:T(8,128)S(1)}, f32[1024,1024]{1,0:T(8,128)}) custom-call(s32[8]{0:T(128)S(1)} %get-tuple-element.1000.place_ref, bf16[1024,512]{1,0:T(8,128)(2,1)S(1)} %copy-done.13, bf16[1024,512]{1,0:T(8,128)(2,1)} %collective-permute-done.2.refs_1_, bf16[1024,512]{1,0:T(8,128)(2,1)} %collective-permute-done.8.refs_2_, ...), custom_call_target="tpu_custom_call" | custom-call | flops 85899344 | bytes 65536 | tf_op jit(solution)/shard_map/pallas_call | solution.py:164
  112.8 14.0 %shard_map.274 = (bf16[1024,512]{1,0:T(8,128)(2,1)S(1)}, bf16[1024,256]{1,0:T(8,128)(2,1)S(1)}, bf16[1024,256]{1,0:T(8,128)(2,1)S(1)}, bf16[1024,512]{1,0:T(8,128)(2,1)S(1)}) custom-call(s32[1]{0:T(128)} %constant.69.clone.1._.order_ref, f32[1024,1024]{1,0:T(8,128)} %get-tuple-element.760.q_ref.k_ref.v_ref, ...), custom_call_target="tpu_custom_call" | custom-call | flops 120795952 | bytes 65536 | tf_op jit(solution)/shard_map/pallas_call | solution.py:164
  147.2 19.0 %collective-permute-done.21 = bf16[1024,512]{1,0:T(8,128)(2,1)S(1)} collective-permute-done((bf16[1024,512]{1,0:T(8,128)(2,1)S(1)}, bf16[1024,512]{1,0:T(8,128)(2,1)S(1)}, u32[]{:S(2)}, u32[]{:S(2)}) %collective-permute-start.21) | collective-permute-done | bytes 1048608 | tf_op jit(solution)/shard_map/ppermute | solution.py:140
  168.5 8.2 %collective-permute-done.22 = bf16[512,512]{1,0:T(8,128)(2,1)S(1)} collective-permute-done((bf16[512,512]{1,0:T(8,128)(2,1)S(1)}, bf16[512,512]{1,0:T(8,128)(2,1)S(1)}, u32[]{:S(2)}, u32[]{:S(2)}) %collective-permute-start.22) | collective-permute-done | bytes 524320 | tf_op jit(solution)/shard_map/ppermute | solution.py:140
  188.6 15.0 %collective-permute-done.27.refs_1_ = bf16[1024,512]{1,0:T(8,128)(2,1)} collective-permute-done((bf16[1024,512]{1,0:T(8,128)(2,1)}, bf16[1024,512]{1,0:T(8,128)(2,1)}, u32[]{:S(2)}, u32[]{:S(2)}) %collective-permute-start.27) | collective-permute-done | bytes 1048608 | tf_op jit(solution)/shard_map/ppermute | solution.py:140
  214.0 15.3 %shard_map.278 = (bf16[1024,2048]{1,0:T(8,128)(2,1)}, f32[1024,1]{1,0:T(8,128)S(1)}, f32[1024,768]{1,0:T(8,128)}, f32[1024,768]{1,0:T(8,128)}, bf16[1024,768]{1,0:T(8,128)(2,1)}) custom-call(s32[8]{0:T(128)S(1)} %fusion.7.place_ref, bf16[1024,512]{1,0:T(8,128)(2,1)} %get-tuple-element.586.refs_0_, bf16[1024,512]{1,0:T(8,128)(2,1)} %collective-permute-done.27.refs_1_, ...), custom_call_target="tpu_custom_call" | custom-call | flops 128849016 | bytes 65536 | tf_op jit(solution)/shard_map/pallas_call | solution.py:164
  232.8 14.2 %shard_map.279 = (bf16[1024,2048]{1,0:T(8,128)(2,1)}, f32[1024,1]{1,0:T(8,128)}, f32[1024,768]{1,0:T(8,128)}, f32[1024,768]{1,0:T(8,128)}, bf16[1024,768]{1,0:T(8,128)(2,1)}) custom-call(s32[8]{0:T(128)S(1)} %fusion.7.place_ref, bf16[1024,512]{1,0:T(8,128)(2,1)} %collective-permute-done.28.refs_0_, bf16[1024,512]{1,0:T(8,128)(2,1)S(1)} %pad_maximum_fusion.6.refs_1_, ...), custom_call_target="tpu_custom_call" | custom-call | flops 128849016 | bytes 65536 | tf_op jit(solution)/shard_map/pallas_call | solution.py:164
  247.5 11.5 %shard_map.280 = bf16[4,768,512]{2,1,0:T(8,128)(2,1)} custom-call(s32[4]{0:T(128)} %iota.28._, bf16[1024,768]{1,0:T(8,128)(2,1)} %get-tuple-element.709.refs_0_, bf16[1024,768]{1,0:T(8,128)(2,1)} %get-tuple-element.703.refs_1_.refs_0_, bf16[1024,2048]{1,0:T(8,128)(2,1)} %copy-done.9, bf16[1024,2048]{1,0:T(8,128)(2,1)} %copy-done.10), custom_call_target="tpu_custom_call" | custom-call | flops 128849016 | bytes 65536 | tf_op jit(solution)/shard_map/pallas_call | solution.py:164
  259.1 13.0 %all-gather.11.cloned.1.call-done = bf16[3072,512]{1,0:T(8,128)(2,1)} async-done(((bf16[768,512]{1,0:T(8,128)(2,1)}), bf16[3072,512]{1,0:T(8,128)(2,1)}) %all-gather.11.cloned.1.call-update) | async-done | bytes 3145744 | tf_op jit(solution)/shard_map/all_gather | solution.py:108
  272.1 8.8 %shard_map.281.refs_0_.refs_3_ = bf16[1024,1536]{1,0:T(8,128)(2,1)S(1)} custom-call(s32[1]{0:T(128)} %constant.69.clone.1._.order_ref, bf16[1024,2048]{1,0:T(8,128)(2,1)} %copy-done.10, f32[1024,768]{1,0:T(8,128)} %get-tuple-element.636.refs_1_, f32[1024,768]{1,0:T(8,128)} %get-tuple-element.637.refs_2_, bf16[4,768,512]{2,1,0:T(8,128)(2,1)} %bitcast.61), custom_call_target="tpu_custom_call" | custom-call | flops 64424508 | bytes 65536 | tf_op jit(solution)/shard_map/pallas_call | solution.py:164
  282.5 12.9 %shard_map.282 = (bf16[1024,1024]{1,0:T(8,128)(2,1)S(1)}, bf16[1024,1024]{1,0:T(8,128)(2,1)}, f32[1024,1]{1,0:T(8,128)S(1)}) custom-call(s32[8]{0:T(128)S(1)} %fusion.7.place_ref, bf16[1024,1536]{1,0:T(8,128)(2,1)} %copy-done.12, bf16[4,512,1536]{2,1,0:T(8,128)(2,1)} %bitcast.59, bf16[1024,2048]{1,0:T(8,128)(2,1)} %get-tuple-element.671.refs_2_.refs_1_), custom_call_target="tpu_custom_call" | custom-call | flops 128849016 | bytes 65536 | tf_op jit(solution)/shard_map/pallas_call | solution.py:164
  300.1 8.3 %shard_map.283.refs_2_.refs_0_ = bf16[1024,1536]{1,0:T(8,128)(2,1)S(1)} custom-call(s32[1]{0:T(128)} %constant.69.clone.1._.order_ref, bf16[1024,2048]{1,0:T(8,128)(2,1)} %copy-done.9, f32[1024,768]{1,0:T(8,128)} %get-tuple-element.656.refs_1_, f32[1024,768]{1,0:T(8,128)} %get-tuple-element.657.refs_2_, bf16[4,768,512]{2,1,0:T(8,128)(2,1)} %bitcast.62), custom_call_target="tpu_custom_call" | custom-call | flops 64424508 | bytes 65536 | tf_op jit(solution)/shard_map/pallas_call | solution.py:164
  317.7 19.2 %shard_map.284 = bf16[4,512,1536]{2,1,0:T(8,128)(2,1)} custom-call(s32[4]{0:T(128)} %iota.29._, bf16[1024,2048]{1,0:T(8,128)(2,1)} %get-tuple-element.683.refs_0_.refs_2_, bf16[1024,2048]{1,0:T(8,128)(2,1)} %get-tuple-element.671.refs_2_.refs_1_, bf16[1024,1536]{1,0:T(8,128)(2,1)} %copy-done.11, bf16[1024,1536]{1,0:T(8,128)(2,1)} %copy-done.12), custom_call_target="tpu_custom_call" | custom-call | flops 257698032 | bytes 65536 | tf_op jit(solution)/shard_map/pallas_call | solution.py:164
  340.9 13.5 %shard_map.285 = (bf16[1024,1024]{1,0:T(8,128)(2,1)S(1)}, bf16[1024,1024]{1,0:T(8,128)(2,1)}, f32[1024,1]{1,0:T(8,128)S(1)}) custom-call(s32[8]{0:T(128)S(1)} %fusion.7.place_ref, bf16[1024,1536]{1,0:T(8,128)(2,1)} %copy-done.11, bf16[4,512,1536]{2,1,0:T(8,128)(2,1)} %bitcast.60, bf16[1024,2048]{1,0:T(8,128)(2,1)} %get-tuple-element.683.refs_0_.refs_2_), custom_call_target="tpu_custom_call" | custom-call | flops 128849016 | bytes 65536 | tf_op jit(solution)/shard_map/pallas_call | solution.py:164
  380.3 8.0 %shard_map.287 = (bf16[1024,1024]{1,0:T(8,128)(2,1)S(1)}, bf16[1024,1024]{1,0:T(8,128)(2,1)}) custom-call(s32[8]{0:T(128)S(1)} %fusion.7.place_ref, bf16[1024,768]{1,0:T(8,128)(2,1)S(1)} %copy-done.16, bf16[4,768,512]{2,1,0:T(8,128)(2,1)} %bitcast.64), custom_call_target="tpu_custom_call" | custom-call | flops 64424508 | bytes 65536 | tf_op jit(solution)/shard_map/pallas_call | solution.py:164
  414.7 12.1 %collective-permute-done.45.refs_1_ = bf16[1024,512]{1,0:T(8,128)(2,1)S(1)} collective-permute-done((bf16[1024,512]{1,0:T(8,128)(2,1)S(1)}, bf16[1024,512]{1,0:T(8,128)(2,1)S(1)}, u32[]{:S(2)}, u32[]{:S(2)}) %collective-permute-start.45) | collective-permute-done | bytes 1048608 | tf_op jit(solution)/shard_map/ppermute | solution.py:140
  452.4 19.6 %shard_map.290 = (bf16[1024,512]{1,0:T(8,128)(2,1)S(1)}, bf16[1024,256]{1,0:T(8,128)(2,1)S(1)}, bf16[1024,256]{1,0:T(8,128)(2,1)S(1)}, f32[16,128]{1,0:T(8,128)S(1)}) custom-call(s32[1]{0:T(128)} %constant.69.clone.1._.order_ref, f32[1024,1024]{1,0:T(8,128)} %get-tuple-element.760.q_ref.k_ref.v_ref, f32[1024,1024]{1,0:T(8,128)} %get-tuple-element.760.q_ref.k_ref.v_ref, ...), custom_call_target="tpu_custom_call" | custom-call | flops 169114336 | bytes 65536 | tf_op jit(solution)/shard_map/pallas_call | solution.py:164
  489.5 9.7 %shard_map.292 = (bf16[1024,1024]{1,0:T(8,128)(2,1)}, bf16[1024,1024]{1,0:T(8,128)(2,1)}, f32[1024,1]{1,0:T(8,128)S(1)}, f32[8,2048]{1,0:T(8,128)S(1)}) custom-call(s32[8]{0:T(128)S(1)} %get-tuple-element.1000.place_ref, bf16[1024,1024]{1,0:T(8,128)(2,1)} %copy-done.7, bf16[256,1024]{1,0:T(8,128)(2,1)S(1)} %copy-done.19, bf16[256,1024]{1,0:T(8,128)(2,1)S(1)} %copy-done.39, ...), custom_call_target="tpu_custom_call" | custom-call | flops 85899344 | bytes 65536 | tf_op jit(solution)/shard_map/pallas_call | solution.py:164
  539.8 14.9 %collective-permute-done.57.refs_4_ = bf16[256,1536]{1,0:T(8,128)(2,1)} collective-permute-done((bf16[256,1536]{1,0:T(8,128)(2,1)}, bf16[256,1536]{1,0:T(8,128)(2,1)}, u32[]{:S(2)}, u32[]{:S(2)}) %collective-permute-start.57) | collective-permute-done | bytes 786464 | tf_op jit(solution)/shard_map/ppermute | solution.py:73
  596.1 14.5 %collective-permute-done.65 = bf16[1024,512]{1,0:T(8,128)(2,1)S(1)} collective-permute-done((bf16[1024,512]{1,0:T(8,128)(2,1)S(1)}, bf16[1024,512]{1,0:T(8,128)(2,1)S(1)}, u32[]{:S(2)}, u32[]{:S(2)}) %collective-permute-start.65) | collective-permute-done | bytes 1048608 | tf_op jit(solution)/shard_map/ppermute | solution.py:79
  612.4 9.8 %collective-permute-done.68.refs_5_ = bf16[256,1536]{1,0:T(8,128)(2,1)S(1)} collective-permute-done((bf16[256,1536]{1,0:T(8,128)(2,1)S(1)}, bf16[256,1536]{1,0:T(8,128)(2,1)S(1)}, u32[]{:S(2)}, u32[]{:S(2)}) %collective-permute-start.68) | collective-permute-done | bytes 786464 | tf_op jit(solution)/shard_map/ppermute | solution.py:76
  (468 shorter events, 305.6 us)
Async XLA Ops:
  7.2 85.5 %all-gather.7.cloned.1.call-start = ((), (), s32[]{:S(2)}) async-start(), calls=%async_computation.4 | async-start | bytes 2359296 | tf_op jit(solution)/shard_map/all_gather | solution.py:82
  7.9 200.3 %all-gather.9.cloned.1.call-start = ((), (), s32[]{:S(2)}) async-start(), calls=%async_computation.5 | async-start | bytes 7864320 | tf_op jit(solution)/shard_map/all_gather | solution.py:108
  8.0 31.3 %collective-permute-start.2 = (bf16[1024,512]{1,0:T(8,128)(2,1)}, bf16[1024,512]{1,0:T(8,128)(2,1)}, u32[]{:S(2)}, u32[]{:S(2)}) collective-permute-start(bf16[1024,512]{1,0:T(8,128)(2,1)} %refs_0_), channel_id=1, source_target_pairs={{0,2},{1,3},{2,0},{3,1},{4,6},{5,7},{6,4},{7,5},{8,10},{9,11},{10,... | collective-permute-start | bytes 3145736 | tf_op jit(solution)/shard_map/ppermute | solution.py:140
  47.8 26.6 %collective-permute-start.11 = (bf16[256,1024]{1,0:T(8,128)(2,1)S(1)}, bf16[256,1024]{1,0:T(8,128)(2,1)S(1)}, u32[]{:S(2)}, u32[]{:S(2)}) collective-permute-start(bf16[256,1024]{1,0:T(8,128)(2,1)S(1)} %collective-permute-done.5.refs_11_.refs_7_), channel_id=1, source_target_pairs={{8,0},{16,8},{24,16},{28,24},{20,28},{12,20},{4,12},{0,4},{9,1},{1... | collective-permute-start | bytes 1572872 | tf_op jit(solution)/shard_map/ppermute | solution.py:76
  49.8 36.8 %collective-permute-start.14 = (bf16[256,1536]{1,0:T(8,128)(2,1)S(1)}, bf16[256,1536]{1,0:T(8,128)(2,1)S(1)}, u32[]{:S(2)}, u32[]{:S(2)}) collective-permute-start(bf16[256,1536]{1,0:T(8,128)(2,1)S(1)} %pad_maximum_fusion.12), channel_id=1, source_target_pairs={{0,4},{4,0},{8,12},{12,8},{16,20},{20,16},{24,28},{28,24},{1,5},{5... | collective-permute-start | bytes 2359304 | tf_op jit(solution)/shard_map/ppermute | solution.py:79
  92.7 179.4 %all-gather.11.cloned.1.call-start = ((), (), s32[]{:S(2)}) async-start(), calls=%async_computation.6 | async-start | bytes 3932160 | tf_op jit(solution)/shard_map/all_gather | solution.py:108
  96.5 32.8 %collective-permute-start.16 = (bf16[1024,512]{1,0:T(8,128)(2,1)S(1)}, bf16[1024,512]{1,0:T(8,128)(2,1)}, u32[]{:S(2)}, u32[]{:S(2)}) collective-permute-start(bf16[1024,512]{1,0:T(8,128)(2,1)S(1)} %copy-done.20), channel_id=1, source_target_pairs={{0,4},{4,0},{8,12},{12,8},{16,20},{20,16},{24,28},{28,24},{1,5},{5... | collective-permute-start | bytes 3145736 | tf_op jit(solution)/shard_map/ppermute | solution.py:79
  96.8 32.6 %collective-permute-start.15 = (bf16[1024,512]{1,0:T(8,128)(2,1)S(1)}, bf16[1024,512]{1,0:T(8,128)(2,1)S(1)}, u32[]{:S(2)}, u32[]{:S(2)}) collective-permute-start(bf16[1024,512]{1,0:T(8,128)(2,1)S(1)} %copy-done.20), channel_id=1, source_target_pairs={{0,2},{1,3},{2,0},{3,1},{4,6},{5,7},{6,4},{7,5},{8,10},{9,11},{10,... | collective-permute-start | bytes 3145736 | tf_op jit(solution)/shard_map/ppermute | solution.py:140
  99.4 29.9 %collective-permute-start.17 = (bf16[768,256]{1,0:T(8,128)(2,1)S(1)}, bf16[768,256]{1,0:T(8,128)(2,1)S(1)}, u32[]{:S(2)}, u32[]{:S(2)}) collective-permute-start(bf16[768,256]{1,0:T(8,128)(2,1)S(1)} %get-tuple-element.980), channel_id=1, source_target_pairs={{0,4},{4,0},{8,12},{12,8},{16,20},{20,16},{24,28},{28,24},{1,5},{5... | collective-permute-start | bytes 1179656 | tf_op jit(solution)/shard_map/ppermute | solution.py:79
  143.4 33.3 %collective-permute-start.22 = (bf16[512,512]{1,0:T(8,128)(2,1)S(1)}, bf16[512,512]{1,0:T(8,128)(2,1)S(1)}, u32[]{:S(2)}, u32[]{:S(2)}) collective-permute-start(bf16[512,512]{1,0:T(8,128)(2,1)S(1)} %slice.171), channel_id=1, source_target_pairs={{0,2},{1,3},{2,0},{3,1},{4,6},{5,7},{6,4},{7,5},{8,10},{9,11},{10,... | collective-permute-start | bytes 1572872 | tf_op jit(solution)/shard_map/ppermute | solution.py:140
  145.6 35.5 %collective-permute-start.25 = (bf16[1024,512]{1,0:T(8,128)(2,1)}, bf16[1024,512]{1,0:T(8,128)(2,1)}, u32[]{:S(2)}, u32[]{:S(2)}) collective-permute-start(bf16[1024,512]{1,0:T(8,128)(2,1)} %collective-permute-done.16.refs_0_), channel_id=1, source_target_pairs={{0,1},{1,0},{2,3},{3,2},{4,5},{5,4},{6,7},{7,6},{8,9},{9,8},{10,11... | collective-permute-start | bytes 3145736 | tf_op jit(solution)/shard_map/ppermute | solution.py:140
  208.2 132.7 %reduce-scatter.3.cloned.1.call-start = ((), (), s32[]{:S(2)}) async-start(), calls=%async_computation.2 | async-start | bytes 3932160 | tf_op jit(solution)/shard_map/reduce_scatter | solution.py:112
  259.1 187.1 %reduce-scatter.5.cloned.1.call-start = ((), (), s32[]{:S(2)}) async-start(), calls=%async_computation.3 | async-start | bytes 7864320 | tf_op jit(solution)/shard_map/reduce_scatter | solution.py:112
  358.4 38.0 %collective-permute-start.41 = (bf16[1024,512]{1,0:T(8,128)(2,1)}, bf16[1024,512]{1,0:T(8,128)(2,1)}, u32[]{:S(2)}, u32[]{:S(2)}) collective-permute-start(bf16[1024,512]{1,0:T(8,128)(2,1)} %pad_maximum_fusion.7), channel_id=1, source_target_pairs={{0,4},{4,0},{8,12},{12,8},{16,20},{20,16},{24,28},{28,24},{1,5},{5... | collective-permute-start | bytes 3145736 | tf_op jit(solution)/shard_map/ppermute | solution.py:79
  368.3 28.1 %collective-permute-start.42 = (bf16[1024,512]{1,0:T(8,128)(2,1)}, bf16[1024,512]{1,0:T(8,128)(2,1)}, u32[]{:S(2)}, u32[]{:S(2)}) collective-permute-start(bf16[1024,512]{1,0:T(8,128)(2,1)} %pad_maximum_fusion.8), channel_id=1, source_target_pairs={{0,2},{1,3},{2,0},{3,1},{4,6},{5,7},{6,4},{7,5},{8,10},{9,11},{10,... | collective-permute-start | bytes 3145736 | tf_op jit(solution)/shard_map/ppermute | solution.py:140
  447.5 30.7 %collective-permute-start.49 = (bf16[256,1536]{1,0:T(8,128)(2,1)S(1)}, bf16[256,1536]{1,0:T(8,128)(2,1)S(1)}, u32[]{:S(2)}, u32[]{:S(2)}) collective-permute-start(bf16[256,1536]{1,0:T(8,128)(2,1)S(1)} %slice.187), channel_id=1, source_target_pairs={{0,4},{4,0},{8,12},{12,8},{16,20},{20,16},{24,28},{28,24},{1,5},{5... | collective-permute-start | bytes 2359304 | tf_op jit(solution)/shard_map/ppermute | solution.py:79
  450.3 27.8 %collective-permute-start.51 = (bf16[512,512]{1,0:T(8,128)(2,1)S(1)}, bf16[512,512]{1,0:T(8,128)(2,1)S(1)}, u32[]{:S(2)}, u32[]{:S(2)}) collective-permute-start(bf16[512,512]{1,0:T(8,128)(2,1)S(1)} %get-tuple-element.971), channel_id=1, source_target_pairs={{0,4},{4,0},{8,12},{12,8},{16,20},{20,16},{24,28},{28,24},{1,5},{5... | collective-permute-start | bytes 1572872 | tf_op jit(solution)/shard_map/ppermute | solution.py:79
  450.9 27.2 %collective-permute-start.50 = (bf16[512,512]{1,0:T(8,128)(2,1)S(1)}, bf16[512,512]{1,0:T(8,128)(2,1)S(1)}, u32[]{:S(2)}, u32[]{:S(2)}) collective-permute-start(bf16[512,512]{1,0:T(8,128)(2,1)S(1)} %get-tuple-element.972), channel_id=1, source_target_pairs={{0,2},{1,3},{2,0},{3,1},{4,6},{5,7},{6,4},{7,5},{8,10},{9,11},{10,... | collective-permute-start | bytes 1572872 | tf_op jit(solution)/shard_map/ppermute | solution.py:140
  499.2 27.3 %collective-permute-start.54 = (bf16[1024,1024]{1,0:T(8,128)(2,1)}, bf16[1024,1024]{1,0:T(8,128)(2,1)}, u32[]{:S(2)}, u32[]{:S(2)}) collective-permute-start(bf16[1024,1024]{1,0:T(8,128)(2,1)} %get-tuple-element.820), channel_id=1, source_target_pairs={{0,1},{1,0},{2,3},{3,2},{4,5},{5,4},{6,7},{7,6},{8,9},{9,8},{10,11... | collective-permute-start | bytes 6291464 | tf_op jit(solution)/shard_map/ppermute | solution.py:140
  533.8 37.8 %collective-permute-start.59 = (bf16[1024,512]{1,0:T(8,128)(2,1)}, bf16[1024,512]{1,0:T(8,128)(2,1)}, u32[]{:S(2)}, u32[]{:S(2)}) collective-permute-start(bf16[1024,512]{1,0:T(8,128)(2,1)} %slice.278), channel_id=1, source_target_pairs={{0,2},{1,3},{2,0},{3,1},{4,6},{5,7},{6,4},{7,5},{8,10},{9,11},{10,... | collective-permute-start | bytes 3145736 | tf_op jit(solution)/shard_map/ppermute | solution.py:140
  568.3 42.3 %collective-permute-start.65 = (bf16[1024,512]{1,0:T(8,128)(2,1)S(1)}, bf16[1024,512]{1,0:T(8,128)(2,1)S(1)}, u32[]{:S(2)}, u32[]{:S(2)}) collective-permute-start(bf16[1024,512]{1,0:T(8,128)(2,1)S(1)} %copy-done.81), channel_id=1, source_target_pairs={{0,4},{4,0},{8,12},{12,8},{16,20},{20,16},{24,28},{28,24},{1,5},{5... | collective-permute-start | bytes 3145736 | tf_op jit(solution)/shard_map/ppermute | solution.py:79
  570.1 40.5 %collective-permute-start.66 = (bf16[1024,512]{1,0:T(8,128)(2,1)S(1)}, bf16[1024,512]{1,0:T(8,128)(2,1)S(1)}, u32[]{:S(2)}, u32[]{:S(2)}) collective-permute-start(bf16[1024,512]{1,0:T(8,128)(2,1)S(1)} %copy-done.80), channel_id=1, source_target_pairs={{0,2},{1,3},{2,0},{3,1},{4,6},{5,7},{6,4},{7,5},{8,10},{9,11},{10,... | collective-permute-start | bytes 3145736 | tf_op jit(solution)/shard_map/ppermute | solution.py:140
  591.8 30.4 %collective-permute-start.68 = (bf16[256,1536]{1,0:T(8,128)(2,1)S(1)}, bf16[256,1536]{1,0:T(8,128)(2,1)S(1)}, u32[]{:S(2)}, u32[]{:S(2)}) collective-permute-start(bf16[256,1536]{1,0:T(8,128)(2,1)S(1)} %shard_map.298), channel_id=1, source_target_pairs={{8,0},{16,8},{24,16},{28,24},{20,28},{12,20},{4,12},{0,4},{9,1},{1... | collective-permute-start | bytes 2359304 | tf_op jit(solution)/shard_map/ppermute | solution.py:76
  591.8 32.7 %collective-permute-start.67 = (bf16[256,1536]{1,0:T(8,128)(2,1)S(1)}, bf16[256,1536]{1,0:T(8,128)(2,1)S(1)}, u32[]{:S(2)}, u32[]{:S(2)}) collective-permute-start(bf16[256,1536]{1,0:T(8,128)(2,1)S(1)} %shard_map.297), channel_id=1, source_target_pairs={{0,8},{8,16},{16,24},{24,28},{28,20},{20,12},{12,4},{4,0},{1,9},{9... | collective-permute-start | bytes 2359304 | tf_op jit(solution)/shard_map/ppermute | solution.py:73
  (150 other events, 1308.8 us)
Sparse Core Ops, SparseCore 0:
  10.1 64.5 all-gather.6
  92.8 115.3 all-gather.8
  210.3 61.7 all-gather.10
  274.3 58.8 reduce-scatter.2
  337.1 108.9 reduce-scatter.4

commit v4 on v3

--- a/solution.py
+++ b/solution.py
@@ -453,35 +453,25 @@
     )[0]
 
 
-def block_grad(lefts, rights, number, count, extras):
+def block_grads(lefts, rights, order, count):
     tokens, full = lefts[0].shape
     rows = full // count
     widths = [right.shape[1] for right in rights]
-    many, more = len(lefts), len(extras)
+    many, steps = len(lefts), order.shape[0]
 
     def body(_, *refs):
-        out_ref = refs[-1]
         start = 0
         for c, width in enumerate(widths):
-            at = slice(start, start + width)
-            total = dot_tn(refs[c][...], refs[many + c][...])
-            for e, (value, first) in enumerate(extras):
-                got = refs[2 * many + e][:, at].astype(jnp.float32)
-                if value.shape[0] == rows:
-                    total = total + got
-                elif first == 0:
-                    total = jnp.concatenate([total[: value.shape[0]] + got, total[value.shape[0] :]], 0)
-                else:
-                    total = jnp.concatenate([total[:first], total[first:] + got], 0)
-            out_ref[:, at] = total.astype(jnp.bfloat16)
+            refs[-1][0, :, start : start + width] = dot_tn(refs[c][...], refs[many + c][...]).astype(jnp.bfloat16)
             start += width
 
-    outs = (shape_of((rows, sum(widths)), jnp.bfloat16),)
-    operands = (*lefts, *rights, *(value for value, _ in extras))
-    specs = [pl.BlockSpec((tokens, rows), lambda *_: (0, number))] * many + [whole_spec(a) for a in operands[many:]]
+    outs = (shape_of((steps, rows, sum(widths)), jnp.bfloat16),)
+    operands = (*lefts, *rights)
+    specs = [pl.BlockSpec((tokens, rows), lambda i, order_ref: (0, order_ref[i]))] * many
+    specs += [whole_spec(a) for a in operands[many:]]
     return kernel_call(
-        body, jnp.zeros((1,), jnp.int32), operands, specs, outs, (whole_spec(outs[0]),), (1,), [],
-        2 * tokens * rows * sum(widths), 32,
+        body, order, operands, specs, outs, (pl.BlockSpec((1, rows, sum(widths)), lambda i, *_: (i, 0, 0)),), (steps,), [],
+        2 * tokens * steps * rows * sum(widths), 60,
     )[0]
 
 
@@ -763,37 +753,31 @@
     both_other = pin(keep_other).astype(f32) + got_other
     both_other, corner = pin(both_other, both_other[:, part_width:].astype(low))
     from_far, from_partner = far(corner[:half]), ring.to_partner(corner[half:])
-    gate_up_grad, from_far, from_partner = run(
-        lambda *ops: weight_grad(ops[:2], ops[2:], pair_order, True),
-        normed,
-        normed_other,
-        low_mine,
-        low_other,
-        beside=(from_far, from_partner),
-    )
-    to_partner = jnp.concatenate([both_other[:half, :part_width] + from_far, both_other[half:, :part_width]], 0)
-    to_partner, down_grad = pin(to_partner.astype(low), down_grad)
-    gate_up_grad = pair_sum(ring, gate_up_grad)
-    to_partner = ring.to_partner(to_partner)
-    keep, send, inner = run(spread_back, low_mine, gate_up_all, normed)
+    keep, send, inner, from_far, from_partner = run(
+        spread_back, low_mine, gate_up_all, normed, beside=(from_far, from_partner)
+    )
     got = near(send)
     inner = pin(inner[:, 0] + inner_other)
     inner_near = near(inner)
-    keep, got, inner_near = pin(keep, got, inner_near)
+    to_partner = jnp.concatenate([both_other[:half, :part_width] + from_far, both_other[half:, :part_width]], 0)
+    keep, got, inner_near, to_partner = pin(keep, got, inner_near, to_partner.astype(low))
+    to_partner = ring.to_partner(to_partner)
     both = keep.astype(f32) + got
     to_far = jnp.concatenate([both[:half, part_width:], both[half:, part_width:] + from_partner], 0)
     own, to_far, inner = pin(both[:, :part_width], to_far.astype(low), inner + inner_near)
     inner_far = far(inner)
     from_far = far(to_far)
-    cut = down_grad.shape[1] // 2
-    down_got = ring.to_partner(pin(down_grad[:, cut:]))
+    gate_up_grad = run(
+        lambda *ops: weight_grad(ops[:2], ops[2:], pair_order, True), normed, normed_other, low_mine, low_other
+    )
+    own, from_partner, from_far, inner_far, down_grad, gate_up_grad = pin(
+        own, to_partner, from_far, inner_far, down_grad, gate_up_grad
+    )
+    gate_up_grad = pair_sum(ring, gate_up_grad)
 
     def spread_down(left, weights):
         return spread_product(pair_place, left, [weights], False)
 
-    out_keep_other, out_send_other = run(spread_down, hidden_other, down_all)
-    out_keep, out_send, inner_far = run(spread_down, hidden, down_all, beside=(inner_far,))
-    own, from_partner, from_far = pin(own, to_partner, from_far)
     grad_normed = own + from_partner + from_far
     inner = (inner + inner_far)[:, None] / full_width
     grad_middle = (
@@ -803,113 +787,101 @@
     )
     grad_middle, grad_low = pin(grad_middle, grad_middle.astype(low))
     grad_far, grad_near = far(grad_low), near(grad_low)
+    down_got = ring.to_partner(pin(down_grad[:, down_grad.shape[1] // 2 :]))
+    out_keep_other, out_send_other = run(spread_down, hidden_other, down_all)
+    out_keep, out_send, grad_near, down_got = run(spread_down, hidden, down_all, beside=(grad_near, down_got))
+    grad_far = pin(grad_far)
+    grad_diagonal = near(grad_far)
     out_got_other, out_got = near(out_send_other), near(out_send)
-    out_got_other, out_got, out_keep_other = pin(out_got_other, out_got, out_keep_other)
-    both_other = out_keep_other.astype(f32) + out_got_other
-    both_other, corner = pin(both_other, both_other[:, part_width:].astype(low))
-    grad_far, grad_near, down_got = pin(grad_far, grad_near, down_got)
-    grad_diagonal = pin(near(grad_far))
+    out_got_other, out_got, out_keep_other, grad_diagonal = pin(out_got_other, out_got, out_keep_other, grad_diagonal)
+    out_other = pin((out_keep_other.astype(f32) + out_got_other).astype(low))
+    out_partner = ring.to_partner(out_other)
+    ffwd_gain = pin(jnp.sum(grad_normed * middle * factor_two, 0))
 
     middle_wide = run(lambda *blocks: assemble(place, blocks), grad_low, grad_far, grad_near, grad_diagonal)
     grad_mixed = run(lambda wide, weights: times_transposed(wide, [weights], ring.behind), middle_wide, output_all)
-    gate_up_grad = pin(gate_up_grad)
-    columns_here = gate_up_grad.shape[0] // 2
-    gate_up_got = ring.to_partner(pin(gate_up_grad[columns_here:]))
-    out_far, out_partner = far(corner[:half]), ring.to_partner(corner[half:])
-    query_low, key_low, value_low, head_gains, gate_up_got, out_far, out_partner = run(
-        lambda *ops: attend_back(*ops, *turning, MOST, EPS),
-        qkv_raw,
-        turned_q,
-        turned_k,
-        values,
-        grad_mixed,
-        beside=(gate_up_got, out_far, out_partner),
+    query_low, key_low, value_low, head_gains = run(
+        lambda *ops: attend_back(*ops, *turning, MOST, EPS), qkv_raw, turned_q, turned_k, values, grad_mixed
     )
     qkv_low = pin(jnp.concatenate([query_low, key_low, value_low], 1))
 
-    def part(j, extras):
-        ops = (wide_one, middle_wide, qkv_low, mixed, *(value for value, _ in extras))
+    def parts(*numbers, beside=()):
+        order = jnp.array(numbers, jnp.int32)
         return run(
-            lambda *ops: block_grad(ops[:2], ops[2:4], j, ring.count, list(zip(ops[4:], (r for _, r in extras), strict=True))), *ops
+            lambda *ops: block_grads(ops[:2], ops[2:], order, ring.count), wide_one, middle_wide, qkv_low, mixed, beside=beside
         )
 
-    first = part(ring.half, [])
+    def go(on, back, *beside):
+        on, back, *beside = pin(on.astype(low), back.astype(low), *beside)
+        return ring.send_on(on), ring.send_back(back), *beside
+
+    first = parts(steps)[0]
     cut = first.shape[0] // 2
-    on, back = ring.send_on(first[:cut]), ring.send_back(first[cut:])
-    keep, send, inner, attn_gain, on, back = run(
-        lambda left, weights, wide: spread_product(place, left, weights, True, wide, True),
-        qkv_low,
-        qkv_all,
-        wide_one,
-        beside=(on, back),
+    on, back = go(first[:cut], first[cut:])
+    own, on, back = parts(steps + 1, steps - 1, beside=(on, back))
+    on = jnp.concatenate([own[0, :cut] + on.astype(f32), own[0, cut:].astype(f32)], 0)
+    back = jnp.concatenate([own[1, :cut].astype(f32), own[1, cut:] + back.astype(f32)], 0)
+    on, back = go(on, back)
+    keep, send, inner, attn_gain = run(
+        lambda left, weights, wide: spread_product(place, left, weights, True, wide, True), qkv_low, qkv_all, wide_one
     )
     got = near(send)
+    own, out_partner, got = parts(
+        *(n for s in range(2, steps) for n in (steps + s, steps - s)), 0, beside=(out_partner, got)
+    )
     gain_keep, gain_send = attn_gain[:1, : full_width // 2], attn_gain[:1, full_width // 2 :]
     head_gains = jnp.sum(head_gains.reshape(-1, 8, head_size), 0)[:2].reshape(-1)
     sums = pin(jnp.concatenate([gain_send[0], head_gains, inner[:, 0]]))
-    sums_got = near(sums)
-    on = part(ring.half + 1, [(on, 0)])
-    back, got, sums_got = run(
-        lambda *ops: block_grad(ops[:2], ops[2:4], ring.half - 1, ring.count, [(ops[4], cut)]),
-        wide_one,
-        middle_wide,
-        qkv_low,
-        mixed,
-        back,
-        beside=(got, sums_got),
-    )
-    on, back = ring.send_on(on), ring.send_back(back)
+    sums_got, keep, gate_up_grad = pin(near(sums), keep, gate_up_grad)
+    both = keep.astype(f32) + got
     both_gain = gain_keep[0] + sums_got[: full_width // 2]
     sums = jnp.concatenate([both_gain[part_width:], (sums + sums_got)[full_width // 2 :]])
-    sums = pin(sums)
+    both, to_far, sums = pin(both, both[:, part_width:].astype(low), sums)
     sums_got = far(sums)
-    both = keep.astype(f32) + got
-    both, to_far, sums_got = pin(both, both[:, part_width:].astype(low), sums_got)
     grad_far = far(to_far)
-    to_partner = jnp.concatenate([both_other[:half, :part_width] + out_far, both_other[half:, :part_width]], 0)
-    out_both = out_keep.astype(f32) + out_got
-    to_far = jnp.concatenate([out_both[:half, part_width:], out_both[half:, part_width:] + out_partner], 0)
+    columns_here = gate_up_grad.shape[0] // 2
+    gate_up_got = ring.to_partner(pin(gate_up_grad[columns_here:]))
+    on, back = pin(on, back)
+    on, back, sums_got = go(own[0] + on.astype(f32), own[1] + back.astype(f32), sums_got)
     attn_gain = (both_gain[:part_width] + sums_got[:part_width]) / attn_norm
     rest = (sums + sums_got)[part_width:]
     inner = rest[2 * head_size :][:, None] / full_width
-    ffwd_gain = jnp.sum(grad_normed * middle * factor_two, 0)
     sums = jnp.concatenate([attn_gain, ffwd_gain, rest[: 2 * head_size]])
-    out_own, to_partner, to_far, sums, on, back = pin(
-        out_both[:, :part_width], to_partner.astype(low), to_far.astype(low), sums, on, back
-    )
-    on, back = part(ring.half + 2, [(on, 0)]), part(ring.half - 2, [(back, 0)])
-    on, back = ring.send_on(on), ring.send_back(back)
+    sums, grad_far, out_keep, out_got = pin(sums, grad_far, out_keep, out_got)
     bit, rows = 1, lax.axis_size("row")
     sums_got = swap(sums, "row", bit)
-    grad_far, sums_got = pin(grad_far, sums_got)
-    out_partner, out_far = ring.to_partner(to_partner), far(to_far)
+    out_both = out_keep.astype(f32) + out_got + out_partner
+    out_own, to_far = pin(out_both[:, :part_width], out_both[:, part_width:].astype(low))
+    out_far = far(to_far)
     hidden_grad = (
         grad_middle
         + factor_one * attn_norm * (both[:, :part_width] + grad_far)
         - residual * (factor_one * factor_one * inner)
     )
-    sums, hidden_grad = pin(sums + sums_got, hidden_grad)
+    hidden_grad, on, back, sums_got = pin(hidden_grad, on, back, sums_got)
+    on, back, gate_up_grad, gate_up_got, down_got = go(
+        own[2] + on.astype(f32), own[3] + back.astype(f32), gate_up_grad, gate_up_got, down_got
+    )
+    sums = pin(sums + sums_got)
+    bit *= 2
+    sums_got = swap(sums, "row", bit)
     gate_grad, up_grad = (
         pair_join(ring, gate_up_grad[:columns_here, at], gate_up_got[:, at], 1)
         for at in (slice(0, gate_up_grad.shape[1] // 2), slice(gate_up_grad.shape[1] // 2, None))
     )
-    gate_grad, up_grad = pin(gate_grad, up_grad)
-    bit *= 2
-    sums_got = swap(sums, "row", bit)
-    on, back, sums_got = pin(on, back, sums_got)
-    on, back = part(ring.half + 3, [(on, 0)]), part(ring.half - 3, [(back, 0)])
-    on, back = ring.send_on(on), ring.send_back(back)
+    down_out = pair_join(ring, down_grad[:, : down_grad.shape[1] // 2], down_got, 0)
+    gate_grad, up_grad, down_out, sums_got = pin(gate_grad, up_grad, down_out, sums_got)
     sums = pin(sums + sums_got)
     bit *= 2
     while bit < rows:
-        sums = pin(sums + swap(sums, "row", bit))
+        sums_got = swap(sums, "row", bit)
         bit *= 2
-    out_partner, out_far = pin(out_partner, out_far)
-    hidden_out = pin((middle + out_own + out_partner + out_far).astype(low))
-    down_cut = down_grad.shape[1] // 2
-    down_out = pin(pair_join(ring, down_grad[:, :down_cut], down_got, 0))
-    on, back = pin(on, back)
-    total = ring.inner_sum(part(0, [(on, 0), (back, 0)]).astype(f32), 0)
+        if bit < rows:
+            sums = pin(sums + sums_got)
+    on, back, sums_got, out_far = pin(on, back, sums_got, out_far)
+    sums = sums + sums_got
+    total = ring.inner_sum(own[4].astype(f32) + on + back, 0)
+    hidden_out = (middle + out_own + out_far).astype(low)
     attn_gain, ffwd_gain, query_gain, key_gain = jnp.split(
         sums, [part_width, 2 * part_width, 2 * part_width + head_size]
     )

time: 642 us -> 596 us (0.928)
  local copies, waits for them, and re-layouts: 70.9 us -> 41.9 us
  waiting for transfers between devices: 222 us -> 206 us
    unnamed x203 -> x161, local copies, waits for them, and re-layouts: 41.5 us -> 18.4 us
    ppermute x13 -> x12, waiting for transfers between devices: 37.7 us -> 14.7 us  [to_partner(): return lax.ppermute(value, 'row', self.partner)]
    ppermute x40 -> x39, waiting for transfers between devices: 80.4 us -> 94.6 us  [swap(): lax.ppermute(value, axis, [(i, i ^ bit) for i in range(lax.axis_size(axis...]
    convert_element_type x2 -> x4, other arithmetic: 1.93 us -> 11.9 us  [the longest x1 4.63 us: local(): out_other = pin((out_keep_other.astype(f32) + out_got_other).astype(low))]
    reduce_scatter x2, waiting for transfers between devices: 6.73 us -> 0.01 us  [pair_sum(): lax.psum_scatter(units, 'row', scatter_dimension=0, axis_index_groups=rin...]
    pallas_call x27 -> x22, Pallas kernels: 207 us -> 211 us  [kernel_call(): pl.pallas_call(body, grid_spec=pltpu.PrefetchScalarGridSpec(num_scalar_pr...]
    ppermute x13 -> x12, starting transfers between devices: 14.3 us -> 12.1 us  [to_partner(): return lax.ppermute(value, 'row', self.partner)]
    ppermute x40 -> x39, starting transfers between devices: 28.2 us -> 26.7 us  [swap(): lax.ppermute(value, axis, [(i, i ^ bit) for i in range(lax.axis_size(axis...]
  transfers between devices with their start and end apart: 74 -> 72, of which waited for: 38 -> 32; matrix products, arithmetic and copies ran while one was open for 14% -> 13% of each run, Pallas kernels for 32% -> 32%
where the time goes in v4:
time: 596 us; the launch traced here: 590 us
  Pallas kernels  211 us (35%)
  waiting for transfers between devices  206 us (35%)
  other arithmetic  59.7 us (10%)
  starting transfers between devices  56.4 us (9%)
  local copies, waits for them, and re-layouts  41.9 us (7%)
  between operations  15.6 us (3%)
    pallas_call x22, Pallas kernels, kernel_call(): pl.pallas_call(body, grid_spec=pltpu.PrefetchScalarGridSpec(num_scalar_pr...  211 us
    ppermute x39, waiting for transfers between devices, swap(): lax.ppermute(value, axis, [(i, i ^ bit) for i in range(lax.axis_size(axis...  94.6 us
    ppermute x8, waiting for transfers between devices, send_on(): return lax.ppermute(value, 'row', self.onward)  47.4 us
    ppermute x8, waiting for transfers between devices, send_back(): return lax.ppermute(value, 'row', self.backward)  33 us
    ppermute x39, starting transfers between devices, swap(): lax.ppermute(value, axis, [(i, i ^ bit) for i in range(lax.axis_size(axis...  26.7 us
    unnamed x161, local copies, waits for them, and re-layouts  18.4 us
    all_gather x2, waiting for transfers between devices, pair_gather(): return lax.all_gather(unit, 'row', axis=0, axis_index_groups=ring.pairs)  15.7 us
    ppermute x12, waiting for transfers between devices, to_partner(): return lax.ppermute(value, 'row', self.partner)  14.7 us
  transfers between devices with their start and end apart: 72, of which 32 were waited for; matrix products, arithmetic and copies ran while one was open for 13% of the time, Pallas kernels for 32%

profile of v4, /device:TPU:0, one launch (start us, length us, event | category | flops | bytes accessed | tf_op | source)
XLA Modules:
  0.0 590.2 jit_solution(10965351411557605639)
XLA Ops:
  14.2 14.2 %collective-permute-done.1.refs_12_.refs_8_ = bf16[256,1024]{1,0:T(8,128)(2,1)S(1)} collective-permute-done((bf16[256,1024]{1,0:T(8,128)(2,1)S(1)}, bf16[256,1024]{1,0:T(8,128)(2,1)S(1)}, u32[]{:S(2)}, u32[]{:S(2)}) %collective-permute-start.1) | collective-permute-done | bytes 524320 | tf_op jit(solution)/shard_map/ppermute | solution.py:76
  53.1 16.8 %collective-permute-done.10.refs_8_.refs_4_ = bf16[256,1024]{1,0:T(8,128)(2,1)S(1)} collective-permute-done((bf16[256,1024]{1,0:T(8,128)(2,1)S(1)}, bf16[256,1024]{1,0:T(8,128)(2,1)S(1)}, u32[]{:S(2)}, u32[]{:S(2)}) %collective-permute-start.10) | collective-permute-done | bytes 524320 | tf_op jit(solution)/shard_map/ppermute | solution.py:73
  77.2 9.5 %collective-permute-done.14 = bf16[256,1536]{1,0:T(8,128)(2,1)S(1)} collective-permute-done((bf16[256,1536]{1,0:T(8,128)(2,1)S(1)}, bf16[256,1536]{1,0:T(8,128)(2,1)S(1)}, u32[]{:S(2)}, u32[]{:S(2)}) %collective-permute-start.14) | collective-permute-done | bytes 786464 | tf_op jit(solution)/shard_map/ppermute | solution.py:79
  101.8 11.5 %shard_map.300 = (bf16[1024,2048]{1,0:T(8,128)(2,1)}, f32[1024,1]{1,0:T(8,128)S(1)}, f32[1024,1024]{1,0:T(8,128)}) custom-call(s32[8]{0:T(128)S(1)} %get-tuple-element.940.place_ref, bf16[1024,512]{1,0:T(8,128)(2,1)S(1)} %copy-done.6, bf16[1024,512]{1,0:T(8,128)(2,1)} %collective-permute-done.2.refs_1_, bf16[1024,512]{1,0:T(8,128)(2,1)} %collective-permute-done.8.refs_2_, ...), custom_call_target="tpu_custom_call" | custom-call | flops 85899344 | bytes 65536 | tf_op jit(solution)/shard_map/pallas_call | solution.py:164
  114.1 13.8 %shard_map.301 = (bf16[1024,512]{1,0:T(8,128)(2,1)S(1)}, bf16[1024,256]{1,0:T(8,128)(2,1)S(1)}, bf16[1024,256]{1,0:T(8,128)(2,1)S(1)}, bf16[1024,512]{1,0:T(8,128)(2,1)S(1)}) custom-call(s32[1]{0:T(128)} %constant.75.clone.1._.order_ref, f32[1024,1024]{1,0:T(8,128)} %get-tuple-element.722.q_ref.k_ref.v_ref, ...), custom_call_target="tpu_custom_call" | custom-call | flops 120795952 | bytes 65536 | tf_op jit(solution)/shard_map/pallas_call | solution.py:164
  148.3 19.1 %collective-permute-done.21 = bf16[1024,512]{1,0:T(8,128)(2,1)S(1)} collective-permute-done((bf16[1024,512]{1,0:T(8,128)(2,1)S(1)}, bf16[1024,512]{1,0:T(8,128)(2,1)S(1)}, u32[]{:S(2)}, u32[]{:S(2)}) %collective-permute-start.21) | collective-permute-done | bytes 1048608 | tf_op jit(solution)/shard_map/ppermute | solution.py:140
  169.4 8.5 %collective-permute-done.22 = bf16[512,512]{1,0:T(8,128)(2,1)S(1)} collective-permute-done((bf16[512,512]{1,0:T(8,128)(2,1)S(1)}, bf16[512,512]{1,0:T(8,128)(2,1)S(1)}, u32[]{:S(2)}, u32[]{:S(2)}) %collective-permute-start.22) | collective-permute-done | bytes 524320 | tf_op jit(solution)/shard_map/ppermute | solution.py:140
  189.6 15.0 %collective-permute-done.27.refs_1_ = bf16[1024,512]{1,0:T(8,128)(2,1)} collective-permute-done((bf16[1024,512]{1,0:T(8,128)(2,1)S(1)}, bf16[1024,512]{1,0:T(8,128)(2,1)}, u32[]{:S(2)}, u32[]{:S(2)}) %collective-permute-start.27) | collective-permute-done | bytes 1048608 | tf_op jit(solution)/shard_map/ppermute | solution.py:140
  214.0 14.9 %shard_map.305 = (bf16[1024,2048]{1,0:T(8,128)(2,1)}, f32[1024,1]{1,0:T(8,128)S(1)}, f32[1024,768]{1,0:T(8,128)}, f32[1024,768]{1,0:T(8,128)}, bf16[1024,768]{1,0:T(8,128)(2,1)}) custom-call(s32[8]{0:T(128)S(1)} %fusion.13.place_ref, bf16[1024,512]{1,0:T(8,128)(2,1)S(1)} %get-tuple-element.553.refs_0_, bf16[1024,512]{1,0:T(8,128)(2,1)} %collective-permute-done.27.refs_1_, ...), custom_call_target="tpu_custom_call" | custom-call | flops 128849016 | bytes 65536 | tf_op jit(solution)/shard_map/pallas_call | solution.py:164
  232.3 14.2 %shard_map.306 = (bf16[1024,2048]{1,0:T(8,128)(2,1)}, f32[1024,1]{1,0:T(8,128)}, f32[1024,768]{1,0:T(8,128)}, f32[1024,768]{1,0:T(8,128)}, bf16[1024,768]{1,0:T(8,128)(2,1)}) custom-call(s32[8]{0:T(128)S(1)} %fusion.13.place_ref, bf16[1024,512]{1,0:T(8,128)(2,1)} %collective-permute-done.28.refs_0_, bf16[1024,512]{1,0:T(8,128)(2,1)S(1)} %pad_maximum_fusion.6.refs_1_, ...), custom_call_target="tpu_custom_call" | custom-call | flops 128849016 | bytes 65536 | tf_op jit(solution)/shard_map/pallas_call | solution.py:164
  247.0 11.5 %shard_map.307 = bf16[4,768,512]{2,1,0:T(8,128)(2,1)} custom-call(s32[4]{0:T(128)} %iota.28._, bf16[1024,768]{1,0:T(8,128)(2,1)} %get-tuple-element.687.refs_0_, bf16[1024,768]{1,0:T(8,128)(2,1)} %get-tuple-element.681.refs_1_.refs_0_, bf16[1024,2048]{1,0:T(8,128)(2,1)} %copy-done.1, bf16[1024,2048]{1,0:T(8,128)(2,1)} %copy-done.2), custom_call_target="tpu_custom_call" | custom-call | flops 128849016 | bytes 65536 | tf_op jit(solution)/shard_map/pallas_call | solution.py:164
  258.6 13.5 %all-gather.11.cloned.1.call-done = bf16[3072,512]{1,0:T(8,128)(2,1)} async-done(((bf16[768,512]{1,0:T(8,128)(2,1)}), bf16[3072,512]{1,0:T(8,128)(2,1)}) %all-gather.11.cloned.1.call-update) | async-done | bytes 3145744 | tf_op jit(solution)/shard_map/all_gather | solution.py:108
  281.9 12.9 %shard_map.309 = (bf16[1024,1024]{1,0:T(8,128)(2,1)S(1)}, bf16[1024,1024]{1,0:T(8,128)(2,1)}, f32[1024,1]{1,0:T(8,128)S(1)}) custom-call(s32[8]{0:T(128)S(1)} %fusion.13.place_ref, bf16[1024,1536]{1,0:T(8,128)(2,1)} %copy-done.3, bf16[4,512,1536]{2,1,0:T(8,128)(2,1)} %bitcast.88, bf16[1024,2048]{1,0:T(8,128)(2,1)} %get-tuple-element.661.refs_2_.refs_1_), custom_call_target="tpu_custom_call" | custom-call | flops 128849016 | bytes 65536 | tf_op jit(solution)/shard_map/pallas_call | solution.py:164
  312.6 12.9 %shard_map.311 = (bf16[1024,1024]{1,0:T(8,128)(2,1)S(1)}, bf16[1024,1024]{1,0:T(8,128)(2,1)}, f32[1024,1]{1,0:T(8,128)S(1)}) custom-call(s32[8]{0:T(128)S(1)} %fusion.13.place_ref, bf16[1024,1536]{1,0:T(8,128)(2,1)} %copy-done.4, bf16[4,512,1536]{2,1,0:T(8,128)(2,1)} %bitcast.89, bf16[1024,2048]{1,0:T(8,128)(2,1)} %get-tuple-element.660.refs_2_.refs_0_), custom_call_target="tpu_custom_call" | custom-call | flops 128849016 | bytes 65536 | tf_op jit(solution)/shard_map/pallas_call | solution.py:164
  340.6 19.3 %shard_map.312 = bf16[4,512,1536]{2,1,0:T(8,128)(2,1)} custom-call(s32[4]{0:T(128)} %iota.29._, bf16[1024,2048]{1,0:T(8,128)(2,1)} %get-tuple-element.660.refs_2_.refs_0_, bf16[1024,2048]{1,0:T(8,128)(2,1)} %get-tuple-element.661.refs_2_.refs_1_, bf16[1024,1536]{1,0:T(8,128)(2,1)} %copy-done.4, bf16[1024,1536]{1,0:T(8,128)(2,1)} %copy-done.3), custom_call_target="tpu_custom_call" | custom-call | flops 257698032 | bytes 65536 | tf_op jit(solution)/shard_map/pallas_call | solution.py:164
  388.2 9.5 %collective-permute-done.45.refs_1_ = bf16[1024,512]{1,0:T(8,128)(2,1)S(1)} collective-permute-done((bf16[1024,512]{1,0:T(8,128)(2,1)S(1)}, bf16[1024,512]{1,0:T(8,128)(2,1)S(1)}, u32[]{:S(2)}, u32[]{:S(2)}) %collective-permute-start.45) | collective-permute-done | bytes 1048608 | tf_op jit(solution)/shard_map/ppermute | solution.py:140
  415.3 19.7 %shard_map.317 = (bf16[1024,512]{1,0:T(8,128)(2,1)S(1)}, bf16[1024,256]{1,0:T(8,128)(2,1)S(1)}, bf16[1024,256]{1,0:T(8,128)(2,1)S(1)}, f32[16,128]{1,0:T(8,128)S(1)}) custom-call(s32[1]{0:T(128)} %constant.75.clone.1._.order_ref, f32[1024,1024]{1,0:T(8,128)} %get-tuple-element.722.q_ref.k_ref.v_ref, f32[1024,1024]{1,0:T(8,128)} %get-tuple-element.722.q_ref.k_ref.v_ref, ...), custom_call_target="tpu_custom_call" | custom-call | flops 169114336 | bytes 65536 | tf_op jit(solution)/shard_map/pallas_call | solution.py:164
  450.8 8.9 %collective-permute-done.49 = bf16[128,1536]{1,0:T(8,128)(2,1)S(1)} collective-permute-done((bf16[128,1536]{1,0:T(8,128)(2,1)S(1)}, bf16[128,1536]{1,0:T(8,128)(2,1)S(1)}, u32[]{:S(2)}, u32[]{:S(2)}) %collective-permute-start.49) | collective-permute-done | bytes 393248 | tf_op jit(solution)/shard_map/ppermute | solution.py:73
  459.7 10.9 %collective-permute-done.50 = bf16[128,1536]{1,0:T(8,128)(2,1)S(1)} collective-permute-done((bf16[128,1536]{1,0:T(8,128)(2,1)S(1)}, bf16[128,1536]{1,0:T(8,128)(2,1)S(1)}, u32[]{:S(2)}, u32[]{:S(2)}) %collective-permute-start.50) | collective-permute-done | bytes 393248 | tf_op jit(solution)/shard_map/ppermute | solution.py:76
  474.5 9.3 %shard_map.320 = (bf16[1024,1024]{1,0:T(8,128)(2,1)}, bf16[1024,1024]{1,0:T(8,128)(2,1)}, f32[1024,1]{1,0:T(8,128)S(1)}, f32[8,2048]{1,0:T(8,128)S(1)}) custom-call(s32[8]{0:T(128)S(1)} %get-tuple-element.940.place_ref, bf16[1024,1024]{1,0:T(8,128)(2,1)} %pad_maximum_fusion.refs_2_.refs_0_, bf16[256,1024]{1,0:T(8,128)(2,1)S(1)} %copy-done.11, ...), custom_call_target="tpu_custom_call" | custom-call | flops 85899344 | bytes 65536 | tf_op jit(solution)/shard_map/pallas_call | solution.py:164
  484.1 10.0 %shard_map.321 = bf16[5,256,1536]{2,1,0:T(8,128)(2,1)} custom-call(s32[5]{0:T(128)} %constant.86.clone._, bf16[1024,2048]{1,0:T(8,128)(2,1)} %get-tuple-element.775.refs_0_.refs_9_, bf16[1024,2048]{1,0:T(8,128)(2,1)} %copy-done, bf16[1024,1024]{1,0:T(8,128)(2,1)} %pad_maximum_fusion.refs_2_.refs_0_, bf16[1024,512]{1,0:T(8,128)(2,1)} %copy-done.5), custom_call_target="tpu_custom_call" | custom-call | flops 80530640 | bytes 65536 | tf_op jit(solution)/shard_map/pallas_call | solution.py:164
  505.9 12.4 %collective-permute-done.54 = bf16[256,1536]{1,0:T(8,128)(2,1)} collective-permute-done((bf16[256,1536]{1,0:T(8,128)(2,1)}, bf16[256,1536]{1,0:T(8,128)(2,1)}, u32[]{:S(2)}, u32[]{:S(2)}) %collective-permute-start.54) | collective-permute-done | bytes 786464 | tf_op jit(solution)/shard_map/ppermute | solution.py:73
  530.1 14.9 %collective-permute-done.57 = bf16[1024,512]{1,0:T(8,128)(2,1)} collective-permute-done((bf16[1024,512]{1,0:T(8,128)(2,1)}, bf16[1024,512]{1,0:T(8,128)(2,1)}, u32[]{:S(2)}, u32[]{:S(2)}) %collective-permute-start.57) | collective-permute-done | bytes 1048608 | tf_op jit(solution)/shard_map/ppermute | solution.py:140
  566.2 9.4 %collective-permute-done.65 = f32[1280]{0:T(1024)S(1)} collective-permute-done((f32[1280]{0:T(1024)S(1)}, f32[1280]{0:T(1024)S(1)}, u32[]{:S(2)}, u32[]{:S(2)}) %collective-permute-start.65) | collective-permute-done | bytes 5152 | tf_op jit(solution)/shard_map/ppermute | solution.py:140
  (414 shorter events, 262.0 us)
Async XLA Ops:
  7.2 85.5 %all-gather.7.cloned.1.call-start = ((), (), s32[]{:S(2)}) async-start(), calls=%async_computation.4 | async-start | bytes 2359296 | tf_op jit(solution)/shard_map/all_gather | solution.py:82
  7.9 200.2 %all-gather.9.cloned.1.call-start = ((), (), s32[]{:S(2)}) async-start(), calls=%async_computation.5 | async-start | bytes 7864320 | tf_op jit(solution)/shard_map/all_gather | solution.py:108
  8.0 29.7 %collective-permute-start.2 = (bf16[1024,512]{1,0:T(8,128)(2,1)}, bf16[1024,512]{1,0:T(8,128)(2,1)}, u32[]{:S(2)}, u32[]{:S(2)}) collective-permute-start(bf16[1024,512]{1,0:T(8,128)(2,1)} %refs_0_), channel_id=1, source_target_pairs={{0,2},{1,3},{2,0},{3,1},{4,6},{5,7},{6,4},{7,5},{8,10},{9,11},{10,... | collective-permute-start | bytes 3145736 | tf_op jit(solution)/shard_map/ppermute | solution.py:140
  47.5 26.8 %collective-permute-start.11 = (bf16[256,1024]{1,0:T(8,128)(2,1)S(1)}, bf16[256,1024]{1,0:T(8,128)(2,1)S(1)}, u32[]{:S(2)}, u32[]{:S(2)}) collective-permute-start(bf16[256,1024]{1,0:T(8,128)(2,1)S(1)} %collective-permute-done.5.refs_11_.refs_7_), channel_id=1, source_target_pairs={{8,0},{16,8},{24,16},{28,24},{20,28},{12,20},{4,12},{0,4},{9,1},{1... | collective-permute-start | bytes 1572872 | tf_op jit(solution)/shard_map/ppermute | solution.py:76
  49.8 36.8 %collective-permute-start.14 = (bf16[256,1536]{1,0:T(8,128)(2,1)S(1)}, bf16[256,1536]{1,0:T(8,128)(2,1)S(1)}, u32[]{:S(2)}, u32[]{:S(2)}) collective-permute-start(bf16[256,1536]{1,0:T(8,128)(2,1)S(1)} %pad_maximum_fusion.10), channel_id=1, source_target_pairs={{0,4},{4,0},{8,12},{12,8},{16,20},{20,16},{24,28},{28,24},{1,5},{5... | collective-permute-start | bytes 2359304 | tf_op jit(solution)/shard_map/ppermute | solution.py:79
  92.7 179.3 %all-gather.11.cloned.1.call-start = ((), (), s32[]{:S(2)}) async-start(), calls=%async_computation.6 | async-start | bytes 3932160 | tf_op jit(solution)/shard_map/all_gather | solution.py:108
  96.5 34.0 %collective-permute-start.16 = (bf16[1024,512]{1,0:T(8,128)(2,1)S(1)}, bf16[1024,512]{1,0:T(8,128)(2,1)}, u32[]{:S(2)}, u32[]{:S(2)}) collective-permute-start(bf16[1024,512]{1,0:T(8,128)(2,1)S(1)} %copy-done.14), channel_id=1, source_target_pairs={{0,4},{4,0},{8,12},{12,8},{16,20},{20,16},{24,28},{28,24},{1,5},{5... | collective-permute-start | bytes 3145736 | tf_op jit(solution)/shard_map/ppermute | solution.py:79
  96.8 33.7 %collective-permute-start.15 = (bf16[1024,512]{1,0:T(8,128)(2,1)S(1)}, bf16[1024,512]{1,0:T(8,128)(2,1)S(1)}, u32[]{:S(2)}, u32[]{:S(2)}) collective-permute-start(bf16[1024,512]{1,0:T(8,128)(2,1)S(1)} %copy-done.14), channel_id=1, source_target_pairs={{0,2},{1,3},{2,0},{3,1},{4,6},{5,7},{6,4},{7,5},{8,10},{9,11},{10,... | collective-permute-start | bytes 3145736 | tf_op jit(solution)/shard_map/ppermute | solution.py:140
  99.5 31.0 %collective-permute-start.17 = (bf16[768,256]{1,0:T(8,128)(2,1)S(1)}, bf16[768,256]{1,0:T(8,128)(2,1)S(1)}, u32[]{:S(2)}, u32[]{:S(2)}) collective-permute-start(bf16[768,256]{1,0:T(8,128)(2,1)S(1)} %get-tuple-element.920), channel_id=1, source_target_pairs={{0,4},{4,0},{8,12},{12,8},{16,20},{20,16},{24,28},{28,24},{1,5},{5... | collective-permute-start | bytes 1179656 | tf_op jit(solution)/shard_map/ppermute | solution.py:79
  141.4 26.1 %collective-permute-start.21 = (bf16[1024,512]{1,0:T(8,128)(2,1)S(1)}, bf16[1024,512]{1,0:T(8,128)(2,1)S(1)}, u32[]{:S(2)}, u32[]{:S(2)}) collective-permute-start(bf16[1024,512]{1,0:T(8,128)(2,1)S(1)} %slice.301), channel_id=1, source_target_pairs={{0,2},{1,3},{2,0},{3,1},{4,6},{5,7},{6,4},{7,5},{8,10},{9,11},{10,... | collective-permute-start | bytes 3145736 | tf_op jit(solution)/shard_map/ppermute | solution.py:140
  144.1 25.2 %collective-permute-start.23 = (bf16[512,512]{1,0:T(8,128)(2,1)S(1)}, bf16[512,512]{1,0:T(8,128)(2,1)S(1)}, u32[]{:S(2)}, u32[]{:S(2)}) collective-permute-start(bf16[512,512]{1,0:T(8,128)(2,1)S(1)} %slice.186), channel_id=1, source_target_pairs={{0,4},{4,0},{8,12},{12,8},{16,20},{20,16},{24,28},{28,24},{1,5},{5... | collective-permute-start | bytes 1572872 | tf_op jit(solution)/shard_map/ppermute | solution.py:79
  144.4 33.5 %collective-permute-start.22 = (bf16[512,512]{1,0:T(8,128)(2,1)S(1)}, bf16[512,512]{1,0:T(8,128)(2,1)S(1)}, u32[]{:S(2)}, u32[]{:S(2)}) collective-permute-start(bf16[512,512]{1,0:T(8,128)(2,1)S(1)} %slice.184), channel_id=1, source_target_pairs={{0,2},{1,3},{2,0},{3,1},{4,6},{5,7},{6,4},{7,5},{8,10},{9,11},{10,... | collective-permute-start | bytes 1572872 | tf_op jit(solution)/shard_map/ppermute | solution.py:140
  146.9 35.3 %collective-permute-start.25 = (bf16[1024,512]{1,0:T(8,128)(2,1)}, bf16[1024,512]{1,0:T(8,128)(2,1)}, u32[]{:S(2)}, u32[]{:S(2)}) collective-permute-start(bf16[1024,512]{1,0:T(8,128)(2,1)} %collective-permute-done.16.refs_0_), channel_id=1, source_target_pairs={{0,1},{1,0},{2,3},{3,2},{4,5},{5,4},{6,7},{7,6},{8,9},{9,8},{10,11... | collective-permute-start | bytes 3145736 | tf_op jit(solution)/shard_map/ppermute | solution.py:140
  179.4 25.2 %collective-permute-start.27 = (bf16[1024,512]{1,0:T(8,128)(2,1)S(1)}, bf16[1024,512]{1,0:T(8,128)(2,1)}, u32[]{:S(2)}, u32[]{:S(2)}) collective-permute-start(bf16[1024,512]{1,0:T(8,128)(2,1)S(1)} %get-tuple-element.553.refs_0_), channel_id=1, source_target_pairs={{0,2},{1,3},{2,0},{3,1},{4,6},{5,7},{6,4},{7,5},{8,10},{9,11},{10,... | collective-permute-start | bytes 3145736 | tf_op jit(solution)/shard_map/ppermute | solution.py:140
  208.1 151.8 %reduce-scatter.3.cloned.1.call-start = ((), (), s32[]{:S(2)}) async-start(), calls=%async_computation.2 | async-start | bytes 3932160 | tf_op jit(solution)/shard_map/reduce_scatter | solution.py:112
  296.2 203.8 %reduce-scatter.5.cloned.1.call-start = ((), (), s32[]{:S(2)}) async-start(), calls=%async_computation.3 | async-start | bytes 7864320 | tf_op jit(solution)/shard_map/reduce_scatter | solution.py:112
  336.3 26.8 %collective-permute-start.40 = (bf16[1024,512]{1,0:T(8,128)(2,1)}, bf16[1024,512]{1,0:T(8,128)(2,1)}, u32[]{:S(2)}, u32[]{:S(2)}) collective-permute-start(bf16[1024,512]{1,0:T(8,128)(2,1)} %pad_maximum_fusion.7), channel_id=1, source_target_pairs={{0,4},{4,0},{8,12},{12,8},{16,20},{20,16},{24,28},{28,24},{1,5},{5... | collective-permute-start | bytes 3145736 | tf_op jit(solution)/shard_map/ppermute | solution.py:79
  338.0 25.1 %collective-permute-start.41 = (bf16[1024,512]{1,0:T(8,128)(2,1)S(1)}, bf16[1024,512]{1,0:T(8,128)(2,1)}, u32[]{:S(2)}, u32[]{:S(2)}) collective-permute-start(bf16[1024,512]{1,0:T(8,128)(2,1)S(1)} %pad_maximum_fusion.8), channel_id=1, source_target_pairs={{0,2},{1,3},{2,0},{3,1},{4,6},{5,7},{6,4},{7,5},{8,10},{9,11},{10,... | collective-permute-start | bytes 3145736 | tf_op jit(solution)/shard_map/ppermute | solution.py:140
  372.4 25.3 %collective-permute-start.45 = (bf16[1024,512]{1,0:T(8,128)(2,1)S(1)}, bf16[1024,512]{1,0:T(8,128)(2,1)S(1)}, u32[]{:S(2)}, u32[]{:S(2)}) collective-permute-start(bf16[1024,512]{1,0:T(8,128)(2,1)S(1)} %get-tuple-element.707.refs_0_), channel_id=1, source_target_pairs={{0,2},{1,3},{2,0},{3,1},{4,6},{5,7},{6,4},{7,5},{8,10},{9,11},{10,... | collective-permute-start | bytes 3145736 | tf_op jit(solution)/shard_map/ppermute | solution.py:140
  441.9 28.6 %collective-permute-start.50 = (bf16[128,1536]{1,0:T(8,128)(2,1)S(1)}, bf16[128,1536]{1,0:T(8,128)(2,1)S(1)}, u32[]{:S(2)}, u32[]{:S(2)}) collective-permute-start(bf16[128,1536]{1,0:T(8,128)(2,1)S(1)} %get-tuple-element.752), channel_id=1, source_target_pairs={{8,0},{16,8},{24,16},{28,24},{20,28},{12,20},{4,12},{0,4},{9,1},{1... | collective-permute-start | bytes 1179656 | tf_op jit(solution)/shard_map/ppermute | solution.py:76
  443.9 54.1 %collective-permute-start.51 = (bf16[1024,1024]{1,0:T(8,128)(2,1)}, bf16[1024,1024]{1,0:T(8,128)(2,1)}, u32[]{:S(2)}, u32[]{:S(2)}) collective-permute-start(bf16[1024,1024]{1,0:T(8,128)(2,1)} %add_convert_fusion), channel_id=1, source_target_pairs={{0,4},{4,0},{8,12},{12,8},{16,20},{20,16},{24,28},{28,24},{1,5},{5... | collective-permute-start | bytes 6291464 | tf_op jit(solution)/shard_map/ppermute | solution.py:79
  518.7 37.4 %collective-permute-start.61 = (bf16[256,1536]{1,0:T(8,128)(2,1)}, bf16[256,1536]{1,0:T(8,128)(2,1)}, u32[]{:S(2)}, u32[]{:S(2)}) collective-permute-start(bf16[256,1536]{1,0:T(8,128)(2,1)} %slice.214), channel_id=1, source_target_pairs={{0,4},{4,0},{8,12},{12,8},{16,20},{20,16},{24,28},{28,24},{1,5},{5... | collective-permute-start | bytes 2359304 | tf_op jit(solution)/shard_map/ppermute | solution.py:79
  526.5 29.1 %collective-permute-start.58 = (bf16[256,1536]{1,0:T(8,128)(2,1)}, bf16[256,1536]{1,0:T(8,128)(2,1)S(1)}, u32[]{:S(2)}, u32[]{:S(2)}) collective-permute-start(bf16[256,1536]{1,0:T(8,128)(2,1)} %get-tuple-element.819), channel_id=1, source_target_pairs={{0,8},{8,16},{16,24},{24,28},{28,20},{20,12},{12,4},{4,0},{1,9},{9... | collective-permute-start | bytes 2359304 | tf_op jit(solution)/shard_map/ppermute | solution.py:73
  528.2 27.4 %collective-permute-start.59 = (bf16[256,1536]{1,0:T(8,128)(2,1)}, bf16[256,1536]{1,0:T(8,128)(2,1)S(1)}, u32[]{:S(2)}, u32[]{:S(2)}) collective-permute-start(bf16[256,1536]{1,0:T(8,128)(2,1)} %get-tuple-element.820), channel_id=1, source_target_pairs={{8,0},{16,8},{24,16},{28,24},{20,28},{12,20},{4,12},{0,4},{9,1},{1... | collective-permute-start | bytes 2359304 | tf_op jit(solution)/shard_map/ppermute | solution.py:76
  (126 other events, 1283.9 us)
Sparse Core Ops, SparseCore 0:
  10.1 64.9 all-gather.6
  92.8 115.2 all-gather.8
  210.3 61.7 all-gather.10
  296.4 59.0 reduce-scatter.2
  363.3 116.3 reduce-scatter.4

commit v5 on v4

--- a/solution.py
+++ b/solution.py
@@ -317,13 +317,13 @@
     def body(place_ref, *refs):
         y_ref, w_refs = refs[0], units_of(refs[1 : 1 + many])
         rest = refs[1 + many + len(extras) :]
-        keep_ref, send_ref, all_ref = rest[0], rest[1], rest[-1]
+        part_refs, all_ref = rest[:cols], rest[-1]
         rows = jnp.zeros((tile, 1), jnp.float32)
         if by_feature:
 
             @pl.when(pl.program_id(0) == 0)
             def _():
-                rest[3][...] = jnp.zeros_like(rest[3])
+                rest[cols + 1][...] = jnp.zeros_like(rest[cols + 1])
 
         for j in range(count):
             total = dot(y_ref[...], w_refs[j][...])
@@ -334,17 +334,18 @@
                     sums = jnp.broadcast_to(jnp.sum(weighted, 0, keepdims=True), (8, unit))
                     for i in range(per_unit):
                         at = piece_at(place_ref, j * per_unit + i, piece)
-                        rest[3][:, at] += sums[:, i * piece : (i + 1) * piece]
+                        rest[cols + 1][:, at] += sums[:, i * piece : (i + 1) * piece]
             total = total.astype(jnp.bfloat16)
             for i in range(per_unit):
                 at = piece_at(place_ref, j * per_unit + i, piece)
                 all_ref[:, at] = total[:, i * piece : (i + 1) * piece]
-        keep_ref[...] = all_ref[:, : full // 2]
-        send_ref[...] = all_ref[:, full // 2 :]
+        for c, ref in enumerate(part_refs):
+            ref[...] = all_ref[:, c * (full // cols) : (c + 1) * (full // cols)]
         if extras:
-            rest[2][...] = rows
-
-    outs = (shape_of((tokens, full // 2), jnp.bfloat16),) * 2
+            rest[cols][...] = rows
+
+    cols = len(COL_ORDER)
+    outs = (shape_of((tokens, full // cols), jnp.bfloat16),) * cols
     if extras:
         outs += (shape_of((tokens, 1), jnp.float32),)
     operands = (left, *weights, *extras)
@@ -352,7 +353,7 @@
     out_specs = tuple(rows_spec(o, tile) for o in outs)
     if by_feature:
         outs += (shape_of((8, full), jnp.float32),)
-        out_specs += (whole_spec(outs[3]),)
+        out_specs += (whole_spec(outs[cols + 1]),)
     scratch = [pltpu.VMEM((tile, full), jnp.bfloat16)]
     return kernel_call(
         body, place, operands, specs, outs, out_specs, (tokens // tile,), scratch, 2 * tokens * full * inner, 48
@@ -382,14 +383,15 @@
 
 
 def times_transposed(wide, weights, order):
-    return back_product(wide, weights, (), lambda total: (total,), order)
+    return back_product(wide, weights, (), lambda total: (total,), order)[0]
 
 
 def swish_back(wide, weights, gate, up):
     def gradients(total, gate_value, up_value):
         sigma = 1.0 / (1.0 + jnp.exp(-gate_value))
         grad_gate = total * up_value * sigma * (1.0 + gate_value * (1.0 - sigma))
-        return grad_gate, total * gate_value * sigma
+        grad_up = total * gate_value * sigma
+        return grad_gate, grad_up, jnp.sum(grad_gate * gate_value + grad_up * up_value, 1, keepdims=True)
 
     return back_product(wide, weights, (gate, up), gradients)
 
@@ -406,7 +408,7 @@
 
     def body(order_ref, *refs):
         wide_ref, extra_refs = refs[0], refs[1 : 1 + others]
-        w_refs, out_ref = refs[1 + others : -1], refs[-1]
+        w_refs, out_ref = refs[1 + others : 1 + others + units], refs[1 + others + units]
         if not stacked:
             w_refs = units_of(w_refs)
         else:
@@ -414,17 +416,22 @@
         total = dot_nt(wide_ref[:, :unit], w_refs[0][...])
         for j in range(1, count):
             total = total + dot_nt(wide_ref[:, j * unit : (j + 1) * unit], w_refs[j][...])
-        for i, part in enumerate(epilogue(total, *(e[...] for e in extra_refs))):
+        results = epilogue(total, *(e[...] for e in extra_refs))
+        for i, part in enumerate(results[:parts]):
             out_ref[:, i * columns : (i + 1) * columns] = part.astype(jnp.bfloat16)
+        for ref, value in zip(refs[2 + others + units :], results[parts:], strict=True):
+            ref[...] = value
 
     outs = (shape_of((tokens, parts * columns), jnp.bfloat16),)
+    if extras:
+        outs += (shape_of((tokens, 1), jnp.float32),)
     operands = (wide, *extras, *weights)
     specs = [rows_spec(b, tile) for b in (wide, *extras)] + [whole_spec(w) for w in weights]
     order = order if stacked else jnp.zeros((1,), jnp.int32)
     return kernel_call(
-        body, order, operands, specs, outs, (rows_spec(outs[0], tile),), (tokens // tile,), [],
+        body, order, operands, specs, outs, tuple(rows_spec(o, tile) for o in outs), (tokens // tile,), [],
         2 * tokens * full * columns, 48,
-    )[0]
+    )
 
 
 def weight_grad(lefts, rights, order, by_left):
@@ -640,7 +647,7 @@
     def far(value):
         return swap(value, "col", 2)
 
-    qkv = pin(jnp.concatenate([w_query, key_weight, value_weight], 1))
+    qkv, hidden_in = pin(jnp.concatenate([w_query, key_weight, value_weight], 1), hidden_in)
     qkv = ring.inner_gather(qkv, 0)
     on, back = ring.send_on(qkv), ring.send_back(qkv)
     output_all = ring.gather_stack(ring.inner_gather(w_output, 1))
@@ -663,6 +670,8 @@
     gate_up_mine = side_of(gate_up, 1, ring.parity)
     gate_up_got = ring.to_partner(side_of(gate_up, 1, 1 - ring.parity))
     gains_diagonal, gate_up_mine, *hidden_blocks = pin(near(gains_far), gate_up_mine, *hidden_blocks)
+    position = tables(seq_lengths[0], tokens)[:, None]
+    position, cos_wide, sin_wide, behind_order = pin(position, *rotary(position[:, 0], head_size), ring.behind)
     on, back = pin(on, back)
     behind.append(on)
     ahead.append(back)
@@ -679,9 +688,7 @@
     down_mine = side_of(down, 0, ring.parity)
     down_got = ring.to_partner(side_of(down, 0, 1 - ring.parity))
     up_far, up_partner = far(upstream), ring.to_partner(upstream)
-    position = tables(seq_lengths[0], tokens)
-    cos_wide, sin_wide = rotary(position, head_size)
-    turning = (position[:, None], cos_wide, sin_wide, query_norm[None, :], key_norm[None, :])
+    turning = (position, cos_wide, sin_wide, query_norm[None, :], key_norm[None, :])
     residual = hidden_in.astype(f32)
     wide_one, factor_one, qkv_raw = run(
         lambda blocks, gain, weights: gather_norm_matmul(place, blocks, gain, weights, EPS), hidden_blocks, gains[0], qkv_all
@@ -690,18 +697,19 @@
         lambda raw: attend(raw, *turning, q_width, k_width, MOST, EPS), qkv_raw
     )
     up_far, up_partner, down_got, down_mine = pin(up_far, up_partner, down_got, down_mine)
-    keep, send = run(lambda left, weights: spread_product(plain_place, left, [weights], False), mixed, output_all)
-    got = near(send)
+    own, to_far, to_near, to_diagonal = run(
+        lambda left, weights: spread_product(plain_place, left, [weights], False), mixed, output_all
+    )
+    got_far, got_own = near(to_diagonal), near(to_near)
     up_near, up_diagonal = near(upstream), near(up_far)
-    keep, got = pin(keep, got)
-    both = keep.astype(f32) + got
-    attended = far(pin(both[:, part_width:].astype(low)))
+    to_far, got_far = pin(to_far, got_far)
+    attended = far(pin((to_far.astype(f32) + got_far).astype(low)))
     corner = far(pin(up_partner[:half])), ring.to_partner(up_far[half:])
     up_near, up_diagonal = pin(up_near, up_diagonal)
     upstream_wide = run(lambda *blocks: assemble(pair_place, blocks), upstream, up_far, up_near, up_diagonal)
-    attended, both = pin(attended, both)
-
-    middle = residual + both[:, :part_width] + attended
+    attended, own, got_own = pin(attended, own, got_own)
+
+    middle = residual + own + got_own + attended
     middle, middle_low = pin(middle, middle.astype(low))
     mid_far, mid_partner = far(middle_low), ring.to_partner(middle_low)
     mid_near = near(middle_low)
@@ -741,45 +749,46 @@
     def back_swish(wide, weights, gate_value, up_value):
         return swish_back(wide, [weights], gate_value, up_value)
 
-    def spread_back(left, weights, normed_rows):
-        return spread_product(pair_place, left, [weights], True, normed_rows)
-
-    low_other = run(back_swish, upstream_other, down_all, gate_other, up_other)
-    keep_other, send_other, inner_other = run(spread_back, low_other, gate_up_all, normed_other)
-    got_other, inner_other = near(send_other), ring.to_partner(pin(inner_other[:, 0]))
-    low_mine, got_other, inner_other = run(
-        back_swish, upstream_wide, down_all, gate, up, beside=(got_other, inner_other)
-    )
-    both_other = pin(keep_other).astype(f32) + got_other
-    both_other, corner = pin(both_other, both_other[:, part_width:].astype(low))
+    def spread_back(left, weights):
+        return spread_product(pair_place, left, [weights], True)
+
+    low_other, inner_other = run(back_swish, upstream_other, down_all, gate_other, up_other)
+    own_other, far_other, near_other, diagonal_other = run(spread_back, low_other, gate_up_all)
+    diagonal_other, near_other, inner_other = near(diagonal_other), near(near_other), ring.to_partner(pin(inner_other[:, 0]))
+    low_mine, inner, diagonal_other, near_other, inner_other = run(
+        back_swish, upstream_wide, down_all, gate, up, beside=(diagonal_other, near_other, inner_other)
+    )
+    corner = pin((pin(far_other).astype(f32) + diagonal_other).astype(low))
     from_far, from_partner = far(corner[:half]), ring.to_partner(corner[half:])
-    keep, send, inner, from_far, from_partner = run(
-        spread_back, low_mine, gate_up_all, normed, beside=(from_far, from_partner)
-    )
-    got = near(send)
     inner = pin(inner[:, 0] + inner_other)
     inner_near = near(inner)
-    to_partner = jnp.concatenate([both_other[:half, :part_width] + from_far, both_other[half:, :part_width]], 0)
-    keep, got, inner_near, to_partner = pin(keep, got, inner_near, to_partner.astype(low))
+    own, to_far, to_near, to_diagonal, from_far, from_partner, inner_near = run(
+        spread_back, low_mine, gate_up_all, beside=(from_far, from_partner, inner_near)
+    )
+    got_far, got_own = near(to_diagonal), near(to_near)
+    inner = pin(inner + inner_near)
+    inner_far = far(inner)
+    to_partner = own_other.astype(f32) + near_other
+    to_partner = jnp.concatenate([to_partner[:half] + from_far, to_partner[half:]], 0)
+    to_far, got_far, to_partner = pin(to_far, got_far, to_partner.astype(low))
     to_partner = ring.to_partner(to_partner)
-    both = keep.astype(f32) + got
-    to_far = jnp.concatenate([both[:half, part_width:], both[half:, part_width:] + from_partner], 0)
-    own, to_far, inner = pin(both[:, :part_width], to_far.astype(low), inner + inner_near)
-    inner_far = far(inner)
+    to_far = to_far.astype(f32) + got_far
+    to_far = jnp.concatenate([to_far[:half], to_far[half:] + from_partner], 0)
+    own, got_own, to_far, inner_far = pin(own, got_own, to_far.astype(low), inner_far)
     from_far = far(to_far)
     gate_up_grad = run(
         lambda *ops: weight_grad(ops[:2], ops[2:], pair_order, True), normed, normed_other, low_mine, low_other
     )
-    own, from_partner, from_far, inner_far, down_grad, gate_up_grad = pin(
-        own, to_partner, from_far, inner_far, down_grad, gate_up_grad
+    inner = (inner + inner_far)[:, None] / full_width
+    own, got_own, from_partner, from_far, inner, down_grad, gate_up_grad = pin(
+        own, got_own, to_partner, from_far, inner, down_grad, gate_up_grad
     )
     gate_up_grad = pair_sum(ring, gate_up_grad)
 
     def spread_down(left, weights):
         return spread_product(pair_place, left, [weights], False)
 
-    grad_normed = own + from_partner + from_far
-    inner = (inner + inner_far)[:, None] / full_width
+    grad_normed = own.astype(f32) + got_own + from_partner + from_far
     grad_middle = (
         cotangent.astype(f32)
         + factor_two * ffwd_norm * grad_normed
@@ -788,21 +797,35 @@
     grad_middle, grad_low = pin(grad_middle, grad_middle.astype(low))
     grad_far, grad_near = far(grad_low), near(grad_low)
     down_got = ring.to_partner(pin(down_grad[:, down_grad.shape[1] // 2 :]))
-    out_keep_other, out_send_other = run(spread_down, hidden_other, down_all)
-    out_keep, out_send, grad_near, down_got = run(spread_down, hidden, down_all, beside=(grad_near, down_got))
+    own_other, far_other, near_other, diagonal_other = run(spread_down, hidden_other, down_all)
+    out_own, out_to_far, out_to_near, out_to_diagonal, grad_near, down_got = run(
+        spread_down, hidden, down_all, beside=(grad_near, down_got)
+    )
+    near_other, diagonal_other = near(near_other), near(diagonal_other)
     grad_far = pin(grad_far)
     grad_diagonal = near(grad_far)
-    out_got_other, out_got = near(out_send_other), near(out_send)
-    out_got_other, out_got, out_keep_other, grad_diagonal = pin(out_got_other, out_got, out_keep_other, grad_diagonal)
-    out_other = pin((out_keep_other.astype(f32) + out_got_other).astype(low))
-    out_partner = ring.to_partner(out_other)
+    near_other, diagonal_other, grad_diagonal, own_other, far_other = pin(
+        near_other, diagonal_other, grad_diagonal, own_other, far_other
+    )
+    out_first, out_second = pin(
+        (own_other.astype(f32) + near_other).astype(low), (far_other.astype(f32) + diagonal_other).astype(low)
+    )
+    out_first = ring.to_partner(out_first)
+    out_got_own, out_got_far = near(out_to_near), near(out_to_diagonal)
     ffwd_gain = pin(jnp.sum(grad_normed * middle * factor_two, 0))
 
     middle_wide = run(lambda *blocks: assemble(place, blocks), grad_low, grad_far, grad_near, grad_diagonal)
-    grad_mixed = run(lambda wide, weights: times_transposed(wide, [weights], ring.behind), middle_wide, output_all)
-    query_low, key_low, value_low, head_gains = run(
-        lambda *ops: attend_back(*ops, *turning, MOST, EPS), qkv_raw, turned_q, turned_k, values, grad_mixed
-    )
+    grad_mixed = run(lambda wide, weights: times_transposed(wide, [weights], behind_order), middle_wide, output_all)
+    query_low, key_low, value_low, head_gains, out_first, out_got_own, out_got_far = run(
+        lambda *ops: attend_back(*ops, *turning, MOST, EPS),
+        qkv_raw,
+        turned_q,
+        turned_k,
+        values,
+        grad_mixed,
+        beside=(out_first, out_got_own, out_got_far),
+    )
+    out_second = ring.to_partner(out_second)
     qkv_low = pin(jnp.concatenate([query_low, key_low, value_low], 1))
 
     def parts(*numbers, beside=()):
@@ -815,73 +838,70 @@
         on, back, *beside = pin(on.astype(low), back.astype(low), *beside)
         return ring.send_on(on), ring.send_back(back), *beside
 
-    first = parts(steps)[0]
-    cut = first.shape[0] // 2
-    on, back = go(first[:cut], first[cut:])
-    own, on, back = parts(steps + 1, steps - 1, beside=(on, back))
-    on = jnp.concatenate([own[0, :cut] + on.astype(f32), own[0, cut:].astype(f32)], 0)
-    back = jnp.concatenate([own[1, :cut].astype(f32), own[1, cut:] + back.astype(f32)], 0)
-    on, back = go(on, back)
-    keep, send, inner, attn_gain = run(
+    first = parts(steps)
+    cut = first.shape[1] // 2
+    on, back = go(first[0, :cut], first[0, cut:])
+    own_first, to_far, to_near, to_diagonal, inner, attn_gain = run(
         lambda left, weights, wide: spread_product(place, left, weights, True, wide, True), qkv_low, qkv_all, wide_one
     )
-    got = near(send)
-    own, out_partner, got = parts(
-        *(n for s in range(2, steps) for n in (steps + s, steps - s)), 0, beside=(out_partner, got)
-    )
+    got_far, got_own = near(to_diagonal), near(to_near)
+    second = parts(steps + 1, steps - 1)
+    own, on, back, out_second, gate_up_grad = parts(
+        *(n for s in range(2, steps) for n in (steps + s, steps - s)), 0, beside=(on, back, out_second, gate_up_grad)
+    )
+    on = jnp.concatenate([second[0, :cut] + on.astype(f32), second[0, cut:].astype(f32)], 0)
+    back = jnp.concatenate([second[1, :cut].astype(f32), second[1, cut:] + back.astype(f32)], 0)
+    on, back, got_far, got_own, to_far = go(on, back, got_far, got_own, to_far)
+    to_far = pin((to_far.astype(f32) + got_far).astype(low))
     gain_keep, gain_send = attn_gain[:1, : full_width // 2], attn_gain[:1, full_width // 2 :]
     head_gains = jnp.sum(head_gains.reshape(-1, 8, head_size), 0)[:2].reshape(-1)
     sums = pin(jnp.concatenate([gain_send[0], head_gains, inner[:, 0]]))
-    sums_got, keep, gate_up_grad = pin(near(sums), keep, gate_up_grad)
-    both = keep.astype(f32) + got
+    sums_got = pin(near(sums))
     both_gain = gain_keep[0] + sums_got[: full_width // 2]
-    sums = jnp.concatenate([both_gain[part_width:], (sums + sums_got)[full_width // 2 :]])
-    both, to_far, sums = pin(both, both[:, part_width:].astype(low), sums)
+    sums = pin(jnp.concatenate([both_gain[part_width:], (sums + sums_got)[full_width // 2 :]]))
     sums_got = far(sums)
     grad_far = far(to_far)
-    columns_here = gate_up_grad.shape[0] // 2
-    gate_up_got = ring.to_partner(pin(gate_up_grad[columns_here:]))
-    on, back = pin(on, back)
-    on, back, sums_got = go(own[0] + on.astype(f32), own[1] + back.astype(f32), sums_got)
+    sums_got, out_to_far = pin(sums_got, out_to_far)
     attn_gain = (both_gain[:part_width] + sums_got[:part_width]) / attn_norm
     rest = (sums + sums_got)[part_width:]
     inner = rest[2 * head_size :][:, None] / full_width
     sums = jnp.concatenate([attn_gain, ffwd_gain, rest[: 2 * head_size]])
-    sums, grad_far, out_keep, out_got = pin(sums, grad_far, out_keep, out_got)
-    bit, rows = 1, lax.axis_size("row")
-    sums_got = swap(sums, "row", bit)
-    out_both = out_keep.astype(f32) + out_got + out_partner
-    out_own, to_far = pin(out_both[:, :part_width], out_both[:, part_width:].astype(low))
-    out_far = far(to_far)
+    sums, inner = pin(sums, inner)
+    bits = [1 << n for n in range(lax.axis_size("row").bit_length() - 1)]
+    sums_got = swap(sums, "row", bits[0])
+    on, back, sums_got = pin(on, back, sums_got)
+    on, back = go(own[0] + on.astype(f32), own[1] + back.astype(f32))
+    sums = pin(sums + sums_got)
+    sums_got = swap(sums, "row", bits[1])
+    columns_here = gate_up_grad.shape[0] // 2
+    gate_up_got = ring.to_partner(pin(gate_up_grad[columns_here:]))
+    grad_far = pin(grad_far)
+    to_far = (out_to_far.astype(f32) + out_got_far + out_second).astype(low)
     hidden_grad = (
         grad_middle
-        + factor_one * attn_norm * (both[:, :part_width] + grad_far)
+        + factor_one * attn_norm * (own_first.astype(f32) + got_own + grad_far)
         - residual * (factor_one * factor_one * inner)
     )
-    hidden_grad, on, back, sums_got = pin(hidden_grad, on, back, sums_got)
-    on, back, gate_up_grad, gate_up_got, down_got = go(
-        own[2] + on.astype(f32), own[3] + back.astype(f32), gate_up_grad, gate_up_got, down_got
-    )
+    hidden_grad, to_far = pin(hidden_grad, to_far)
+    out_far = far(to_far)
+    on, back, sums_got = pin(on, back, sums_got)
+    on, back = go(own[2] + on.astype(f32), own[3] + back.astype(f32))
     sums = pin(sums + sums_got)
-    bit *= 2
-    sums_got = swap(sums, "row", bit)
+    for bit in bits[2:-1]:
+        sums = pin(sums + pin(swap(sums, "row", bit)))
+    sums_got = swap(sums, "row", bits[-1])
+    out_far = pin(out_far)
+    hidden_out = pin((middle + out_own + out_got_own + out_first + out_far).astype(low))
+    gate_up_grad, gate_up_got, down_got = pin(gate_up_grad, gate_up_got, down_got)
     gate_grad, up_grad = (
         pair_join(ring, gate_up_grad[:columns_here, at], gate_up_got[:, at], 1)
         for at in (slice(0, gate_up_grad.shape[1] // 2), slice(gate_up_grad.shape[1] // 2, None))
     )
     down_out = pair_join(ring, down_grad[:, : down_grad.shape[1] // 2], down_got, 0)
-    gate_grad, up_grad, down_out, sums_got = pin(gate_grad, up_grad, down_out, sums_got)
-    sums = pin(sums + sums_got)
-    bit *= 2
-    while bit < rows:
-        sums_got = swap(sums, "row", bit)
-        bit *= 2
-        if bit < rows:
-            sums = pin(sums + sums_got)
-    on, back, sums_got, out_far = pin(on, back, sums_got, out_far)
+    gate_grad, up_grad, down_out = pin(gate_grad, up_grad, down_out)
+    on, back, sums_got = pin(on, back, sums_got)
     sums = sums + sums_got
     total = ring.inner_sum(own[4].astype(f32) + on + back, 0)
-    hidden_out = (middle + out_own + out_far).astype(low)
     attn_gain, ffwd_gain, query_gain, key_gain = jnp.split(
         sums, [part_width, 2 * part_width, 2 * part_width + head_size]
     )

time: 596 us -> 583 us (0.978)
  waiting for transfers between devices: 206 us -> 183 us
    ppermute x8, waiting for transfers between devices: 33 us -> 18.8 us  [send_back(): return lax.ppermute(value, 'row', self.backward)]
    ppermute x8, waiting for transfers between devices: 47.4 us -> 33.7 us  [send_on(): return lax.ppermute(value, 'row', self.onward)]
    add x6 -> x3, other arithmetic: 13.1 us -> 1.84 us  [the longest x1 1.53 us: local(): to_partner = own_other.astype(f32) + near_other]
    convert_element_type x2 -> x7, other arithmetic: 8.13 us -> 15.1 us  [the longest x1 2.99 us: local(): to_far = (out_to_far.astype(f32) + out_got_far + out_second).astype(low)]
    slice x9 -> x2, local copies, waits for them, and re-layouts: 6.18 us -> 0.13 us  [the longest x1 0.07 us: local(): to_partner[half:]]
    ppermute x39 -> x45, waiting for transfers between devices: 94.6 us -> 92.6 us  [swap(): lax.ppermute(value, axis, [(i, i ^ bit) for i in range(lax.axis_size(axis...]
    ppermute x12 -> x13, starting transfers between devices: 12.1 us -> 13.5 us  [to_partner(): return lax.ppermute(value, 'row', self.partner)]
    ppermute x39 -> x45, starting transfers between devices: 26.7 us -> 25.5 us  [swap(): lax.ppermute(value, axis, [(i, i ^ bit) for i in range(lax.axis_size(axis...]
  transfers between devices with their start and end apart: 72 -> 79, of which waited for: 32 -> 34; matrix products, arithmetic and copies ran while one was open for 13% -> 14% of each run, Pallas kernels for 32% -> 36%
where the time goes in v5:
time: 583 us; the launch traced here: 577 us
  Pallas kernels  210 us (36%)
  waiting for transfers between devices  183 us (31%)
  other arithmetic  64.2 us (11%)
  starting transfers between devices  60.6 us (10%)
  local copies, waits for them, and re-layouts  43.1 us (7%)
  between operations  15.5 us (3%)
    pallas_call x22, Pallas kernels, kernel_call(): pl.pallas_call(body, grid_spec=pltpu.PrefetchScalarGridSpec(num_scalar_pr...  210 us
    ppermute x45, waiting for transfers between devices, swap(): lax.ppermute(value, axis, [(i, i ^ bit) for i in range(lax.axis_size(axis...  92.6 us
    ppermute x8, waiting for transfers between devices, send_on(): return lax.ppermute(value, 'row', self.onward)  33.7 us
    ppermute x45, starting transfers between devices, swap(): lax.ppermute(value, axis, [(i, i ^ bit) for i in range(lax.axis_size(axis...  25.5 us
    unnamed x161, local copies, waits for them, and re-layouts  22.3 us
    all_gather x2, waiting for transfers between devices, pair_gather(): return lax.all_gather(unit, 'row', axis=0, axis_index_groups=ring.pairs)  19.3 us
    ppermute x8, waiting for transfers between devices, send_back(): return lax.ppermute(value, 'row', self.backward)  18.8 us
    ppermute x13, waiting for transfers between devices, to_partner(): return lax.ppermute(value, 'row', self.partner)  15.7 us
  transfers between devices with their start and end apart: 79, of which 34 were waited for; matrix products, arithmetic and copies ran while one was open for 14% of the time, Pallas kernels for 36%

profile of v5, /device:TPU:0, one launch (start us, length us, event | category | flops | bytes accessed | tf_op | source)
XLA Modules:
  0.0 576.7 jit_solution(6079633399501210395)
XLA Ops:
  16.7 9.4 %collective-permute-done.1.refs_12_.refs_8_ = bf16[256,1024]{1,0:T(8,128)(2,1)S(1)} collective-permute-done((bf16[256,1024]{1,0:T(8,128)(2,1)S(1)}, bf16[256,1024]{1,0:T(8,128)(2,1)S(1)}, u32[]{:S(2)}, u32[]{:S(2)}) %collective-permute-start.1) | collective-permute-done | bytes 524320 | tf_op jit(solution)/shard_map/ppermute | solution.py:76
  55.8 14.0 %collective-permute-done.10.refs_8_.refs_4_ = bf16[256,1024]{1,0:T(8,128)(2,1)S(1)} collective-permute-done((bf16[256,1024]{1,0:T(8,128)(2,1)}, bf16[256,1024]{1,0:T(8,128)(2,1)S(1)}, u32[]{:S(2)}, u32[]{:S(2)}) %collective-permute-start.10) | collective-permute-done | bytes 524320 | tf_op jit(solution)/shard_map/ppermute | solution.py:73
  76.6 10.2 %collective-permute-done.14 = bf16[256,1536]{1,0:T(8,128)(2,1)} collective-permute-done((bf16[256,1536]{1,0:T(8,128)(2,1)}, bf16[256,1536]{1,0:T(8,128)(2,1)}, u32[]{:S(2)}, u32[]{:S(2)}) %collective-permute-start.14) | collective-permute-done | bytes 786464 | tf_op jit(solution)/shard_map/ppermute | solution.py:79
  100.8 11.9 %shard_map.300 = (bf16[1024,2048]{1,0:T(8,128)(2,1)}, f32[1024,1]{1,0:T(8,128)S(1)}, f32[1024,1024]{1,0:T(8,128)}) custom-call(s32[8]{0:T(128)S(1)} %get-tuple-element.1034.place_ref, bf16[1024,512]{1,0:T(8,128)(2,1)S(1)} %copy-done.6, bf16[1024,512]{1,0:T(8,128)(2,1)} %collective-permute-done.2.refs_1_, bf16[1024,512]{1,0:T(8,128)(2,1)} %collective-permute-done.8.refs_2_, ...), custom_call_target="tpu_custom_call" | custom-call | flops 85899344 | bytes 65536 | tf_op jit(solution)/shard_map/pallas_call | solution.py:164
  113.5 13.8 %shard_map.301 = (bf16[1024,512]{1,0:T(8,128)(2,1)S(1)}, bf16[1024,256]{1,0:T(8,128)(2,1)S(1)}, bf16[1024,256]{1,0:T(8,128)(2,1)S(1)}, bf16[1024,512]{1,0:T(8,128)(2,1)S(1)}) custom-call(s32[1]{0:T(128)} %constant.77.clone.1._.order_ref, f32[1024,1024]{1,0:T(8,128)} %get-tuple-element.798.q_ref.k_ref.v_ref, ...), custom_call_target="tpu_custom_call" | custom-call | flops 120795952 | bytes 65536 | tf_op jit(solution)/shard_map/pallas_call | solution.py:164
  148.1 17.3 %collective-permute-done.21 = bf16[1024,512]{1,0:T(8,128)(2,1)S(1)} collective-permute-done((bf16[1024,512]{1,0:T(8,128)(2,1)S(1)}, bf16[1024,512]{1,0:T(8,128)(2,1)S(1)}, u32[]{:S(2)}, u32[]{:S(2)}) %collective-permute-start.21) | collective-permute-done | bytes 1048608 | tf_op jit(solution)/shard_map/ppermute | solution.py:140
  167.4 8.4 %collective-permute-done.23 = bf16[512,512]{1,0:T(8,128)(2,1)S(1)} collective-permute-done((bf16[512,512]{1,0:T(8,128)(2,1)S(1)}, bf16[512,512]{1,0:T(8,128)(2,1)S(1)}, u32[]{:S(2)}, u32[]{:S(2)}) %collective-permute-start.23) | collective-permute-done | bytes 524320 | tf_op jit(solution)/shard_map/ppermute | solution.py:140
  187.1 15.4 %collective-permute-done.28.refs_1_ = bf16[1024,512]{1,0:T(8,128)(2,1)} collective-permute-done((bf16[1024,512]{1,0:T(8,128)(2,1)S(1)}, bf16[1024,512]{1,0:T(8,128)(2,1)}, u32[]{:S(2)}, u32[]{:S(2)}) %collective-permute-start.28) | collective-permute-done | bytes 1048608 | tf_op jit(solution)/shard_map/ppermute | solution.py:140
  215.6 14.9 %shard_map.305 = (bf16[1024,2048]{1,0:T(8,128)(2,1)}, f32[1024,1]{1,0:T(8,128)S(1)}, f32[1024,768]{1,0:T(8,128)}, f32[1024,768]{1,0:T(8,128)}, bf16[1024,768]{1,0:T(8,128)(2,1)}) custom-call(s32[8]{0:T(128)S(1)} %fusion.16.place_ref, bf16[1024,512]{1,0:T(8,128)(2,1)S(1)} %get-tuple-element.608.refs_0_, bf16[1024,512]{1,0:T(8,128)(2,1)} %collective-permute-done.28.refs_1_, ...), custom_call_target="tpu_custom_call" | custom-call | flops 128849016 | bytes 65536 | tf_op jit(solution)/shard_map/pallas_call | solution.py:164
  233.9 14.3 %shard_map.306 = (bf16[1024,2048]{1,0:T(8,128)(2,1)}, f32[1024,1]{1,0:T(8,128)}, f32[1024,768]{1,0:T(8,128)}, f32[1024,768]{1,0:T(8,128)}, bf16[1024,768]{1,0:T(8,128)(2,1)}) custom-call(s32[8]{0:T(128)S(1)} %fusion.16.place_ref, bf16[1024,512]{1,0:T(8,128)(2,1)} %collective-permute-done.29.refs_0_, bf16[1024,512]{1,0:T(8,128)(2,1)S(1)} %pad_maximum_fusion.6.refs_1_, ...), custom_call_target="tpu_custom_call" | custom-call | flops 128849016 | bytes 65536 | tf_op jit(solution)/shard_map/pallas_call | solution.py:164
  248.7 11.5 %shard_map.307 = bf16[4,768,512]{2,1,0:T(8,128)(2,1)} custom-call(s32[4]{0:T(128)} %iota.28._, bf16[1024,768]{1,0:T(8,128)(2,1)} %get-tuple-element.757.refs_0_, bf16[1024,768]{1,0:T(8,128)(2,1)} %get-tuple-element.749.refs_1_.refs_0_, bf16[1024,2048]{1,0:T(8,128)(2,1)} %copy-done.1, bf16[1024,2048]{1,0:T(8,128)(2,1)} %copy-done.2), custom_call_target="tpu_custom_call" | custom-call | flops 128849016 | bytes 65536 | tf_op jit(solution)/shard_map/pallas_call | solution.py:164
  260.5 12.8 %all-gather.11.cloned.1.call-done = bf16[3072,512]{1,0:T(8,128)(2,1)} async-done(((bf16[768,512]{1,0:T(8,128)(2,1)}), bf16[3072,512]{1,0:T(8,128)(2,1)}) %all-gather.11.cloned.1.call-update) | async-done | bytes 3145744 | tf_op jit(solution)/shard_map/all_gather | solution.py:108
  273.2 9.2 %shard_map.308 = (bf16[1024,1536]{1,0:T(8,128)(2,1)S(1)}, f32[1024,1]{1,0:T(8,128)S(1)}) custom-call(s32[1]{0:T(128)} %constant.77.clone.1._.order_ref, bf16[1024,2048]{1,0:T(8,128)(2,1)} %copy-done.2, f32[1024,768]{1,0:T(8,128)} %get-tuple-element.658.refs_1_, f32[1024,768]{1,0:T(8,128)} %get-tuple-element.659.refs_2_, bf16[4,768,512]{2,1,0:T(8,128)(2,1)} %bitcast.90), custom_call_target="tpu_custom_call" | custom-call | flops 64424508 | bytes 65536 | tf_op jit(solution)/shard_map/pallas_call | solution.py:164
  284.9 12.3 %shard_map.309 = (bf16[1024,512]{1,0:T(8,128)(2,1)S(1)}, bf16[1024,512]{1,0:T(8,128)(2,1)S(1)}, bf16[1024,512]{1,0:T(8,128)(2,1)}, bf16[1024,512]{1,0:T(8,128)(2,1)}) custom-call(s32[8]{0:T(128)S(1)} %fusion.16.place_ref, bf16[1024,1536]{1,0:T(8,128)(2,1)} %copy-done.4, bf16[4,512,1536]{2,1,0:T(8,128)(2,1)} %bitcast.88), custom_call_target="tpu_custom_call" | custom-call | flops 128849016 | bytes 65536 | tf_op jit(solution)/shard_map/pallas_call | solution.py:164
  301.1 8.8 %shard_map.310 = (bf16[1024,1536]{1,0:T(8,128)(2,1)S(1)}, f32[1024,1]{1,0:T(8,128)S(1)}) custom-call(s32[1]{0:T(128)} %constant.77.clone.1._.order_ref, bf16[1024,2048]{1,0:T(8,128)(2,1)} %copy-done.1, f32[1024,768]{1,0:T(8,128)} %get-tuple-element.679.refs_1_, f32[1024,768]{1,0:T(8,128)} %get-tuple-element.680.refs_2_, bf16[4,768,512]{2,1,0:T(8,128)(2,1)} %bitcast.91), custom_call_target="tpu_custom_call" | custom-call | flops 64424508 | bytes 65536 | tf_op jit(solution)/shard_map/pallas_call | solution.py:164
  316.6 11.5 %shard_map.311 = (bf16[1024,512]{1,0:T(8,128)(2,1)S(1)}, bf16[1024,512]{1,0:T(8,128)(2,1)S(1)}, bf16[1024,512]{1,0:T(8,128)(2,1)S(1)}, bf16[1024,512]{1,0:T(8,128)(2,1)S(1)}) custom-call(s32[8]{0:T(128)S(1)} %fusion.16.place_ref, bf16[1024,1536]{1,0:T(8,128)(2,1)} %copy-done.5, bf16[4,512,1536]{2,1,0:T(8,128)(2,1)} %bitcast.89), custom_call_target="tpu_custom_call" | custom-call | flops 128849016 | bytes 65536 | tf_op jit(solution)/shard_map/pallas_call | solution.py:164
  337.6 19.3 %shard_map.312 = bf16[4,512,1536]{2,1,0:T(8,128)(2,1)} custom-call(s32[4]{0:T(128)} %iota.29._, bf16[1024,2048]{1,0:T(8,128)(2,1)} %get-tuple-element.725.refs_0_, bf16[1024,2048]{1,0:T(8,128)(2,1)} %get-tuple-element.726.refs_1_, bf16[1024,1536]{1,0:T(8,128)(2,1)} %copy-done.5, bf16[1024,1536]{1,0:T(8,128)(2,1)} %copy-done.4), custom_call_target="tpu_custom_call" | custom-call | flops 257698032 | bytes 65536 | tf_op jit(solution)/shard_map/pallas_call | solution.py:164
  386.4 8.7 %collective-permute-done.48.refs_1_ = bf16[1024,512]{1,0:T(8,128)(2,1)S(1)} collective-permute-done((bf16[1024,512]{1,0:T(8,128)(2,1)S(1)}, bf16[1024,512]{1,0:T(8,128)(2,1)S(1)}, u32[]{:S(2)}, u32[]{:S(2)}) %collective-permute-start.48) | collective-permute-done | bytes 1048608 | tf_op jit(solution)/shard_map/ppermute | solution.py:140
  414.0 19.7 %shard_map.317 = (bf16[1024,512]{1,0:T(8,128)(2,1)S(1)}, bf16[1024,256]{1,0:T(8,128)(2,1)S(1)}, bf16[1024,256]{1,0:T(8,128)(2,1)S(1)}, f32[16,128]{1,0:T(8,128)S(1)}) custom-call(s32[1]{0:T(128)} %constant.77.clone.1._.order_ref, f32[1024,1024]{1,0:T(8,128)} %get-tuple-element.798.q_ref.k_ref.v_ref, f32[1024,1024]{1,0:T(8,128)} %get-tuple-element.798.q_ref.k_ref.v_ref, ...), custom_call_target="tpu_custom_call" | custom-call | flops 169114336 | bytes 65536 | tf_op jit(solution)/shard_map/pallas_call | solution.py:164
  447.2 9.3 %shard_map.319 = (bf16[1024,512]{1,0:T(8,128)(2,1)S(1)}, bf16[1024,512]{1,0:T(8,128)(2,1)}, bf16[1024,512]{1,0:T(8,128)(2,1)}, bf16[1024,512]{1,0:T(8,128)(2,1)}...) custom-call(s32[8]{0:T(128)S(1)} %get-tuple-element.1034.place_ref, bf16[1024,1024]{1,0:T(8,128)(2,1)} %pad_maximum_fusion.refs_2_.refs_0_, ...), custom_call_target="tpu_custom_call" | custom-call | flops 85899344 | bytes 65536 | tf_op jit(solution)/shard_map/pallas_call | solution.py:164
  466.0 10.0 %shard_map.321 = bf16[5,256,1536]{2,1,0:T(8,128)(2,1)} custom-call(s32[5]{0:T(128)} %constant.86.clone._, bf16[1024,2048]{1,0:T(8,128)(2,1)} %get-tuple-element.850.refs_0_.refs_9_, bf16[1024,2048]{1,0:T(8,128)(2,1)} %copy-done, bf16[1024,1024]{1,0:T(8,128)(2,1)} %pad_maximum_fusion.refs_2_.refs_0_, bf16[1024,512]{1,0:T(8,128)(2,1)} %copy-done.3), custom_call_target="tpu_custom_call" | custom-call | flops 80530640 | bytes 65536 | tf_op jit(solution)/shard_map/pallas_call | solution.py:164
  495.7 12.0 %collective-permute-done.64 = f32[1280]{0:T(1024)S(1)} collective-permute-done((f32[1280]{0:T(1024)S(1)}, f32[1280]{0:T(1024)S(1)}, u32[]{:S(2)}, u32[]{:S(2)}) %collective-permute-start.64) | collective-permute-done | bytes 5152 | tf_op jit(solution)/shard_map/ppermute | solution.py:140
  522.1 10.2 %collective-permute-done.68 = f32[1280]{0:T(1024)S(1)} collective-permute-done((f32[1280]{0:T(1024)S(1)}, f32[1280]{0:T(1024)S(1)}, u32[]{:S(2)}, u32[]{:S(2)}) %collective-permute-start.68) | collective-permute-done | bytes 5152 | tf_op jit(solution)/shard_map/ppermute | solution.py:140
  554.1 10.4 %collective-permute-done.71 = bf16[256,1536]{1,0:T(8,128)(2,1)S(1)} collective-permute-done((bf16[256,1536]{1,0:T(8,128)(2,1)S(1)}, bf16[256,1536]{1,0:T(8,128)(2,1)S(1)}, u32[]{:S(2)}, u32[]{:S(2)}) %collective-permute-start.71) | collective-permute-done | bytes 786464 | tf_op jit(solution)/shard_map/ppermute | solution.py:73
  (424 shorter events, 266.2 us)
Async XLA Ops:
  7.2 86.6 %all-gather.7.cloned.1.call-start = ((), (), s32[]{:S(2)}) async-start(), calls=%async_computation.4 | async-start | bytes 2359296 | tf_op jit(solution)/shard_map/all_gather | solution.py:82
  7.9 201.4 %all-gather.9.cloned.1.call-start = ((), (), s32[]{:S(2)}) async-start(), calls=%async_computation.5 | async-start | bytes 7864320 | tf_op jit(solution)/shard_map/all_gather | solution.py:108
  12.3 42.3 %collective-permute-start.8 = (bf16[1024,512]{1,0:T(8,128)(2,1)}, bf16[1024,512]{1,0:T(8,128)(2,1)}, u32[]{:S(2)}, u32[]{:S(2)}) collective-permute-start(bf16[1024,512]{1,0:T(8,128)(2,1)} %refs_0_), channel_id=1, source_target_pairs={{0,1},{1,0},{2,3},{3,2},{4,5},{5,4},{6,7},{7,6},{8,9},{9,8},{10,11... | collective-permute-start | bytes 3145736 | tf_op jit(solution)/shard_map/ppermute | solution.py:140
  12.3 26.1 %collective-permute-start.2 = (bf16[1024,512]{1,0:T(8,128)(2,1)}, bf16[1024,512]{1,0:T(8,128)(2,1)}, u32[]{:S(2)}, u32[]{:S(2)}) collective-permute-start(bf16[1024,512]{1,0:T(8,128)(2,1)} %refs_0_), channel_id=1, source_target_pairs={{0,2},{1,3},{2,0},{3,1},{4,6},{5,7},{6,4},{7,5},{8,10},{9,11},{10,... | collective-permute-start | bytes 3145736 | tf_op jit(solution)/shard_map/ppermute | solution.py:140
  46.4 28.1 %collective-permute-start.11 = (bf16[256,1024]{1,0:T(8,128)(2,1)}, bf16[256,1024]{1,0:T(8,128)(2,1)S(1)}, u32[]{:S(2)}, u32[]{:S(2)}) collective-permute-start(bf16[256,1024]{1,0:T(8,128)(2,1)} %collective-permute-done.5.refs_11_.refs_7_), channel_id=1, source_target_pairs={{8,0},{16,8},{24,16},{28,24},{20,28},{12,20},{4,12},{0,4},{9,1},{1... | collective-permute-start | bytes 1572872 | tf_op jit(solution)/shard_map/ppermute | solution.py:76
  50.8 35.9 %collective-permute-start.14 = (bf16[256,1536]{1,0:T(8,128)(2,1)}, bf16[256,1536]{1,0:T(8,128)(2,1)}, u32[]{:S(2)}, u32[]{:S(2)}) collective-permute-start(bf16[256,1536]{1,0:T(8,128)(2,1)} %pad_maximum_fusion.10), channel_id=1, source_target_pairs={{0,4},{4,0},{8,12},{12,8},{16,20},{20,16},{24,28},{28,24},{1,5},{5... | collective-permute-start | bytes 2359304 | tf_op jit(solution)/shard_map/ppermute | solution.py:79
  93.8 179.4 %all-gather.11.cloned.1.call-start = ((), (), s32[]{:S(2)}) async-start(), calls=%async_computation.6 | async-start | bytes 3932160 | tf_op jit(solution)/shard_map/all_gather | solution.py:108
  93.9 36.1 %collective-permute-start.16 = (bf16[1024,512]{1,0:T(8,128)(2,1)}, bf16[1024,512]{1,0:T(8,128)(2,1)}, u32[]{:S(2)}, u32[]{:S(2)}) collective-permute-start(bf16[1024,512]{1,0:T(8,128)(2,1)} %refs_0_.1), channel_id=1, source_target_pairs={{0,4},{4,0},{8,12},{12,8},{16,20},{20,16},{24,28},{28,24},{1,5},{5... | collective-permute-start | bytes 3145736 | tf_op jit(solution)/shard_map/ppermute | solution.py:79
  94.3 35.8 %collective-permute-start.15 = (bf16[1024,512]{1,0:T(8,128)(2,1)}, bf16[1024,512]{1,0:T(8,128)(2,1)}, u32[]{:S(2)}, u32[]{:S(2)}) collective-permute-start(bf16[1024,512]{1,0:T(8,128)(2,1)} %refs_0_.1), channel_id=1, source_target_pairs={{0,2},{1,3},{2,0},{3,1},{4,6},{5,7},{6,4},{7,5},{8,10},{9,11},{10,... | collective-permute-start | bytes 3145736 | tf_op jit(solution)/shard_map/ppermute | solution.py:140
  98.1 31.9 %collective-permute-start.17 = (bf16[768,256]{1,0:T(8,128)(2,1)S(1)}, bf16[768,256]{1,0:T(8,128)(2,1)S(1)}, u32[]{:S(2)}, u32[]{:S(2)}) collective-permute-start(bf16[768,256]{1,0:T(8,128)(2,1)S(1)} %get-tuple-element.1012), channel_id=1, source_target_pairs={{0,4},{4,0},{8,12},{12,8},{16,20},{20,16},{24,28},{28,24},{1,5},{5... | collective-permute-start | bytes 1179656 | tf_op jit(solution)/shard_map/ppermute | solution.py:79
  139.3 26.1 %collective-permute-start.21 = (bf16[1024,512]{1,0:T(8,128)(2,1)S(1)}, bf16[1024,512]{1,0:T(8,128)(2,1)S(1)}, u32[]{:S(2)}, u32[]{:S(2)}) collective-permute-start(bf16[1024,512]{1,0:T(8,128)(2,1)S(1)} %add_convert_fusion.6), channel_id=1, source_target_pairs={{0,2},{1,3},{2,0},{3,1},{4,6},{5,7},{6,4},{7,5},{8,10},{9,11},{10,... | collective-permute-start | bytes 3145736 | tf_op jit(solution)/shard_map/ppermute | solution.py:140
  142.4 33.4 %collective-permute-start.23 = (bf16[512,512]{1,0:T(8,128)(2,1)S(1)}, bf16[512,512]{1,0:T(8,128)(2,1)S(1)}, u32[]{:S(2)}, u32[]{:S(2)}) collective-permute-start(bf16[512,512]{1,0:T(8,128)(2,1)S(1)} %slice.149), channel_id=1, source_target_pairs={{0,2},{1,3},{2,0},{3,1},{4,6},{5,7},{6,4},{7,5},{8,10},{9,11},{10,... | collective-permute-start | bytes 1572872 | tf_op jit(solution)/shard_map/ppermute | solution.py:140
  144.9 34.3 %collective-permute-start.26 = (bf16[1024,512]{1,0:T(8,128)(2,1)}, bf16[1024,512]{1,0:T(8,128)(2,1)}, u32[]{:S(2)}, u32[]{:S(2)}) collective-permute-start(bf16[1024,512]{1,0:T(8,128)(2,1)} %collective-permute-done.16.refs_0_), channel_id=1, source_target_pairs={{0,1},{1,0},{2,3},{3,2},{4,5},{5,4},{6,7},{7,6},{8,9},{9,8},{10,11... | collective-permute-start | bytes 3145736 | tf_op jit(solution)/shard_map/ppermute | solution.py:140
  209.4 147.5 %reduce-scatter.3.cloned.1.call-start = ((), (), s32[]{:S(2)}) async-start(), calls=%async_computation.2 | async-start | bytes 3932160 | tf_op jit(solution)/shard_map/reduce_scatter | solution.py:112
  260.3 217.9 %reduce-scatter.5.cloned.1.call-start = ((), (), s32[]{:S(2)}) async-start(), calls=%async_computation.3 | async-start | bytes 7864320 | tf_op jit(solution)/shard_map/reduce_scatter | solution.py:112
  369.5 25.6 %collective-permute-start.48 = (bf16[1024,512]{1,0:T(8,128)(2,1)S(1)}, bf16[1024,512]{1,0:T(8,128)(2,1)S(1)}, u32[]{:S(2)}, u32[]{:S(2)}) collective-permute-start(bf16[1024,512]{1,0:T(8,128)(2,1)S(1)} %get-tuple-element.782.refs_0_), channel_id=1, source_target_pairs={{0,2},{1,3},{2,0},{3,1},{4,6},{5,7},{6,4},{7,5},{8,10},{9,11},{10,... | collective-permute-start | bytes 3145736 | tf_op jit(solution)/shard_map/ppermute | solution.py:140
  395.1 38.6 %collective-permute-start.53 = (bf16[1024,512]{1,0:T(8,128)(2,1)S(1)}, bf16[1024,512]{1,0:T(8,128)(2,1)S(1)}, u32[]{:S(2)}, u32[]{:S(2)}) collective-permute-start(bf16[1024,512]{1,0:T(8,128)(2,1)S(1)} %get-tuple-element.808), channel_id=1, source_target_pairs={{0,1},{1,0},{2,3},{3,2},{4,5},{5,4},{6,7},{7,6},{8,9},{9,8},{10,11... | collective-permute-start | bytes 3145736 | tf_op jit(solution)/shard_map/ppermute | solution.py:140
  395.6 38.2 %collective-permute-start.54 = (bf16[1024,512]{1,0:T(8,128)(2,1)S(1)}, bf16[1024,512]{1,0:T(8,128)(2,1)}, u32[]{:S(2)}, u32[]{:S(2)}) collective-permute-start(bf16[1024,512]{1,0:T(8,128)(2,1)S(1)} %get-tuple-element.809), channel_id=1, source_target_pairs={{0,1},{1,0},{2,3},{3,2},{4,5},{5,4},{6,7},{7,6},{8,9},{9,8},{10,11... | collective-permute-start | bytes 3145736 | tf_op jit(solution)/shard_map/ppermute | solution.py:140
  401.7 32.0 %collective-permute-start.52 = (bf16[1024,512]{1,0:T(8,128)(2,1)S(1)}, bf16[1024,512]{1,0:T(8,128)(2,1)S(1)}, u32[]{:S(2)}, u32[]{:S(2)}) collective-permute-start(bf16[1024,512]{1,0:T(8,128)(2,1)S(1)} %add_convert_fusion.4), channel_id=1, source_target_pairs={{0,4},{4,0},{8,12},{12,8},{16,20},{20,16},{24,28},{28,24},{1,5},{5... | collective-permute-start | bytes 3145736 | tf_op jit(solution)/shard_map/ppermute | solution.py:79
  402.3 73.7 %collective-permute-start.57 = (bf16[1024,512]{1,0:T(8,128)(2,1)}, bf16[1024,512]{1,0:T(8,128)(2,1)}, u32[]{:S(2)}, u32[]{:S(2)}) collective-permute-start(bf16[1024,512]{1,0:T(8,128)(2,1)} %add_convert_fusion.3), channel_id=1, source_target_pairs={{0,4},{4,0},{8,12},{12,8},{16,20},{20,16},{24,28},{28,24},{1,5},{5... | collective-permute-start | bytes 3145736 | tf_op jit(solution)/shard_map/ppermute | solution.py:79
  443.1 33.0 %collective-permute-start.55 = (bf16[128,1536]{1,0:T(8,128)(2,1)}, bf16[128,1536]{1,0:T(8,128)(2,1)}, u32[]{:S(2)}, u32[]{:S(2)}) collective-permute-start(bf16[128,1536]{1,0:T(8,128)(2,1)} %get-tuple-element.854), channel_id=1, source_target_pairs={{0,8},{8,16},{16,24},{24,28},{28,20},{20,12},{12,4},{4,0},{1,9},{9... | collective-permute-start | bytes 1179656 | tf_op jit(solution)/shard_map/ppermute | solution.py:73
  443.1 33.0 %collective-permute-start.56 = (bf16[128,1536]{1,0:T(8,128)(2,1)}, bf16[128,1536]{1,0:T(8,128)(2,1)}, u32[]{:S(2)}, u32[]{:S(2)}) collective-permute-start(bf16[128,1536]{1,0:T(8,128)(2,1)} %get-tuple-element.855), channel_id=1, source_target_pairs={{8,0},{16,8},{24,16},{28,24},{20,28},{12,20},{4,12},{0,4},{9,1},{1... | collective-permute-start | bytes 1179656 | tf_op jit(solution)/shard_map/ppermute | solution.py:76
  520.6 29.2 %collective-permute-start.70 = (bf16[256,1536]{1,0:T(8,128)(2,1)}, bf16[256,1536]{1,0:T(8,128)(2,1)S(1)}, u32[]{:S(2)}, u32[]{:S(2)}) collective-permute-start(bf16[256,1536]{1,0:T(8,128)(2,1)} %slice.179), channel_id=1, source_target_pairs={{0,4},{4,0},{8,12},{12,8},{16,20},{20,16},{24,28},{28,24},{1,5},{5... | collective-permute-start | bytes 2359304 | tf_op jit(solution)/shard_map/ppermute | solution.py:79
  536.5 28.1 %collective-permute-start.71 = (bf16[256,1536]{1,0:T(8,128)(2,1)S(1)}, bf16[256,1536]{1,0:T(8,128)(2,1)S(1)}, u32[]{:S(2)}, u32[]{:S(2)}) collective-permute-start(bf16[256,1536]{1,0:T(8,128)(2,1)S(1)} %get-tuple-element.933), channel_id=1, source_target_pairs={{0,8},{8,16},{16,24},{24,28},{28,20},{20,12},{12,4},{4,0},{1,9},{9... | collective-permute-start | bytes 2359304 | tf_op jit(solution)/shard_map/ppermute | solution.py:73
  (133 other events, 1410.8 us)
Sparse Core Ops, SparseCore 0:
  10.1 64.2 all-gather.6
  93.9 115.3 all-gather.8
  211.5 61.7 all-gather.10
  275.4 58.8 reduce-scatter.2
  361.2 116.9 reduce-scatter.4

commit v6 on v5

--- a/solution.py
+++ b/solution.py
@@ -248,6 +248,24 @@
     return kernel_call(
         body, place, operands, specs, outs, out_specs, (columns // tile,), scratch, 2 * tokens * full * columns, 48
     )
+
+
+def above(first, second):
+    def body(_, first_ref, second_ref, out_ref):
+        @pl.when(pl.program_id(0) == 0)
+        def _():
+            out_ref[...] = first_ref[...]
+
+        @pl.when(pl.program_id(0) == 1)
+        def _():
+            out_ref[...] = second_ref[...]
+
+    rows, columns = first.shape
+    out = shape_of((2 * rows, columns), first.dtype)
+    return kernel_call(
+        body, jnp.zeros((1,), jnp.int32), (first, second), [whole_spec(first), whole_spec(second)], (out,),
+        (rows_spec(out, rows),), (2,), [], 0, 32,
+    )[0]
 
 
 def units_of(refs):
@@ -677,10 +695,10 @@
     ahead.append(back)
     cut = on.shape[0] // 2
     on, back = ring.send_on(on[:cut]), ring.send_back(back[cut:])
-    on, back, gate_up_got = pin(on, back, gate_up_got)
+    gate_up_got, output_all = pin(gate_up_got, output_all)
+    gate_up_all = pair_gather(ring, run(above, gate_up_mine, gate_up_got))
+    on, back = pin(on, back)
     qkv_all = [qkv, *behind, jnp.concatenate([on, back], 0), *ahead[::-1]]
-    gate_up, output_all = pin(jnp.concatenate([gate_up_mine, gate_up_got], 0), output_all)
-    gate_up_all = pair_gather(ring, gate_up)
     gains = jnp.stack([gains, gains_far, gains_near, gains_diagonal], 1).reshape(2, 1, full_width)
 
     down, upstream = pin(w_down, cotangent)
@@ -720,12 +738,11 @@
     upstream_other = run(lambda *blocks: assemble(pair_place, blocks), up_partner, up_corner, up_partner_near, up_corner_near)
     mid_far = pin(mid_far)
     mid_diagonal = near(mid_far)
-    mid_partner = pin(mid_partner)
+    mid_diagonal, mid_partner = pin(mid_diagonal, mid_partner)
     corner = far(mid_partner[:half]), ring.to_partner(mid_far[half:])
     mid_partner_near = near(mid_partner)
     gate_up_all = pin(gate_up_all)
-    down_all = pair_gather(ring, pin(down_unit))
-    mid_diagonal = pin(mid_diagonal)
+    down_all = pair_gather(ring, down_unit)
 
     def swish(blocks, gain, weights):
         return gather_swish(pair_place, blocks, gain, weights, EPS)
@@ -846,8 +863,8 @@
     )
     got_far, got_own = near(to_diagonal), near(to_near)
     second = parts(steps + 1, steps - 1)
-    own, on, back, out_second, gate_up_grad = parts(
-        *(n for s in range(2, steps) for n in (steps + s, steps - s)), 0, beside=(on, back, out_second, gate_up_grad)
+    own, on, back, out_second = parts(
+        *(n for s in range(2, steps) for n in (steps + s, steps - s)), 0, beside=(on, back, out_second)
     )
     on = jnp.concatenate([second[0, :cut] + on.astype(f32), second[0, cut:].astype(f32)], 0)
     back = jnp.concatenate([second[1, :cut].astype(f32), second[1, cut:] + back.astype(f32)], 0)
@@ -861,7 +878,9 @@
     sums = pin(jnp.concatenate([both_gain[part_width:], (sums + sums_got)[full_width // 2 :]]))
     sums_got = far(sums)
     grad_far = far(to_far)
-    sums_got, out_to_far = pin(sums_got, out_to_far)
+    sums_got, out_to_far, gate_up_grad = pin(sums_got, out_to_far, gate_up_grad)
+    columns_here = gate_up_grad.shape[0] // 2
+    gate_up_got = ring.to_partner(pin(gate_up_grad[columns_here:]))
     attn_gain = (both_gain[:part_width] + sums_got[:part_width]) / attn_norm
     rest = (sums + sums_got)[part_width:]
     inner = rest[2 * head_size :][:, None] / full_width
@@ -873,8 +892,6 @@
     on, back = go(own[0] + on.astype(f32), own[1] + back.astype(f32))
     sums = pin(sums + sums_got)
     sums_got = swap(sums, "row", bits[1])
-    columns_here = gate_up_grad.shape[0] // 2
-    gate_up_got = ring.to_partner(pin(gate_up_grad[columns_here:]))
     grad_far = pin(grad_far)
     to_far = (out_to_far.astype(f32) + out_got_far + out_second).astype(low)
     hidden_grad = (
@@ -885,13 +902,12 @@
     hidden_grad, to_far = pin(hidden_grad, to_far)
     out_far = far(to_far)
     on, back, sums_got = pin(on, back, sums_got)
+    gate_up_got = pin(gate_up_got)
     on, back = go(own[2] + on.astype(f32), own[3] + back.astype(f32))
     sums = pin(sums + sums_got)
     for bit in bits[2:-1]:
         sums = pin(sums + pin(swap(sums, "row", bit)))
     sums_got = swap(sums, "row", bits[-1])
-    out_far = pin(out_far)
-    hidden_out = pin((middle + out_own + out_got_own + out_first + out_far).astype(low))
     gate_up_grad, gate_up_got, down_got = pin(gate_up_grad, gate_up_got, down_got)
     gate_grad, up_grad = (
         pair_join(ring, gate_up_grad[:columns_here, at], gate_up_got[:, at], 1)
@@ -899,6 +915,8 @@
     )
     down_out = pair_join(ring, down_grad[:, : down_grad.shape[1] // 2], down_got, 0)
     gate_grad, up_grad, down_out = pin(gate_grad, up_grad, down_out)
+    out_far = pin(out_far)
+    hidden_out = pin((middle + out_own + out_got_own + out_first + out_far).astype(low))
     on, back, sums_got = pin(on, back, sums_got)
     sums = sums + sums_got
     total = ring.inner_sum(own[4].astype(f32) + on + back, 0)

time: 583 us -> 567 us (0.973)
  waiting for transfers between devices: 183 us -> 164 us
  local copies, waits for them, and re-layouts: 43.1 us -> 54.3 us
    ppermute x8, waiting for transfers between devices: 33.7 us -> 65.7 us  [send_on(): return lax.ppermute(value, 'row', self.onward)]
    all_gather x2, waiting for transfers between devices: 19.3 us -> 1.56 us  [pair_gather(): return lax.all_gather(unit, 'row', axis=0, axis_index_groups=ring.pairs)]
    ppermute x45, waiting for transfers between devices: 92.6 us -> 75.6 us  [swap(): lax.ppermute(value, axis, [(i, i ^ bit) for i in range(lax.axis_size(axis...]
    ppermute x13, waiting for transfers between devices: 15.7 us -> 0.92 us  [to_partner(): return lax.ppermute(value, 'row', self.partner)]
    unnamed x161 -> x171, local copies, waits for them, and re-layouts: 22.3 us -> 28.1 us
    pallas_call x22 -> x23, Pallas kernels: 210 us -> 212 us  [kernel_call(): pl.pallas_call(body, grid_spec=pltpu.PrefetchScalarGridSpec(num_scalar_pr...]
  transfers between devices with their start and end apart: 79 -> 79, of which waited for: 34 -> 30; matrix products, arithmetic and copies ran while one was open for 14% -> 15% of each run, Pallas kernels for 36% -> 37%
where the time goes in v6:
time: 567 us; the launch traced here: 561 us
  Pallas kernels  212 us (37%)
  waiting for transfers between devices  164 us (29%)
  other arithmetic  58.9 us (10%)
  starting transfers between devices  56 us (10%)
  local copies, waits for them, and re-layouts  54.3 us (10%)
  between operations  15.5 us (3%)
    pallas_call x23, Pallas kernels, kernel_call(): pl.pallas_call(body, grid_spec=pltpu.PrefetchScalarGridSpec(num_scalar_pr...  212 us
    ppermute x45, waiting for transfers between devices, swap(): lax.ppermute(value, axis, [(i, i ^ bit) for i in range(lax.axis_size(axis...  75.6 us
    ppermute x8, waiting for transfers between devices, send_on(): return lax.ppermute(value, 'row', self.onward)  65.7 us
    unnamed x171, local copies, waits for them, and re-layouts  28.1 us
    ppermute x45, starting transfers between devices, swap(): lax.ppermute(value, axis, [(i, i ^ bit) for i in range(lax.axis_size(axis...  22.8 us
    ppermute x8, waiting for transfers between devices, send_back(): return lax.ppermute(value, 'row', self.backward)  19.6 us
    ppermute x13, starting transfers between devices, to_partner(): return lax.ppermute(value, 'row', self.partner)  12 us
  transfers between devices with their start and end apart: 79, of which 30 were waited for; matrix products, arithmetic and copies ran while one was open for 15% of the time, Pallas kernels for 37%

profile of v6, /device:TPU:0, one launch (start us, length us, event | category | flops | bytes accessed | tf_op | source)
XLA Modules:
  0.0 561.2 jit_solution(17532384826639579918)
XLA Ops:
  16.6 9.5 %collective-permute-done.1.refs_12_.refs_8_ = bf16[256,1024]{1,0:T(8,128)(2,1)S(1)} collective-permute-done((bf16[256,1024]{1,0:T(8,128)(2,1)S(1)}, bf16[256,1024]{1,0:T(8,128)(2,1)S(1)}, u32[]{:S(2)}, u32[]{:S(2)}) %collective-permute-start.1) | collective-permute-done | bytes 524320 | tf_op jit(solution)/shard_map/ppermute | solution.py:76
  57.4 28.3 %collective-permute-done.10.refs_8_.refs_4_ = bf16[256,1024]{1,0:T(8,128)(2,1)S(1)} collective-permute-done((bf16[256,1024]{1,0:T(8,128)(2,1)}, bf16[256,1024]{1,0:T(8,128)(2,1)S(1)}, u32[]{:S(2)}, u32[]{:S(2)}) %collective-permute-start.10) | collective-permute-done | bytes 524320 | tf_op jit(solution)/shard_map/ppermute | solution.py:73
  104.8 11.5 %shard_map.301 = (bf16[1024,2048]{1,0:T(8,128)(2,1)}, f32[1024,1]{1,0:T(8,128)S(1)}, f32[1024,1024]{1,0:T(8,128)}) custom-call(s32[8]{0:T(128)S(1)} %get-tuple-element.1040.place_ref, bf16[1024,512]{1,0:T(8,128)(2,1)S(1)} %copy-done.6, bf16[1024,512]{1,0:T(8,128)(2,1)} %collective-permute-done.2.refs_1_, bf16[1024,512]{1,0:T(8,128)(2,1)} %collective-permute-done.8.refs_2_, ...), custom_call_target="tpu_custom_call" | custom-call | flops 85899344 | bytes 65536 | tf_op jit(solution)/shard_map/pallas_call | solution.py:164
  117.1 13.8 %shard_map.302 = (bf16[1024,512]{1,0:T(8,128)(2,1)S(1)}, bf16[1024,256]{1,0:T(8,128)(2,1)S(1)}, bf16[1024,256]{1,0:T(8,128)(2,1)S(1)}, bf16[1024,512]{1,0:T(8,128)(2,1)S(1)}) custom-call(s32[1]{0:T(128)} %constant.75.clone.1._.order_ref, f32[1024,1024]{1,0:T(8,128)} %get-tuple-element.802.q_ref.k_ref.v_ref, ...), custom_call_target="tpu_custom_call" | custom-call | flops 120795952 | bytes 65536 | tf_op jit(solution)/shard_map/pallas_call | solution.py:164
  157.4 12.7 %collective-permute-done.21 = bf16[1024,512]{1,0:T(8,128)(2,1)} collective-permute-done((bf16[1024,512]{1,0:T(8,128)(2,1)}, bf16[1024,512]{1,0:T(8,128)(2,1)}, u32[]{:S(2)}, u32[]{:S(2)}) %collective-permute-start.21) | collective-permute-done | bytes 1048608 | tf_op jit(solution)/shard_map/ppermute | solution.py:140
  173.7 6.9 %collective-permute-done.23 = bf16[512,512]{1,0:T(8,128)(2,1)} collective-permute-done((bf16[512,512]{1,0:T(8,128)(2,1)}, bf16[512,512]{1,0:T(8,128)(2,1)}, u32[]{:S(2)}, u32[]{:S(2)}) %collective-permute-start.23) | collective-permute-done | bytes 524320 | tf_op jit(solution)/shard_map/ppermute | solution.py:140
  195.7 13.8 %collective-permute-done.28.refs_1_ = bf16[1024,512]{1,0:T(8,128)(2,1)S(1)} collective-permute-done((bf16[1024,512]{1,0:T(8,128)(2,1)S(1)}, bf16[1024,512]{1,0:T(8,128)(2,1)S(1)}, u32[]{:S(2)}, u32[]{:S(2)}) %collective-permute-start.28) | collective-permute-done | bytes 1048608 | tf_op jit(solution)/shard_map/ppermute | solution.py:140
  220.6 13.9 %shard_map.306 = (bf16[1024,2048]{1,0:T(8,128)(2,1)}, f32[1024,1]{1,0:T(8,128)S(1)}, f32[1024,768]{1,0:T(8,128)}, f32[1024,768]{1,0:T(8,128)}, bf16[1024,768]{1,0:T(8,128)(2,1)}) custom-call(s32[8]{0:T(128)S(1)} %fusion.16.place_ref, bf16[1024,512]{1,0:T(8,128)(2,1)S(1)} %get-tuple-element.612.refs_0_, bf16[1024,512]{1,0:T(8,128)(2,1)S(1)} %copy-done.23, ...), custom_call_target="tpu_custom_call" | custom-call | flops 128849016 | bytes 65536 | tf_op jit(solution)/shard_map/pallas_call | solution.py:164
  238.7 14.6 %shard_map.307 = (bf16[1024,2048]{1,0:T(8,128)(2,1)}, f32[1024,1]{1,0:T(8,128)}, f32[1024,768]{1,0:T(8,128)}, f32[1024,768]{1,0:T(8,128)}, bf16[1024,768]{1,0:T(8,128)(2,1)}) custom-call(s32[8]{0:T(128)S(1)} %fusion.16.place_ref, bf16[1024,512]{1,0:T(8,128)(2,1)} %collective-permute-done.30.refs_0_, bf16[1024,512]{1,0:T(8,128)(2,1)S(1)} %pad_maximum_fusion.5.refs_1_, ...), custom_call_target="tpu_custom_call" | custom-call | flops 128849016 | bytes 65536 | tf_op jit(solution)/shard_map/pallas_call | solution.py:164
  253.8 11.5 %shard_map.308 = bf16[4,768,512]{2,1,0:T(8,128)(2,1)} custom-call(s32[4]{0:T(128)} %iota.28._, bf16[1024,768]{1,0:T(8,128)(2,1)} %get-tuple-element.761.refs_0_, bf16[1024,768]{1,0:T(8,128)(2,1)} %get-tuple-element.753.refs_1_.refs_0_, bf16[1024,2048]{1,0:T(8,128)(2,1)} %copy-done.1, bf16[1024,2048]{1,0:T(8,128)(2,1)} %copy-done.2), custom_call_target="tpu_custom_call" | custom-call | flops 128849016 | bytes 65536 | tf_op jit(solution)/shard_map/pallas_call | solution.py:164
  267.1 9.2 %shard_map.309 = (bf16[1024,1536]{1,0:T(8,128)(2,1)S(1)}, f32[1024,1]{1,0:T(8,128)S(1)}) custom-call(s32[1]{0:T(128)} %constant.75.clone.1._.order_ref, bf16[1024,2048]{1,0:T(8,128)(2,1)} %copy-done.2, f32[1024,768]{1,0:T(8,128)} %get-tuple-element.662.refs_1_, f32[1024,768]{1,0:T(8,128)} %get-tuple-element.663.refs_2_, bf16[4,768,512]{2,1,0:T(8,128)(2,1)} %bitcast.90), custom_call_target="tpu_custom_call" | custom-call | flops 64424508 | bytes 65536 | tf_op jit(solution)/shard_map/pallas_call | solution.py:164
  278.7 12.3 %shard_map.310 = (bf16[1024,512]{1,0:T(8,128)(2,1)S(1)}, bf16[1024,512]{1,0:T(8,128)(2,1)S(1)}, bf16[1024,512]{1,0:T(8,128)(2,1)}, bf16[1024,512]{1,0:T(8,128)(2,1)}) custom-call(s32[8]{0:T(128)S(1)} %fusion.16.place_ref, bf16[1024,1536]{1,0:T(8,128)(2,1)} %copy-done.4, bf16[4,512,1536]{2,1,0:T(8,128)(2,1)} %bitcast.88), custom_call_target="tpu_custom_call" | custom-call | flops 128849016 | bytes 65536 | tf_op jit(solution)/shard_map/pallas_call | solution.py:164
  294.9 8.8 %shard_map.311 = (bf16[1024,1536]{1,0:T(8,128)(2,1)S(1)}, f32[1024,1]{1,0:T(8,128)S(1)}) custom-call(s32[1]{0:T(128)} %constant.75.clone.1._.order_ref, bf16[1024,2048]{1,0:T(8,128)(2,1)} %copy-done.1, f32[1024,768]{1,0:T(8,128)} %get-tuple-element.683.refs_1_, f32[1024,768]{1,0:T(8,128)} %get-tuple-element.684.refs_2_, bf16[4,768,512]{2,1,0:T(8,128)(2,1)} %bitcast.91), custom_call_target="tpu_custom_call" | custom-call | flops 64424508 | bytes 65536 | tf_op jit(solution)/shard_map/pallas_call | solution.py:164
  310.4 11.5 %shard_map.312 = (bf16[1024,512]{1,0:T(8,128)(2,1)S(1)}, bf16[1024,512]{1,0:T(8,128)(2,1)S(1)}, bf16[1024,512]{1,0:T(8,128)(2,1)S(1)}, bf16[1024,512]{1,0:T(8,128)(2,1)S(1)}) custom-call(s32[8]{0:T(128)S(1)} %fusion.16.place_ref, bf16[1024,1536]{1,0:T(8,128)(2,1)} %copy-done.5, bf16[4,512,1536]{2,1,0:T(8,128)(2,1)} %bitcast.89), custom_call_target="tpu_custom_call" | custom-call | flops 128849016 | bytes 65536 | tf_op jit(solution)/shard_map/pallas_call | solution.py:164
  331.4 19.3 %shard_map.313 = bf16[4,512,1536]{2,1,0:T(8,128)(2,1)} custom-call(s32[4]{0:T(128)} %iota.29._, bf16[1024,2048]{1,0:T(8,128)(2,1)} %get-tuple-element.729.refs_0_, bf16[1024,2048]{1,0:T(8,128)(2,1)} %get-tuple-element.730.refs_1_, bf16[1024,1536]{1,0:T(8,128)(2,1)} %copy-done.5, bf16[1024,1536]{1,0:T(8,128)(2,1)} %copy-done.4), custom_call_target="tpu_custom_call" | custom-call | flops 257698032 | bytes 65536 | tf_op jit(solution)/shard_map/pallas_call | solution.py:164
  364.5 7.2 %shard_map.314 = (bf16[1024,512]{1,0:T(8,128)(2,1)S(1)}, bf16[1024,512]{1,0:T(8,128)(2,1)S(1)}, bf16[1024,512]{1,0:T(8,128)(2,1)S(1)}, bf16[1024,512]{1,0:T(8,128)(2,1)S(1)}) custom-call(s32[8]{0:T(128)S(1)} %fusion.16.place_ref, bf16[1024,768]{1,0:T(8,128)(2,1)S(1)} %copy-done.9, bf16[4,768,512]{2,1,0:T(8,128)(2,1)} %bitcast.92), custom_call_target="tpu_custom_call" | custom-call | flops 64424508 | bytes 65536 | tf_op jit(solution)/shard_map/pallas_call | solution.py:164
  372.3 7.0 %shard_map.315 = (bf16[1024,512]{1,0:T(8,128)(2,1)S(1)}, bf16[1024,512]{1,0:T(8,128)(2,1)S(1)}, bf16[1024,512]{1,0:T(8,128)(2,1)S(1)}, bf16[1024,512]{1,0:T(8,128)(2,1)S(1)}) custom-call(s32[8]{0:T(128)S(1)} %fusion.16.place_ref, bf16[1024,768]{1,0:T(8,128)(2,1)S(1)} %copy-done.8, bf16[4,768,512]{2,1,0:T(8,128)(2,1)} %bitcast.93), custom_call_target="tpu_custom_call" | custom-call | flops 64424508 | bytes 65536 | tf_op jit(solution)/shard_map/pallas_call | solution.py:164
  379.4 8.3 %collective-permute-done.48.refs_1_ = bf16[1024,512]{1,0:T(8,128)(2,1)S(1)} collective-permute-done((bf16[1024,512]{1,0:T(8,128)(2,1)S(1)}, bf16[1024,512]{1,0:T(8,128)(2,1)S(1)}, u32[]{:S(2)}, u32[]{:S(2)}) %collective-permute-start.48) | collective-permute-done | bytes 1048608 | tf_op jit(solution)/shard_map/ppermute | solution.py:140
  406.6 19.7 %shard_map.318 = (bf16[1024,512]{1,0:T(8,128)(2,1)S(1)}, bf16[1024,256]{1,0:T(8,128)(2,1)S(1)}, bf16[1024,256]{1,0:T(8,128)(2,1)S(1)}, f32[16,128]{1,0:T(8,128)S(1)}) custom-call(s32[1]{0:T(128)} %constant.75.clone.1._.order_ref, f32[1024,1024]{1,0:T(8,128)} %get-tuple-element.802.q_ref.k_ref.v_ref, f32[1024,1024]{1,0:T(8,128)} %get-tuple-element.802.q_ref.k_ref.v_ref, ...), custom_call_target="tpu_custom_call" | custom-call | flops 169114336 | bytes 65536 | tf_op jit(solution)/shard_map/pallas_call | solution.py:164
  437.7 9.6 %shard_map.320 = (bf16[1024,512]{1,0:T(8,128)(2,1)S(1)}, bf16[1024,512]{1,0:T(8,128)(2,1)}, bf16[1024,512]{1,0:T(8,128)(2,1)}, bf16[1024,512]{1,0:T(8,128)(2,1)}...) custom-call(s32[8]{0:T(128)S(1)} %get-tuple-element.1040.place_ref, bf16[1024,1024]{1,0:T(8,128)(2,1)} %pad_maximum_fusion.refs_2_.refs_0_, ...), custom_call_target="tpu_custom_call" | custom-call | flops 85899344 | bytes 65536 | tf_op jit(solution)/shard_map/pallas_call | solution.py:164
  457.7 10.0 %shard_map.322 = bf16[5,256,1536]{2,1,0:T(8,128)(2,1)} custom-call(s32[5]{0:T(128)} %constant.86.clone._, bf16[1024,2048]{1,0:T(8,128)(2,1)} %get-tuple-element.854.refs_0_.refs_9_, bf16[1024,2048]{1,0:T(8,128)(2,1)} %copy-done, bf16[1024,1024]{1,0:T(8,128)(2,1)} %pad_maximum_fusion.refs_2_.refs_0_, bf16[1024,512]{1,0:T(8,128)(2,1)} %copy-done.3), custom_call_target="tpu_custom_call" | custom-call | flops 80530640 | bytes 65536 | tf_op jit(solution)/shard_map/pallas_call | solution.py:164
  485.2 8.9 %collective-permute-done.62 = bf16[256,1536]{1,0:T(8,128)(2,1)S(1)} collective-permute-done((bf16[256,1536]{1,0:T(8,128)(2,1)}, bf16[256,1536]{1,0:T(8,128)(2,1)S(1)}, u32[]{:S(2)}, u32[]{:S(2)}) %collective-permute-start.62) | collective-permute-done | bytes 786464 | tf_op jit(solution)/shard_map/ppermute | solution.py:73
  516.3 11.4 %collective-permute-done.66 = bf16[256,1536]{1,0:T(8,128)(2,1)S(1)} collective-permute-done((bf16[256,1536]{1,0:T(8,128)(2,1)S(1)}, bf16[256,1536]{1,0:T(8,128)(2,1)S(1)}, u32[]{:S(2)}, u32[]{:S(2)}) %collective-permute-start.66) | collective-permute-done | bytes 786464 | tf_op jit(solution)/shard_map/ppermute | solution.py:73
  539.9 8.1 %collective-permute-done.71 = bf16[256,1536]{1,0:T(8,128)(2,1)S(1)} collective-permute-done((bf16[256,1536]{1,0:T(8,128)(2,1)S(1)}, bf16[256,1536]{1,0:T(8,128)(2,1)S(1)}, u32[]{:S(2)}, u32[]{:S(2)}) %collective-permute-start.71) | collective-permute-done | bytes 786464 | tf_op jit(solution)/shard_map/ppermute | solution.py:73
  (434 shorter events, 258.1 us)
Async XLA Ops:
  7.2 78.5 %all-gather.7.cloned.1.call-start = ((), (), s32[]{:S(2)}) async-start(), calls=%async_computation.4 | async-start | bytes 2359296 | tf_op jit(solution)/shard_map/all_gather | solution.py:82
  7.9 209.0 %all-gather.9.cloned.1.call-start = ((), (), s32[]{:S(2)}) async-start(), calls=%async_computation.5 | async-start | bytes 7864320 | tf_op jit(solution)/shard_map/all_gather | solution.py:108
  48.2 37.5 %collective-permute-start.12 = (bf16[256,1536]{1,0:T(8,128)(2,1)}, bf16[256,1536]{1,0:T(8,128)(2,1)}, u32[]{:S(2)}, u32[]{:S(2)}) collective-permute-start(bf16[256,1536]{1,0:T(8,128)(2,1)} %pad_maximum_fusion.9), channel_id=1, source_target_pairs={{0,4},{4,0},{8,12},{12,8},{16,20},{20,16},{24,28},{28,24},{1,5},{5... | collective-permute-start | bytes 2359304 | tf_op jit(solution)/shard_map/ppermute | solution.py:79
  52.4 33.3 %collective-permute-start.10 = (bf16[256,1024]{1,0:T(8,128)(2,1)}, bf16[256,1024]{1,0:T(8,128)(2,1)S(1)}, u32[]{:S(2)}, u32[]{:S(2)}) collective-permute-start(bf16[256,1024]{1,0:T(8,128)(2,1)} %collective-permute-done.4.refs_7_.refs_3_), channel_id=1, source_target_pairs={{0,8},{8,16},{16,24},{24,28},{28,20},{20,12},{12,4},{4,0},{1,9},{9... | collective-permute-start | bytes 1572872 | tf_op jit(solution)/shard_map/ppermute | solution.py:73
  54.0 31.7 %collective-permute-start.11 = (bf16[256,1024]{1,0:T(8,128)(2,1)}, bf16[256,1024]{1,0:T(8,128)(2,1)}, u32[]{:S(2)}, u32[]{:S(2)}) collective-permute-start(bf16[256,1024]{1,0:T(8,128)(2,1)} %collective-permute-done.5.refs_11_.refs_7_), channel_id=1, source_target_pairs={{8,0},{16,8},{24,16},{28,24},{20,28},{12,20},{4,12},{0,4},{9,1},{1... | collective-permute-start | bytes 1572872 | tf_op jit(solution)/shard_map/ppermute | solution.py:76
  88.3 178.8 %all-gather.11.cloned.1.call-start = ((), (), s32[]{:S(2)}) async-start(), calls=%async_computation.6 | async-start | bytes 3932160 | tf_op jit(solution)/shard_map/all_gather | solution.py:108
  98.0 35.5 %collective-permute-start.16 = (bf16[1024,512]{1,0:T(8,128)(2,1)}, bf16[1024,512]{1,0:T(8,128)(2,1)}, u32[]{:S(2)}, u32[]{:S(2)}) collective-permute-start(bf16[1024,512]{1,0:T(8,128)(2,1)} %refs_0_.1), channel_id=1, source_target_pairs={{0,4},{4,0},{8,12},{12,8},{16,20},{20,16},{24,28},{28,24},{1,5},{5... | collective-permute-start | bytes 3145736 | tf_op jit(solution)/shard_map/ppermute | solution.py:79
  98.2 35.4 %collective-permute-start.15 = (bf16[1024,512]{1,0:T(8,128)(2,1)}, bf16[1024,512]{1,0:T(8,128)(2,1)}, u32[]{:S(2)}, u32[]{:S(2)}) collective-permute-start(bf16[1024,512]{1,0:T(8,128)(2,1)} %refs_0_.1), channel_id=1, source_target_pairs={{0,2},{1,3},{2,0},{3,1},{4,6},{5,7},{6,4},{7,5},{8,10},{9,11},{10,... | collective-permute-start | bytes 3145736 | tf_op jit(solution)/shard_map/ppermute | solution.py:140
  102.0 31.6 %collective-permute-start.17 = (bf16[768,256]{1,0:T(8,128)(2,1)S(1)}, bf16[768,256]{1,0:T(8,128)(2,1)S(1)}, u32[]{:S(2)}, u32[]{:S(2)}) collective-permute-start(bf16[768,256]{1,0:T(8,128)(2,1)S(1)} %get-tuple-element.1018), channel_id=1, source_target_pairs={{0,4},{4,0},{8,12},{12,8},{16,20},{20,16},{24,28},{28,24},{1,5},{5... | collective-permute-start | bytes 1179656 | tf_op jit(solution)/shard_map/ppermute | solution.py:79
  143.8 26.3 %collective-permute-start.21 = (bf16[1024,512]{1,0:T(8,128)(2,1)}, bf16[1024,512]{1,0:T(8,128)(2,1)}, u32[]{:S(2)}, u32[]{:S(2)}) collective-permute-start(bf16[1024,512]{1,0:T(8,128)(2,1)} %add_convert_fusion.6), channel_id=1, source_target_pairs={{0,2},{1,3},{2,0},{3,1},{4,6},{5,7},{6,4},{7,5},{8,10},{9,11},{10,... | collective-permute-start | bytes 3145736 | tf_op jit(solution)/shard_map/ppermute | solution.py:140
  150.0 30.5 %collective-permute-start.23 = (bf16[512,512]{1,0:T(8,128)(2,1)}, bf16[512,512]{1,0:T(8,128)(2,1)}, u32[]{:S(2)}, u32[]{:S(2)}) collective-permute-start(bf16[512,512]{1,0:T(8,128)(2,1)} %slice.149), channel_id=1, source_target_pairs={{0,2},{1,3},{2,0},{3,1},{4,6},{5,7},{6,4},{7,5},{8,10},{9,11},{10,... | collective-permute-start | bytes 1572872 | tf_op jit(solution)/shard_map/ppermute | solution.py:140
  182.9 172.0 %reduce-scatter.3.cloned.1.call-start = ((), (), s32[]{:S(2)}) async-start(), calls=%async_computation.2 | async-start | bytes 3932160 | tf_op jit(solution)/shard_map/reduce_scatter | solution.py:112
  265.3 214.0 %reduce-scatter.5.cloned.1.call-start = ((), (), s32[]{:S(2)}) async-start(), calls=%async_computation.3 | async-start | bytes 7864320 | tf_op jit(solution)/shard_map/reduce_scatter | solution.py:112
  362.2 25.6 %collective-permute-start.48 = (bf16[1024,512]{1,0:T(8,128)(2,1)S(1)}, bf16[1024,512]{1,0:T(8,128)(2,1)S(1)}, u32[]{:S(2)}, u32[]{:S(2)}) collective-permute-start(bf16[1024,512]{1,0:T(8,128)(2,1)S(1)} %get-tuple-element.786.refs_0_), channel_id=1, source_target_pairs={{0,2},{1,3},{2,0},{3,1},{4,6},{5,7},{6,4},{7,5},{8,10},{9,11},{10,... | collective-permute-start | bytes 3145736 | tf_op jit(solution)/shard_map/ppermute | solution.py:140
  387.7 38.6 %collective-permute-start.53 = (bf16[1024,512]{1,0:T(8,128)(2,1)S(1)}, bf16[1024,512]{1,0:T(8,128)(2,1)S(1)}, u32[]{:S(2)}, u32[]{:S(2)}) collective-permute-start(bf16[1024,512]{1,0:T(8,128)(2,1)S(1)} %get-tuple-element.812), channel_id=1, source_target_pairs={{0,1},{1,0},{2,3},{3,2},{4,5},{5,4},{6,7},{7,6},{8,9},{9,8},{10,11... | collective-permute-start | bytes 3145736 | tf_op jit(solution)/shard_map/ppermute | solution.py:140
  388.2 38.1 %collective-permute-start.54 = (bf16[1024,512]{1,0:T(8,128)(2,1)S(1)}, bf16[1024,512]{1,0:T(8,128)(2,1)}, u32[]{:S(2)}, u32[]{:S(2)}) collective-permute-start(bf16[1024,512]{1,0:T(8,128)(2,1)S(1)} %get-tuple-element.813), channel_id=1, source_target_pairs={{0,1},{1,0},{2,3},{3,2},{4,5},{5,4},{6,7},{7,6},{8,9},{9,8},{10,11... | collective-permute-start | bytes 3145736 | tf_op jit(solution)/shard_map/ppermute | solution.py:140
  394.4 32.0 %collective-permute-start.52 = (bf16[1024,512]{1,0:T(8,128)(2,1)S(1)}, bf16[1024,512]{1,0:T(8,128)(2,1)S(1)}, u32[]{:S(2)}, u32[]{:S(2)}) collective-permute-start(bf16[1024,512]{1,0:T(8,128)(2,1)S(1)} %add_convert_fusion.4), channel_id=1, source_target_pairs={{0,4},{4,0},{8,12},{12,8},{16,20},{20,16},{24,28},{28,24},{1,5},{5... | collective-permute-start | bytes 3145736 | tf_op jit(solution)/shard_map/ppermute | solution.py:79
  395.3 72.5 %collective-permute-start.57 = (bf16[1024,512]{1,0:T(8,128)(2,1)}, bf16[1024,512]{1,0:T(8,128)(2,1)}, u32[]{:S(2)}, u32[]{:S(2)}) collective-permute-start(bf16[1024,512]{1,0:T(8,128)(2,1)} %add_convert_fusion.3), channel_id=1, source_target_pairs={{0,4},{4,0},{8,12},{12,8},{16,20},{20,16},{24,28},{28,24},{1,5},{5... | collective-permute-start | bytes 3145736 | tf_op jit(solution)/shard_map/ppermute | solution.py:79
  435.6 32.1 %collective-permute-start.55 = (bf16[128,1536]{1,0:T(8,128)(2,1)}, bf16[128,1536]{1,0:T(8,128)(2,1)}, u32[]{:S(2)}, u32[]{:S(2)}) collective-permute-start(bf16[128,1536]{1,0:T(8,128)(2,1)} %get-tuple-element.858), channel_id=1, source_target_pairs={{0,8},{8,16},{16,24},{24,28},{28,20},{20,12},{12,4},{4,0},{1,9},{9... | collective-permute-start | bytes 1179656 | tf_op jit(solution)/shard_map/ppermute | solution.py:73
  436.1 31.7 %collective-permute-start.56 = (bf16[128,1536]{1,0:T(8,128)(2,1)}, bf16[128,1536]{1,0:T(8,128)(2,1)}, u32[]{:S(2)}, u32[]{:S(2)}) collective-permute-start(bf16[128,1536]{1,0:T(8,128)(2,1)} %get-tuple-element.859), channel_id=1, source_target_pairs={{8,0},{16,8},{24,16},{28,24},{20,28},{12,20},{4,12},{0,4},{9,1},{1... | collective-permute-start | bytes 1179656 | tf_op jit(solution)/shard_map/ppermute | solution.py:76
  484.0 43.6 %collective-permute-start.69 = (bf16[256,1536]{1,0:T(8,128)(2,1)}, bf16[256,1536]{1,0:T(8,128)(2,1)S(1)}, u32[]{:S(2)}, u32[]{:S(2)}) collective-permute-start(bf16[256,1536]{1,0:T(8,128)(2,1)} %slice.173), channel_id=1, source_target_pairs={{0,4},{4,0},{8,12},{12,8},{16,20},{20,16},{24,28},{28,24},{1,5},{5... | collective-permute-start | bytes 2359304 | tf_op jit(solution)/shard_map/ppermute | solution.py:79
  496.3 31.3 %collective-permute-start.66 = (bf16[256,1536]{1,0:T(8,128)(2,1)S(1)}, bf16[256,1536]{1,0:T(8,128)(2,1)S(1)}, u32[]{:S(2)}, u32[]{:S(2)}) collective-permute-start(bf16[256,1536]{1,0:T(8,128)(2,1)S(1)} %get-tuple-element.911), channel_id=1, source_target_pairs={{0,8},{8,16},{16,24},{24,28},{28,20},{20,12},{12,4},{4,0},{1,9},{9... | collective-permute-start | bytes 2359304 | tf_op jit(solution)/shard_map/ppermute | solution.py:73
  497.5 30.1 %collective-permute-start.67 = (bf16[256,1536]{1,0:T(8,128)(2,1)S(1)}, bf16[256,1536]{1,0:T(8,128)(2,1)S(1)}, u32[]{:S(2)}, u32[]{:S(2)}) collective-permute-start(bf16[256,1536]{1,0:T(8,128)(2,1)S(1)} %get-tuple-element.912), channel_id=1, source_target_pairs={{8,0},{16,8},{24,16},{28,24},{20,28},{12,20},{4,12},{0,4},{9,1},{1... | collective-permute-start | bytes 2359304 | tf_op jit(solution)/shard_map/ppermute | solution.py:76
  511.0 25.9 %collective-permute-start.70 = (bf16[1024,512]{1,0:T(8,128)(2,1)S(1)}, bf16[1024,512]{1,0:T(8,128)(2,1)S(1)}, u32[]{:S(2)}, u32[]{:S(2)}) collective-permute-start(bf16[1024,512]{1,0:T(8,128)(2,1)S(1)} %add_convert_fusion.1), channel_id=1, source_target_pairs={{0,2},{1,3},{2,0},{3,1},{4,6},{5,7},{6,4},{7,5},{8,10},{9,11},{10,... | collective-permute-start | bytes 3145736 | tf_op jit(solution)/shard_map/ppermute | solution.py:140
  (138 other events, 1374.0 us)
Sparse Core Ops, SparseCore 0:
  10.1 65.2 all-gather.6
  88.4 115.3 all-gather.8
  205.3 61.7 all-gather.10
  269.2 58.8 reduce-scatter.2
  355.0 118.9 reduce-scatter.4

commit v7 on v6

--- a/solution.py
+++ b/solution.py
@@ -862,10 +862,7 @@
         lambda left, weights, wide: spread_product(place, left, weights, True, wide, True), qkv_low, qkv_all, wide_one
     )
     got_far, got_own = near(to_diagonal), near(to_near)
-    second = parts(steps + 1, steps - 1)
-    own, on, back, out_second = parts(
-        *(n for s in range(2, steps) for n in (steps + s, steps - s)), 0, beside=(on, back, out_second)
-    )
+    second, on, back = parts(steps + 1, steps - 1, beside=(on, back))
     on = jnp.concatenate([second[0, :cut] + on.astype(f32), second[0, cut:].astype(f32)], 0)
     back = jnp.concatenate([second[1, :cut].astype(f32), second[1, cut:] + back.astype(f32)], 0)
     on, back, got_far, got_own, to_far = go(on, back, got_far, got_own, to_far)
@@ -888,6 +885,7 @@
     sums, inner = pin(sums, inner)
     bits = [1 << n for n in range(lax.axis_size("row").bit_length() - 1)]
     sums_got = swap(sums, "row", bits[0])
+    own, out_second = parts(*(n for s in range(2, steps) for n in (steps + s, steps - s)), 0, beside=(out_second,))
     on, back, sums_got = pin(on, back, sums_got)
     on, back = go(own[0] + on.astype(f32), own[1] + back.astype(f32))
     sums = pin(sums + sums_got)

time: 567 us -> 586 us (1.034)
  waiting for transfers between devices: 164 us -> 185 us
    ppermute x8, waiting for transfers between devices: 65.7 us -> 74.1 us  [send_on(): return lax.ppermute(value, 'row', self.onward)]
    ppermute x8, waiting for transfers between devices: 19.6 us -> 27.6 us  [send_back(): return lax.ppermute(value, 'row', self.backward)]
    ppermute x13, waiting for transfers between devices: 0.92 us -> 7.1 us  [to_partner(): return lax.ppermute(value, 'row', self.partner)]
    unnamed x171 -> x165, local copies, waits for them, and re-layouts: 28.1 us -> 28.4 us
  transfers between devices with their start and end apart: 79 -> 79, of which waited for: 30 -> 31; matrix products, arithmetic and copies ran while one was open for 15% -> 14% of each run, Pallas kernels for 37% -> 36%
where the time goes in v7:
time: 586 us; the launch traced here: 580 us
  Pallas kernels  212 us (36%)
  waiting for transfers between devices  185 us (32%)
  other arithmetic  58.8 us (10%)
  starting transfers between devices  54.1 us (9%)
  local copies, waits for them, and re-layouts  53.6 us (9%)
  between operations  15.5 us (3%)
    pallas_call x23, Pallas kernels, kernel_call(): pl.pallas_call(body, grid_spec=pltpu.PrefetchScalarGridSpec(num_scalar_pr...  212 us
    ppermute x45, waiting for transfers between devices, swap(): lax.ppermute(value, axis, [(i, i ^ bit) for i in range(lax.axis_size(axis...  74.4 us
    ppermute x8, waiting for transfers between devices, send_on(): return lax.ppermute(value, 'row', self.onward)  74.1 us
    unnamed x165, local copies, waits for them, and re-layouts  28.4 us
    ppermute x8, waiting for transfers between devices, send_back(): return lax.ppermute(value, 'row', self.backward)  27.6 us
    ppermute x45, starting transfers between devices, swap(): lax.ppermute(value, axis, [(i, i ^ bit) for i in range(lax.axis_size(axis...  22.3 us
  transfers between devices with their start and end apart: 79, of which 31 were waited for; matrix products, arithmetic and copies ran while one was open for 14% of the time, Pallas kernels for 36%

profile of v7, /device:TPU:0, one launch (start us, length us, event | category | flops | bytes accessed | tf_op | source)
XLA Modules:
  0.0 579.8 jit_solution(2199644666062995463)
XLA Ops:
  16.6 9.5 %collective-permute-done.1.refs_12_.refs_8_ = bf16[256,1024]{1,0:T(8,128)(2,1)S(1)} collective-permute-done((bf16[256,1024]{1,0:T(8,128)(2,1)S(1)}, bf16[256,1024]{1,0:T(8,128)(2,1)S(1)}, u32[]{:S(2)}, u32[]{:S(2)}) %collective-permute-start.1) | collective-permute-done | bytes 524320 | tf_op jit(solution)/shard_map/ppermute | solution.py:76
  57.4 28.3 %collective-permute-done.10.refs_8_.refs_4_ = bf16[256,1024]{1,0:T(8,128)(2,1)S(1)} collective-permute-done((bf16[256,1024]{1,0:T(8,128)(2,1)}, bf16[256,1024]{1,0:T(8,128)(2,1)S(1)}, u32[]{:S(2)}, u32[]{:S(2)}) %collective-permute-start.10) | collective-permute-done | bytes 524320 | tf_op jit(solution)/shard_map/ppermute | solution.py:73
  104.8 11.5 %shard_map.301 = (bf16[1024,2048]{1,0:T(8,128)(2,1)}, f32[1024,1]{1,0:T(8,128)S(1)}, f32[1024,1024]{1,0:T(8,128)}) custom-call(s32[8]{0:T(128)S(1)} %get-tuple-element.1040.place_ref, bf16[1024,512]{1,0:T(8,128)(2,1)S(1)} %copy-done.6, bf16[1024,512]{1,0:T(8,128)(2,1)} %collective-permute-done.2.refs_1_, bf16[1024,512]{1,0:T(8,128)(2,1)} %collective-permute-done.8.refs_2_, ...), custom_call_target="tpu_custom_call" | custom-call | flops 85899344 | bytes 65536 | tf_op jit(solution)/shard_map/pallas_call | solution.py:164
  117.1 13.8 %shard_map.302 = (bf16[1024,512]{1,0:T(8,128)(2,1)S(1)}, bf16[1024,256]{1,0:T(8,128)(2,1)S(1)}, bf16[1024,256]{1,0:T(8,128)(2,1)S(1)}, bf16[1024,512]{1,0:T(8,128)(2,1)S(1)}) custom-call(s32[1]{0:T(128)} %constant.75.clone.1._.order_ref, f32[1024,1024]{1,0:T(8,128)} %get-tuple-element.802.q_ref.k_ref.v_ref, ...), custom_call_target="tpu_custom_call" | custom-call | flops 120795952 | bytes 65536 | tf_op jit(solution)/shard_map/pallas_call | solution.py:164
  157.5 12.7 %collective-permute-done.21 = bf16[1024,512]{1,0:T(8,128)(2,1)} collective-permute-done((bf16[1024,512]{1,0:T(8,128)(2,1)}, bf16[1024,512]{1,0:T(8,128)(2,1)}, u32[]{:S(2)}, u32[]{:S(2)}) %collective-permute-start.21) | collective-permute-done | bytes 1048608 | tf_op jit(solution)/shard_map/ppermute | solution.py:140
  195.7 13.8 %collective-permute-done.28.refs_1_ = bf16[1024,512]{1,0:T(8,128)(2,1)S(1)} collective-permute-done((bf16[1024,512]{1,0:T(8,128)(2,1)S(1)}, bf16[1024,512]{1,0:T(8,128)(2,1)S(1)}, u32[]{:S(2)}, u32[]{:S(2)}) %collective-permute-start.28) | collective-permute-done | bytes 1048608 | tf_op jit(solution)/shard_map/ppermute | solution.py:140
  220.6 13.9 %shard_map.306 = (bf16[1024,2048]{1,0:T(8,128)(2,1)}, f32[1024,1]{1,0:T(8,128)S(1)}, f32[1024,768]{1,0:T(8,128)}, f32[1024,768]{1,0:T(8,128)}, bf16[1024,768]{1,0:T(8,128)(2,1)}) custom-call(s32[8]{0:T(128)S(1)} %fusion.16.place_ref, bf16[1024,512]{1,0:T(8,128)(2,1)S(1)} %get-tuple-element.612.refs_0_, bf16[1024,512]{1,0:T(8,128)(2,1)S(1)} %copy-done.23, ...), custom_call_target="tpu_custom_call" | custom-call | flops 128849016 | bytes 65536 | tf_op jit(solution)/shard_map/pallas_call | solution.py:164
  238.7 14.6 %shard_map.307 = (bf16[1024,2048]{1,0:T(8,128)(2,1)}, f32[1024,1]{1,0:T(8,128)}, f32[1024,768]{1,0:T(8,128)}, f32[1024,768]{1,0:T(8,128)}, bf16[1024,768]{1,0:T(8,128)(2,1)}) custom-call(s32[8]{0:T(128)S(1)} %fusion.16.place_ref, bf16[1024,512]{1,0:T(8,128)(2,1)} %collective-permute-done.30.refs_0_, bf16[1024,512]{1,0:T(8,128)(2,1)S(1)} %pad_maximum_fusion.5.refs_1_, ...), custom_call_target="tpu_custom_call" | custom-call | flops 128849016 | bytes 65536 | tf_op jit(solution)/shard_map/pallas_call | solution.py:164
  253.8 11.5 %shard_map.308 = bf16[4,768,512]{2,1,0:T(8,128)(2,1)} custom-call(s32[4]{0:T(128)} %iota.28._, bf16[1024,768]{1,0:T(8,128)(2,1)} %get-tuple-element.761.refs_0_, bf16[1024,768]{1,0:T(8,128)(2,1)} %get-tuple-element.753.refs_1_.refs_0_, bf16[1024,2048]{1,0:T(8,128)(2,1)} %copy-done.1, bf16[1024,2048]{1,0:T(8,128)(2,1)} %copy-done.2), custom_call_target="tpu_custom_call" | custom-call | flops 128849016 | bytes 65536 | tf_op jit(solution)/shard_map/pallas_call | solution.py:164
  267.1 9.2 %shard_map.309 = (bf16[1024,1536]{1,0:T(8,128)(2,1)S(1)}, f32[1024,1]{1,0:T(8,128)S(1)}) custom-call(s32[1]{0:T(128)} %constant.75.clone.1._.order_ref, bf16[1024,2048]{1,0:T(8,128)(2,1)} %copy-done.2, f32[1024,768]{1,0:T(8,128)} %get-tuple-element.662.refs_1_, f32[1024,768]{1,0:T(8,128)} %get-tuple-element.663.refs_2_, bf16[4,768,512]{2,1,0:T(8,128)(2,1)} %bitcast.90), custom_call_target="tpu_custom_call" | custom-call | flops 64424508 | bytes 65536 | tf_op jit(solution)/shard_map/pallas_call | solution.py:164
  278.7 12.3 %shard_map.310 = (bf16[1024,512]{1,0:T(8,128)(2,1)S(1)}, bf16[1024,512]{1,0:T(8,128)(2,1)S(1)}, bf16[1024,512]{1,0:T(8,128)(2,1)}, bf16[1024,512]{1,0:T(8,128)(2,1)}) custom-call(s32[8]{0:T(128)S(1)} %fusion.16.place_ref, bf16[1024,1536]{1,0:T(8,128)(2,1)} %copy-done.4, bf16[4,512,1536]{2,1,0:T(8,128)(2,1)} %bitcast.88), custom_call_target="tpu_custom_call" | custom-call | flops 128849016 | bytes 65536 | tf_op jit(solution)/shard_map/pallas_call | solution.py:164
  294.9 8.8 %shard_map.311 = (bf16[1024,1536]{1,0:T(8,128)(2,1)S(1)}, f32[1024,1]{1,0:T(8,128)S(1)}) custom-call(s32[1]{0:T(128)} %constant.75.clone.1._.order_ref, bf16[1024,2048]{1,0:T(8,128)(2,1)} %copy-done.1, f32[1024,768]{1,0:T(8,128)} %get-tuple-element.683.refs_1_, f32[1024,768]{1,0:T(8,128)} %get-tuple-element.684.refs_2_, bf16[4,768,512]{2,1,0:T(8,128)(2,1)} %bitcast.91), custom_call_target="tpu_custom_call" | custom-call | flops 64424508 | bytes 65536 | tf_op jit(solution)/shard_map/pallas_call | solution.py:164
  310.4 11.5 %shard_map.312 = (bf16[1024,512]{1,0:T(8,128)(2,1)S(1)}, bf16[1024,512]{1,0:T(8,128)(2,1)S(1)}, bf16[1024,512]{1,0:T(8,128)(2,1)S(1)}, bf16[1024,512]{1,0:T(8,128)(2,1)S(1)}) custom-call(s32[8]{0:T(128)S(1)} %fusion.16.place_ref, bf16[1024,1536]{1,0:T(8,128)(2,1)} %copy-done.5, bf16[4,512,1536]{2,1,0:T(8,128)(2,1)} %bitcast.89), custom_call_target="tpu_custom_call" | custom-call | flops 128849016 | bytes 65536 | tf_op jit(solution)/shard_map/pallas_call | solution.py:164
  331.4 19.3 %shard_map.313 = bf16[4,512,1536]{2,1,0:T(8,128)(2,1)} custom-call(s32[4]{0:T(128)} %iota.29._, bf16[1024,2048]{1,0:T(8,128)(2,1)} %get-tuple-element.729.refs_0_, bf16[1024,2048]{1,0:T(8,128)(2,1)} %get-tuple-element.730.refs_1_, bf16[1024,1536]{1,0:T(8,128)(2,1)} %copy-done.5, bf16[1024,1536]{1,0:T(8,128)(2,1)} %copy-done.4), custom_call_target="tpu_custom_call" | custom-call | flops 257698032 | bytes 65536 | tf_op jit(solution)/shard_map/pallas_call | solution.py:164
  364.6 7.2 %shard_map.314 = (bf16[1024,512]{1,0:T(8,128)(2,1)S(1)}, bf16[1024,512]{1,0:T(8,128)(2,1)S(1)}, bf16[1024,512]{1,0:T(8,128)(2,1)S(1)}, bf16[1024,512]{1,0:T(8,128)(2,1)S(1)}) custom-call(s32[8]{0:T(128)S(1)} %fusion.16.place_ref, bf16[1024,768]{1,0:T(8,128)(2,1)S(1)} %copy-done.9, bf16[4,768,512]{2,1,0:T(8,128)(2,1)} %bitcast.92), custom_call_target="tpu_custom_call" | custom-call | flops 64424508 | bytes 65536 | tf_op jit(solution)/shard_map/pallas_call | solution.py:164
  379.5 8.3 %collective-permute-done.48.refs_1_ = bf16[1024,512]{1,0:T(8,128)(2,1)S(1)} collective-permute-done((bf16[1024,512]{1,0:T(8,128)(2,1)S(1)}, bf16[1024,512]{1,0:T(8,128)(2,1)S(1)}, u32[]{:S(2)}, u32[]{:S(2)}) %collective-permute-start.48) | collective-permute-done | bytes 1048608 | tf_op jit(solution)/shard_map/ppermute | solution.py:140
  405.4 19.7 %shard_map.318 = (bf16[1024,512]{1,0:T(8,128)(2,1)S(1)}, bf16[1024,256]{1,0:T(8,128)(2,1)S(1)}, bf16[1024,256]{1,0:T(8,128)(2,1)S(1)}, f32[16,128]{1,0:T(8,128)S(1)}) custom-call(s32[1]{0:T(128)} %constant.75.clone.1._.order_ref, f32[1024,1024]{1,0:T(8,128)} %get-tuple-element.802.q_ref.k_ref.v_ref, f32[1024,1024]{1,0:T(8,128)} %get-tuple-element.802.q_ref.k_ref.v_ref, ...), custom_call_target="tpu_custom_call" | custom-call | flops 169114336 | bytes 65536 | tf_op jit(solution)/shard_map/pallas_call | solution.py:164
  436.6 9.6 %shard_map.320 = (bf16[1024,512]{1,0:T(8,128)(2,1)S(1)}, bf16[1024,512]{1,0:T(8,128)(2,1)}, bf16[1024,512]{1,0:T(8,128)(2,1)}, bf16[1024,512]{1,0:T(8,128)(2,1)}...) custom-call(s32[8]{0:T(128)S(1)} %get-tuple-element.1040.place_ref, bf16[1024,1024]{1,0:T(8,128)(2,1)} %pad_maximum_fusion.refs_2_.refs_0_, ...), custom_call_target="tpu_custom_call" | custom-call | flops 85899344 | bytes 65536 | tf_op jit(solution)/shard_map/pallas_call | solution.py:164
  455.7 8.1 %collective-permute-done.56 = bf16[128,1536]{1,0:T(8,128)(2,1)} collective-permute-done((bf16[128,1536]{1,0:T(8,128)(2,1)}, bf16[128,1536]{1,0:T(8,128)(2,1)}, u32[]{:S(2)}, u32[]{:S(2)}) %collective-permute-start.56) | collective-permute-done | bytes 393248 | tf_op jit(solution)/shard_map/ppermute | solution.py:76
  479.7 9.9 %shard_map.322 = bf16[5,256,1536]{2,1,0:T(8,128)(2,1)} custom-call(s32[5]{0:T(128)} %constant.86.clone._, bf16[1024,2048]{1,0:T(8,128)(2,1)} %get-tuple-element.883.refs_0_.refs_9_, bf16[1024,2048]{1,0:T(8,128)(2,1)} %copy-done, bf16[1024,1024]{1,0:T(8,128)(2,1)} %pad_maximum_fusion.refs_2_.refs_0_, bf16[1024,512]{1,0:T(8,128)(2,1)} %copy-done.3), custom_call_target="tpu_custom_call" | custom-call | flops 80530640 | bytes 65536 | tf_op jit(solution)/shard_map/pallas_call | solution.py:164
  496.4 16.2 %collective-permute-done.62 = bf16[256,1536]{1,0:T(8,128)(2,1)S(1)} collective-permute-done((bf16[256,1536]{1,0:T(8,128)(2,1)}, bf16[256,1536]{1,0:T(8,128)(2,1)S(1)}, u32[]{:S(2)}, u32[]{:S(2)}) %collective-permute-start.62) | collective-permute-done | bytes 786464 | tf_op jit(solution)/shard_map/ppermute | solution.py:73
  525.1 8.7 %collective-permute-done.68 = f32[1280]{0:T(1024)S(1)} collective-permute-done((f32[1280]{0:T(1024)S(1)}, f32[1280]{0:T(1024)S(1)}, u32[]{:S(2)}, u32[]{:S(2)}) %collective-permute-start.68) | collective-permute-done | bytes 5152 | tf_op jit(solution)/shard_map/ppermute | solution.py:140
  533.8 12.2 %collective-permute-done.66 = bf16[256,1536]{1,0:T(8,128)(2,1)S(1)} collective-permute-done((bf16[256,1536]{1,0:T(8,128)(2,1)S(1)}, bf16[256,1536]{1,0:T(8,128)(2,1)S(1)}, u32[]{:S(2)}, u32[]{:S(2)}) %collective-permute-start.66) | collective-permute-done | bytes 786464 | tf_op jit(solution)/shard_map/ppermute | solution.py:73
  558.2 8.4 %collective-permute-done.71 = bf16[256,1536]{1,0:T(8,128)(2,1)S(1)} collective-permute-done((bf16[256,1536]{1,0:T(8,128)(2,1)S(1)}, bf16[256,1536]{1,0:T(8,128)(2,1)S(1)}, u32[]{:S(2)}, u32[]{:S(2)}) %collective-permute-start.71) | collective-permute-done | bytes 786464 | tf_op jit(solution)/shard_map/ppermute | solution.py:73
  (428 shorter events, 265.7 us)
Async XLA Ops:
  7.2 78.5 %all-gather.7.cloned.1.call-start = ((), (), s32[]{:S(2)}) async-start(), calls=%async_computation.4 | async-start | bytes 2359296 | tf_op jit(solution)/shard_map/all_gather | solution.py:82
  7.9 209.0 %all-gather.9.cloned.1.call-start = ((), (), s32[]{:S(2)}) async-start(), calls=%async_computation.5 | async-start | bytes 7864320 | tf_op jit(solution)/shard_map/all_gather | solution.py:108
  48.2 37.5 %collective-permute-start.12 = (bf16[256,1536]{1,0:T(8,128)(2,1)}, bf16[256,1536]{1,0:T(8,128)(2,1)}, u32[]{:S(2)}, u32[]{:S(2)}) collective-permute-start(bf16[256,1536]{1,0:T(8,128)(2,1)} %pad_maximum_fusion.9), channel_id=1, source_target_pairs={{0,4},{4,0},{8,12},{12,8},{16,20},{20,16},{24,28},{28,24},{1,5},{5... | collective-permute-start | bytes 2359304 | tf_op jit(solution)/shard_map/ppermute | solution.py:79
  52.4 33.3 %collective-permute-start.10 = (bf16[256,1024]{1,0:T(8,128)(2,1)}, bf16[256,1024]{1,0:T(8,128)(2,1)S(1)}, u32[]{:S(2)}, u32[]{:S(2)}) collective-permute-start(bf16[256,1024]{1,0:T(8,128)(2,1)} %collective-permute-done.4.refs_7_.refs_3_), channel_id=1, source_target_pairs={{0,8},{8,16},{16,24},{24,28},{28,20},{20,12},{12,4},{4,0},{1,9},{9... | collective-permute-start | bytes 1572872 | tf_op jit(solution)/shard_map/ppermute | solution.py:73
  54.0 31.7 %collective-permute-start.11 = (bf16[256,1024]{1,0:T(8,128)(2,1)}, bf16[256,1024]{1,0:T(8,128)(2,1)}, u32[]{:S(2)}, u32[]{:S(2)}) collective-permute-start(bf16[256,1024]{1,0:T(8,128)(2,1)} %collective-permute-done.5.refs_11_.refs_7_), channel_id=1, source_target_pairs={{8,0},{16,8},{24,16},{28,24},{20,28},{12,20},{4,12},{0,4},{9,1},{1... | collective-permute-start | bytes 1572872 | tf_op jit(solution)/shard_map/ppermute | solution.py:76
  88.3 178.8 %all-gather.11.cloned.1.call-start = ((), (), s32[]{:S(2)}) async-start(), calls=%async_computation.6 | async-start | bytes 3932160 | tf_op jit(solution)/shard_map/all_gather | solution.py:108
  98.0 35.5 %collective-permute-start.16 = (bf16[1024,512]{1,0:T(8,128)(2,1)}, bf16[1024,512]{1,0:T(8,128)(2,1)}, u32[]{:S(2)}, u32[]{:S(2)}) collective-permute-start(bf16[1024,512]{1,0:T(8,128)(2,1)} %refs_0_.1), channel_id=1, source_target_pairs={{0,4},{4,0},{8,12},{12,8},{16,20},{20,16},{24,28},{28,24},{1,5},{5... | collective-permute-start | bytes 3145736 | tf_op jit(solution)/shard_map/ppermute | solution.py:79
  98.2 35.4 %collective-permute-start.15 = (bf16[1024,512]{1,0:T(8,128)(2,1)}, bf16[1024,512]{1,0:T(8,128)(2,1)}, u32[]{:S(2)}, u32[]{:S(2)}) collective-permute-start(bf16[1024,512]{1,0:T(8,128)(2,1)} %refs_0_.1), channel_id=1, source_target_pairs={{0,2},{1,3},{2,0},{3,1},{4,6},{5,7},{6,4},{7,5},{8,10},{9,11},{10,... | collective-permute-start | bytes 3145736 | tf_op jit(solution)/shard_map/ppermute | solution.py:140
  102.0 31.6 %collective-permute-start.17 = (bf16[768,256]{1,0:T(8,128)(2,1)S(1)}, bf16[768,256]{1,0:T(8,128)(2,1)S(1)}, u32[]{:S(2)}, u32[]{:S(2)}) collective-permute-start(bf16[768,256]{1,0:T(8,128)(2,1)S(1)} %get-tuple-element.1018), channel_id=1, source_target_pairs={{0,4},{4,0},{8,12},{12,8},{16,20},{20,16},{24,28},{28,24},{1,5},{5... | collective-permute-start | bytes 1179656 | tf_op jit(solution)/shard_map/ppermute | solution.py:79
  150.1 30.6 %collective-permute-start.23 = (bf16[512,512]{1,0:T(8,128)(2,1)}, bf16[512,512]{1,0:T(8,128)(2,1)}, u32[]{:S(2)}, u32[]{:S(2)}) collective-permute-start(bf16[512,512]{1,0:T(8,128)(2,1)} %slice.149), channel_id=1, source_target_pairs={{0,2},{1,3},{2,0},{3,1},{4,6},{5,7},{6,4},{7,5},{8,10},{9,11},{10,... | collective-permute-start | bytes 1572872 | tf_op jit(solution)/shard_map/ppermute | solution.py:140
  182.9 172.0 %reduce-scatter.3.cloned.1.call-start = ((), (), s32[]{:S(2)}) async-start(), calls=%async_computation.2 | async-start | bytes 3932160 | tf_op jit(solution)/shard_map/reduce_scatter | solution.py:112
  265.3 210.5 %reduce-scatter.5.cloned.1.call-start = ((), (), s32[]{:S(2)}) async-start(), calls=%async_computation.3 | async-start | bytes 7864320 | tf_op jit(solution)/shard_map/reduce_scatter | solution.py:112
  387.8 37.4 %collective-permute-start.53 = (bf16[1024,512]{1,0:T(8,128)(2,1)S(1)}, bf16[1024,512]{1,0:T(8,128)(2,1)S(1)}, u32[]{:S(2)}, u32[]{:S(2)}) collective-permute-start(bf16[1024,512]{1,0:T(8,128)(2,1)S(1)} %get-tuple-element.812), channel_id=1, source_target_pairs={{0,1},{1,0},{2,3},{3,2},{4,5},{5,4},{6,7},{7,6},{8,9},{9,8},{10,11... | collective-permute-start | bytes 3145736 | tf_op jit(solution)/shard_map/ppermute | solution.py:140
  388.3 36.9 %collective-permute-start.54 = (bf16[1024,512]{1,0:T(8,128)(2,1)S(1)}, bf16[1024,512]{1,0:T(8,128)(2,1)}, u32[]{:S(2)}, u32[]{:S(2)}) collective-permute-start(bf16[1024,512]{1,0:T(8,128)(2,1)S(1)} %get-tuple-element.813), channel_id=1, source_target_pairs={{0,1},{1,0},{2,3},{3,2},{4,5},{5,4},{6,7},{7,6},{8,9},{9,8},{10,11... | collective-permute-start | bytes 3145736 | tf_op jit(solution)/shard_map/ppermute | solution.py:140
  394.4 30.7 %collective-permute-start.52 = (bf16[1024,512]{1,0:T(8,128)(2,1)S(1)}, bf16[1024,512]{1,0:T(8,128)(2,1)S(1)}, u32[]{:S(2)}, u32[]{:S(2)}) collective-permute-start(bf16[1024,512]{1,0:T(8,128)(2,1)S(1)} %add_convert_fusion.4), channel_id=1, source_target_pairs={{0,4},{4,0},{8,12},{12,8},{16,20},{20,16},{24,28},{28,24},{1,5},{5... | collective-permute-start | bytes 3145736 | tf_op jit(solution)/shard_map/ppermute | solution.py:79
  434.9 28.8 %collective-permute-start.56 = (bf16[128,1536]{1,0:T(8,128)(2,1)}, bf16[128,1536]{1,0:T(8,128)(2,1)}, u32[]{:S(2)}, u32[]{:S(2)}) collective-permute-start(bf16[128,1536]{1,0:T(8,128)(2,1)} %get-tuple-element.853), channel_id=1, source_target_pairs={{8,0},{16,8},{24,16},{28,24},{20,28},{12,20},{4,12},{0,4},{9,1},{1... | collective-permute-start | bytes 1179656 | tf_op jit(solution)/shard_map/ppermute | solution.py:76
  470.1 42.4 %collective-permute-start.62 = (bf16[256,1536]{1,0:T(8,128)(2,1)}, bf16[256,1536]{1,0:T(8,128)(2,1)S(1)}, u32[]{:S(2)}, u32[]{:S(2)}) collective-permute-start(bf16[256,1536]{1,0:T(8,128)(2,1)} %pad_maximum_fusion.11), channel_id=1, source_target_pairs={{0,8},{8,16},{16,24},{24,28},{28,20},{20,12},{12,4},{4,0},{1,9},{9... | collective-permute-start | bytes 2359304 | tf_op jit(solution)/shard_map/ppermute | solution.py:73
  471.4 41.1 %collective-permute-start.63 = (bf16[256,1536]{1,0:T(8,128)(2,1)}, bf16[256,1536]{1,0:T(8,128)(2,1)}, u32[]{:S(2)}, u32[]{:S(2)}) collective-permute-start(bf16[256,1536]{1,0:T(8,128)(2,1)} %pad_maximum_fusion.12), channel_id=1, source_target_pairs={{8,0},{16,8},{24,16},{28,24},{20,28},{12,20},{4,12},{0,4},{9,1},{1... | collective-permute-start | bytes 2359304 | tf_op jit(solution)/shard_map/ppermute | solution.py:76
  473.7 45.6 %collective-permute-start.65 = (bf16[1024,512]{1,0:T(8,128)(2,1)}, bf16[1024,512]{1,0:T(8,128)(2,1)}, u32[]{:S(2)}, u32[]{:S(2)}) collective-permute-start(bf16[1024,512]{1,0:T(8,128)(2,1)} %add_convert_fusion.2), channel_id=1, source_target_pairs={{0,2},{1,3},{2,0},{3,1},{4,6},{5,7},{6,4},{7,5},{8,10},{9,11},{10,... | collective-permute-start | bytes 3145736 | tf_op jit(solution)/shard_map/ppermute | solution.py:140
  478.0 34.7 %collective-permute-start.64 = (f32[1280]{0:T(1024)S(1)}, f32[1280]{0:T(1024)S(1)}, u32[]{:S(2)}, u32[]{:S(2)}) collective-permute-start(f32[1280]{0:T(1024)S(1)} %pad_maximum_fusion.19), channel_id=1, source_target_pairs={{0,4},{4,0},{8,12},{12,8},{16,20},{20,16},{24,28},{28,24},{1,5},{5... | collective-permute-start | bytes 15368 | tf_op jit(solution)/shard_map/ppermute | solution.py:140
  495.8 50.3 %collective-permute-start.69 = (bf16[256,1536]{1,0:T(8,128)(2,1)}, bf16[256,1536]{1,0:T(8,128)(2,1)S(1)}, u32[]{:S(2)}, u32[]{:S(2)}) collective-permute-start(bf16[256,1536]{1,0:T(8,128)(2,1)} %slice.173), channel_id=1, source_target_pairs={{0,4},{4,0},{8,12},{12,8},{16,20},{20,16},{24,28},{28,24},{1,5},{5... | collective-permute-start | bytes 2359304 | tf_op jit(solution)/shard_map/ppermute | solution.py:79
  514.7 31.3 %collective-permute-start.66 = (bf16[256,1536]{1,0:T(8,128)(2,1)S(1)}, bf16[256,1536]{1,0:T(8,128)(2,1)S(1)}, u32[]{:S(2)}, u32[]{:S(2)}) collective-permute-start(bf16[256,1536]{1,0:T(8,128)(2,1)S(1)} %get-tuple-element.911), channel_id=1, source_target_pairs={{0,8},{8,16},{16,24},{24,28},{28,20},{20,12},{12,4},{4,0},{1,9},{9... | collective-permute-start | bytes 2359304 | tf_op jit(solution)/shard_map/ppermute | solution.py:73
  514.8 31.3 %collective-permute-start.67 = (bf16[256,1536]{1,0:T(8,128)(2,1)S(1)}, bf16[256,1536]{1,0:T(8,128)(2,1)S(1)}, u32[]{:S(2)}, u32[]{:S(2)}) collective-permute-start(bf16[256,1536]{1,0:T(8,128)(2,1)S(1)} %get-tuple-element.912), channel_id=1, source_target_pairs={{8,0},{16,8},{24,16},{28,24},{20,28},{12,20},{4,12},{0,4},{9,1},{1... | collective-permute-start | bytes 2359304 | tf_op jit(solution)/shard_map/ppermute | solution.py:76
  523.5 31.8 %collective-permute-start.70 = (bf16[1024,512]{1,0:T(8,128)(2,1)S(1)}, bf16[1024,512]{1,0:T(8,128)(2,1)S(1)}, u32[]{:S(2)}, u32[]{:S(2)}) collective-permute-start(bf16[1024,512]{1,0:T(8,128)(2,1)S(1)} %add_convert_fusion.1), channel_id=1, source_target_pairs={{0,2},{1,3},{2,0},{3,1},{4,6},{5,7},{6,4},{7,5},{8,10},{9,11},{10,... | collective-permute-start | bytes 3145736 | tf_op jit(solution)/shard_map/ppermute | solution.py:140
  (135 other events, 1400.0 us)
Sparse Core Ops, SparseCore 0:
  10.1 65.2 all-gather.6
  88.4 115.3 all-gather.8
  205.3 61.7 all-gather.10
  269.2 58.8 reduce-scatter.2
  355.0 118.8 reduce-scatter.4
